TPU v7x, 256 devices: a whole 4x4x8 slice. The times are simulated.
256 devices in a mesh: nodes: 64 (over y, z, core), mp: 4 (over x).
Axes of the slice: x: 4, y: 4, z: 8, core: 2. Of those that a mesh axis runs over, the one named last changes fastest.
Arguments:
- input_history: float32 [262144, 512], P('nodes', 'mp'), may hold values from -6 to 6
- hidden_history: float32 [262144, 512], P('nodes', 'mp'), may hold values from -6 to 6
- batch_blocks: int32 [64, 24], P('nodes'), may hold values from 0 to 31, as said below
- tile_columns: int32 [1536, 5], P('nodes'), may hold values from 0 to 215, as said below
- tile_values: bfloat16 [1536, 5, 128, 128], P('nodes'), may hold values from -0.25 to 0.25
- send_blocks: int32 [64, 64, 3], P('nodes'), may hold values from 0 to 31
- send_counts: int32 [64, 64], P('nodes'), may hold values from 2 to 3
- weight_first: bfloat16 [512, 512], P('mp'), may hold values from -0.25 to 0.25
- weight_second: bfloat16 [512, 512], P('mp'), may hold values from -0.25 to 0.25
- cotangent: bfloat16 [196608, 512], P('nodes', 'mp'), may hold values from -0.0134887695 to 0.0134887695
Outputs:
- layer_out: bfloat16 [196608, 512], P('nodes', 'mp')
- grad_first: float32 [512, 512], P('mp')
- grad_second: float32 [512, 512], P('mp')
Inputs may be any that keep to these rules, and one draw needn't show every extreme that they name: `batch_blocks`: the 24 blocks of one partition are different. `tile_columns`: column 0 of each row is the row's own block i, column 1 is a batch block below 24; columns 2 to 4 are halo slots 24 + o * 3 + j.
All inputs are finite; a program needn't handle non-finite values.
Results may differ from a plain program's by a relative error of at most 0.012.
Values may be sent and summed in bfloat16 or wider, within the bound.
No kernel may reach another device: no remote copies, remote signals or barrier semaphores. Data moves between devices by JAX's collectives and lax.ppermute only.
A program may use at most 128 MiB of HBM per device.

v0:
```python
import jax
import jax.numpy as jnp
from jax import lax
from jax.sharding import PartitionSpec as P


def slope(value):
    sig = jax.nn.sigmoid(value)
    return sig * (1.0 + value * (1.0 - sig))


def outgoing(table, send_blocks, live):
    blocks = table[send_blocks[0]]
    return jnp.where(live[:, :, None, None], blocks, jnp.zeros_like(blocks)).astype(jnp.bfloat16)


def pull_one(table, send_blocks, live):
    return lax.all_to_all(
        outgoing(table, send_blocks, live), "nodes", split_axis=0, concat_axis=0, tiled=True
    )


def aggregate(local, halo, tiles, columns):
    flat_halo = halo.reshape(-1, halo.shape[2], halo.shape[3])
    source = jnp.concatenate([local, flat_halo], axis=0)
    picked = source[columns]
    summed = jnp.einsum("rtij,rtjc->ric", tiles, picked, preferred_element_type=jnp.float32)
    return summed.astype(jnp.bfloat16).reshape(-1, local.shape[2])


def project(features, weight):
    term = jnp.dot(features, weight, preferred_element_type=jnp.float32)
    return lax.psum_scatter(term, "mp", scatter_dimension=1, tiled=True)


def backward_panel(summed, delta, weight, with_input):
    width = summed.shape[1]
    back_empty = jnp.zeros((summed.shape[0], width), jnp.float32)
    piece = lax.all_gather(delta, "mp", axis=1, tiled=True)
    back_part = back_empty
    block_grad = lax.dot_general(
        summed, piece, (((0,), (0,)), ((), ())), preferred_element_type=jnp.float32
    )
    if with_input:
        back_part = lax.dot_general(
            piece, weight, (((1,), (1,)), ((), ())), preferred_element_type=jnp.float32
        )
    return (block_grad, back_part)


def spread_back(back_rows, tiles, columns, blocks_count):
    width = back_rows.shape[1]
    blocks = back_rows.reshape(blocks_count, -1, width)
    contrib = jnp.einsum("rtji,rjc->rtic", tiles[:, :2], blocks, preferred_element_type=jnp.float32)
    onehot = (
        columns[:, :2][None, :, :] == jnp.arange(blocks_count, dtype=jnp.int32)[:, None, None]
    ).astype(jnp.float32)
    summed = jnp.einsum("krt,rtic->kic", onehot, contrib, precision=lax.Precision.HIGHEST)
    return summed.reshape(-1, width)


def sum_grad(grad_part):
    return lax.psum(grad_part, "nodes")


def body(
    input_history,
    hidden_history,
    batch_blocks,
    tile_columns,
    tile_values,
    send_blocks,
    send_counts,
    weight_first,
    weight_second,
    cotangent,
):
    width = input_history.shape[1]
    block = tile_values.shape[-1]
    blocks_count = batch_blocks.shape[1]
    slots_count = send_blocks.shape[2]
    table_input = input_history.reshape(-1, block, width)
    table_hidden = hidden_history.reshape(-1, block, width)
    live = jnp.arange(slots_count, dtype=jnp.int32)[None, :] < send_counts[0][:, None]
    halo_input = pull_one(table_input, send_blocks, live)
    local = table_input[batch_blocks[0]].astype(jnp.bfloat16)
    summed_first = aggregate(local, halo_input, tile_values, tile_columns)
    pre_first = project(summed_first, weight_first)
    hidden_first = jax.nn.silu(pre_first).astype(jnp.bfloat16)
    halo_hidden = pull_one(table_hidden, send_blocks, live)
    summed_second = aggregate(
        hidden_first.reshape(blocks_count, block, width), halo_hidden, tile_values, tile_columns
    )
    pre_second = project(summed_second, weight_second)
    layer_out = jax.nn.silu(pre_second).astype(jnp.bfloat16)
    delta_second = (cotangent.astype(jnp.float32) * slope(pre_second)).astype(jnp.bfloat16)
    part_second, back_float = backward_panel(summed_second, delta_second, weight_second, True)
    grad_second = sum_grad(part_second)
    back_second = back_float.astype(jnp.bfloat16)
    back_hidden = spread_back(back_second, tile_values, tile_columns, blocks_count)
    delta_first = (back_hidden * slope(pre_first)).astype(jnp.bfloat16)
    part_first, unused_back = backward_panel(summed_first, delta_first, weight_first, False)
    grad_first = sum_grad(part_first)
    return (layer_out, grad_first, grad_second)


def solution(mesh):
    placed = (
        P("nodes", "mp"),
        P("nodes", "mp"),
        P("nodes", None),
        P("nodes", None),
        P("nodes", None, None, None),
        P("nodes", None, None),
        P("nodes", None),
        P("mp", None),
        P("mp", None),
        P("nodes", "mp"),
    )
    return jax.shard_map(
        body,
        mesh=mesh,
        in_specs=placed,
        out_specs=(P("nodes", "mp"), P("mp", None), P("mp", None)),
        check_vma=False,
    )
```

profile of v0, /device:TPU:1, one launch (start us, length us, event | category | flops | bytes accessed | tf_op | source)
XLA Modules:
  0.0 747.8 jit_solution(17334847791018864258)
XLA Ops:
  8.8 4.7 gather_fusion.1
  13.5 10.2 %gather_fusion.3 = bf16[192,128,128]{2,1,0:T(8,128)(2,1)} fusion(f32[32,128,128]{2,1,0:T(8,128)} %bitcast.69, s32[1024]{0:T(1024)S(1)} %pad_clamp_fusion.1), kind=kCustom, calls=%fused_computation.3 | custom fusion | bytes 12583680 | tf_op jit(solution)/shard_map/gather | solution.py:13
  23.8 13.1 %select_convert_fusion.1 = (bf16[64,3,128,128]{3,2,1,0:T(8,128)(2,1)}, bf16[64,3,128,128]{3,2,1,0:T(8,128)(2,1)}) fusion(bf16[64,3,128,128]{3,2,1,0:T(8,128)(2,1)} %bitcast.67, pred[64,3]{1,0:T(8,128)(4,1)S(1)} %iota_compare_fusion, bf16[64,3,128,128]{3,2,1,0:T(8,128)(2,1)} %bitcast.68), kind=kLoop, calls=%fused_computation.6 | loop fusion | flops 6291456 | bytes 25166016 | tf_op jit(solution)/shard_map/convert_element_type | solution.py:14
  36.9 13.5 %all-to-all-start = ((bf16[64,3,128,128]{3,2,1,0:T(8,128)(2,1)}), bf16[64,3,128,128]{3,2,1,0:T(8,128)(2,1)}, u32[]{:S(2)}, u32[]{:S(2)}) async-start(bf16[64,3,128,128]{3,2,1,0:T(8,128)(2,1)} %get-tuple-element.7), calls=%async_computation | async-start | bytes 12582912 | tf_op jit(solution)/shard_map/all_to_all | solution.py:18
  51.4 139.9 %all-to-all-done = bf16[64,3,128,128]{3,2,1,0:T(8,128)(2,1)} async-done(((bf16[64,3,128,128]{3,2,1,0:T(8,128)(2,1)}), bf16[64,3,128,128]{3,2,1,0:T(8,128)(2,1)}, u32[]{:S(2)}, u32[]{:S(2)}) %all-to-all-start) | async-done | bytes 6291488 | tf_op jit(solution)/shard_map/all_to_all | solution.py:18
  191.3 6.2 pad_maximum_fusion
  197.5 5.9 gather_fusion.2
  203.5 4.5 bitcast_convert_fusion.1
  208.0 3.6 fusion.12
  211.6 6.0 all-to-all-start.1
  217.8 57.0 %reduce-scatter.3.cloned.1.call-done = f32[3072,128]{1,0:T(8,128)} async-done(((f32[3072,512]{1,0:T(8,128)}), f32[3072,128]{1,0:T(8,128)}) %reduce-scatter.3.cloned.1.call-update) | async-done | bytes 1572880 | tf_op jit(solution)/shard_map/reduce_scatter | solution.py:33
  276.6 81.8 %all-to-all-done.1 = bf16[64,3,128,128]{3,2,1,0:T(8,128)(2,1)} async-done(((bf16[64,3,128,128]{3,2,1,0:T(8,128)(2,1)}), bf16[64,3,128,128]{3,2,1,0:T(8,128)(2,1)}, u32[]{:S(2)}, u32[]{:S(2)}) %all-to-all-start.1) | async-done | bytes 6291488 | tf_op jit(solution)/shard_map/all_to_all | solution.py:18
  358.5 6.2 pad_maximum_fusion.1
  364.7 6.1 gather_fusion.4
  370.8 4.5 bitcast_convert_fusion
  375.3 3.6 fusion.13
  379.0 63.1 %reduce-scatter.5.cloned.1.call-done = f32[3072,128]{1,0:T(8,128)} async-done(((f32[3072,512]{1,0:T(8,128)}), f32[3072,128]{1,0:T(8,128)}) %reduce-scatter.5.cloned.1.call-update) | async-done | bytes 1572880 | tf_op jit(solution)/shard_map/reduce_scatter | solution.py:33
  442.1 3.4 multiply_convert_fusion
  445.6 44.7 %all-gather.3.cloned.1.call-done = bf16[3072,512]{1,0:T(8,128)(2,1)} async-done(((bf16[3072,128]{1,0:T(8,128)(2,1)}), bf16[3072,512]{1,0:T(8,128)(2,1)}) %all-gather.3.cloned.1.call-update) | async-done | bytes 3145744 | tf_op jit(solution)/shard_map/all_gather | solution.py:39
  493.2 3.7 fusion.3
  496.9 3.6 copy.21
  505.6 3.6 fusion.15
  509.2 43.3 %all-gather.5.cloned.1.call-done = bf16[3072,512]{1,0:T(8,128)(2,1)} async-done(((bf16[3072,128]{1,0:T(8,128)(2,1)}), bf16[3072,512]{1,0:T(8,128)(2,1)}) %all-gather.5.cloned.1.call-update) | async-done | bytes 3145744 | tf_op jit(solution)/shard_map/all_gather | solution.py:39
  555.7 182.2 %all-reduce.3.cloned.1.call-done = (f32[128,512]{1,0:T(8,128)}, f32[128,512]{1,0:T(8,128)}) async-done(((f32[128,512]{1,0:T(8,128)}, f32[128,512]{1,0:T(8,128)}), (f32[128,512]{1,0:T(8,128)}, f32[128,512]{1,0:T(8,128)})) %all-reduce.3.cloned.1.call-update) | async-done | bytes 524304 | tf_op jit(solution)/shard_map/psum | solution.py:63
  (52 shorter events, 19.3 us)
Async XLA Ops:
  7.2 1.6 copy-start
  13.5 10.2 %copy-start.8 = (s32[1,64]{1,0:T(1,128)S(1)}, s32[1,64]{1,0:T(1,128)}, u32[]{:S(2)}) copy-start(s32[1,64]{1,0:T(1,128)} %param.16) | copy-start | bytes 772
  36.9 13.6 %copy-start.9 = (s32[1,24]{1,0:T(1,128)S(1)}, s32[1,24]{1,0:T(1,128)}, u32[]{:S(2)}) copy-start(s32[1,24]{1,0:T(1,128)} %param.12) | copy-start | bytes 292
  36.9 14.3 %copy-start.7 = (s32[24,5]{0,1:T(8,128)S(1)}, s32[24,5]{0,1:T(8,128)}, u32[]{:S(2)}) copy-start(s32[24,5]{0,1:T(8,128)} %param.13) | copy-start | bytes 1444
  36.9 154.4 %all-to-all-start = ((bf16[64,3,128,128]{3,2,1,0:T(8,128)(2,1)}), bf16[64,3,128,128]{3,2,1,0:T(8,128)(2,1)}, u32[]{:S(2)}, u32[]{:S(2)}) async-start(bf16[64,3,128,128]{3,2,1,0:T(8,128)(2,1)} %get-tuple-element.7), calls=%async_computation | async-start | bytes 12582912 | tf_op jit(solution)/shard_map/all_to_all | solution.py:18
  50.4 224.4 %reduce-scatter.3.cloned.1.call-start = ((), (), s32[]{:S(2)}) async-start(), calls=%async_computation.4 | async-start | bytes 7864320 | tf_op jit(solution)/shard_map/reduce_scatter | solution.py:33
  203.5 4.5 copy-start.6
  211.6 146.8 %all-to-all-start.1 = ((bf16[64,3,128,128]{3,2,1,0:T(8,128)(2,1)}), bf16[64,3,128,128]{3,2,1,0:T(8,128)(2,1)}, u32[]{:S(2)}, u32[]{:S(2)}) async-start(bf16[64,3,128,128]{3,2,1,0:T(8,128)(2,1)} %get-tuple-element.8), calls=%async_computation.2 | async-start | bytes 12582912 | tf_op jit(solution)/shard_map/all_to_all | solution.py:18
  217.6 224.5 %reduce-scatter.5.cloned.1.call-start = ((), (), s32[]{:S(2)}) async-start(), calls=%async_computation.5 | async-start | bytes 7864320 | tf_op jit(solution)/shard_map/reduce_scatter | solution.py:33
  370.8 4.5 copy-start.5
  375.3 3.6 copy-start.2
  379.0 63.2 %copy-start.4 = (bf16[3072,128]{1,0:T(8,128)(2,1)S(1)}, bf16[3072,128]{1,0:T(8,128)(2,1)}, u32[]{:S(2)}) copy-start(bf16[3072,128]{1,0:T(8,128)(2,1)} %param.19) | copy-start | bytes 2359300
  379.0 111.3 %all-gather.3.cloned.1.call-start = ((), (), s32[]{:S(2)}) async-start(), calls=%async_computation.6 | async-start | bytes 3932160 | tf_op jit(solution)/shard_map/all_gather | solution.py:39
  445.6 106.9 %all-gather.5.cloned.1.call-start = ((), (), s32[]{:S(2)}) async-start(), calls=%async_computation.7 | async-start | bytes 3932160 | tf_op jit(solution)/shard_map/all_gather | solution.py:39
  496.9 3.6 slice-start
  500.5 3.5 copy-start.3
  505.6 232.3 %all-reduce.3.cloned.1.call-start = ((), (), s32[]{:S(2)}) async-start(), calls=%async_computation.8 | async-start | bytes 1048576 | tf_op jit(solution)/shard_map/psum | solution.py:63
  505.6 235.6 %copy-start.1 = (f32[4096,128]{1,0:T(8,128)S(1)}, f32[4096,128]{1,0:T(8,128)}, u32[]{:S(2)}) copy-start(f32[4096,128]{1,0:T(8,128)} %param.10) | copy-start | bytes 6291460
Sparse Core Ops, SparseCore 0:
  211.8 62.9 reduce-scatter.2
  379.1 62.9 reduce-scatter.4
  445.7 44.5 all-gather.2
  505.7 46.7 all-gather.4
  556.5 181.3 all-reduce.2
where the time goes:
time: 749 us; the launch traced here: 748 us
  waiting for transfers between devices  612 us (82%)
  local copies, waits for them, and re-layouts  35.9 us (5%)
  other arithmetic  33.3 us (4%)
  matrix products  32.8 us (4%)
  starting transfers between devices  19.8 us (3%)
  between operations  14 us (2%)
    all_to_all x2, waiting for transfers between devices, pull_one(): lax.all_to_all(outgoing(table, send_blocks, live), 'nodes', split_axis=0,...  222 us
    psum x1, waiting for transfers between devices, sum_grad(): return lax.psum(grad_part, 'nodes')  182 us
    reduce_scatter x2, waiting for transfers between devices, project(): return lax.psum_scatter(term, 'mp', scatter_dimension=1, tiled=True)  120 us
    all_gather x2, waiting for transfers between devices, backward_panel(): piece = lax.all_gather(delta, 'mp', axis=1, tiled=True)  88 us
    all_to_all x2, starting transfers between devices, pull_one(): lax.all_to_all(outgoing(table, send_blocks, live), 'nodes', split_axis=0,...  19.5 us
  transfers between devices with their start and end apart: 7, of which 7 were waited for; matrix products, arithmetic and copies ran while one was open for 1% of the time, Pallas kernels for 0%

commit v1 on v0

v1 whole, which is shorter than its diff:
```python
import functools

import jax
import jax.numpy as jnp
from jax import lax
from jax.experimental import pallas as pl
from jax.experimental.pallas import tpu as pltpu
from jax.sharding import Mesh
from jax.sharding import PartitionSpec as P

Y, Z, C, X = 4, 8, 2, 4
G = Y * C
BS = 128
NB = 24
TPR = 5
CAP = 3
HB = 32
ROWS = NB * BS
QUARTER = ROWS // X
STEP = 4
F32 = jnp.float32
BF16 = jnp.bfloat16
ANY = pl.BlockSpec(memory_space=pltpu.HBM)
VMEM = pl.BlockSpec(memory_space=pltpu.VMEM)
SMEM = pl.BlockSpec(memory_space=pltpu.SMEM)
LIMIT = 48 * 1024 * 1024


def call(kernel, out_shape, in_specs, out_specs, scratch, cost, name):
    return pl.pallas_call(
        kernel,
        out_shape=out_shape,
        in_specs=in_specs,
        out_specs=out_specs,
        scratch_shapes=scratch,
        compiler_params=pltpu.CompilerParams(vmem_limit_bytes=LIMIT),
        cost_estimate=pl.CostEstimate(flops=cost[0], bytes_accessed=cost[1], transcendentals=cost[2]),
        name=name,
    )


HEAD = 16
HALF = HB // 2
MIDDLE = HEAD + HALF * BS


def pack_kernel(blocks_ref, counts_ref, history_ref, after_ref, out_ref, wanted):
    del after_ref
    wanted[...] = jnp.zeros_like(wanted)
    blocks = blocks_ref[...]
    slot = lax.broadcasted_iota(jnp.int32, blocks.shape, 0)
    wanted[0:CAP, 0 : blocks.shape[1]] = jnp.where(slot < counts_ref[...], blocks, HB)
    out_ref[0:HEAD, :] = wanted[...].astype(F32).astype(BF16)

    def one(block, carry):
        rows = pl.multiple_of(block * BS, BS)
        out_ref[pl.ds(pl.multiple_of(HEAD + rows, HEAD), BS), :] = history_ref[pl.ds(rows, BS), :].astype(BF16)
        return carry

    lax.fori_loop(0, HB, one, 0)


def pack(blocks, counts, history, after):
    return call(
        pack_kernel,
        jax.ShapeDtypeStruct((HEAD + HB * BS, BS), BF16),
        [VMEM, VMEM, VMEM, ANY],
        VMEM,
        [pltpu.VMEM((HEAD, BS), jnp.int32)],
        (0, 3 * 1024 * 1024, 0),
        "pack",
    )(blocks, counts, history, after)


def stage_kernel(sizes, z_ref, *refs):
    count = len(sizes)
    total = sum(sizes)
    flat, (after_ref, out_ref, zeros, ints, asked, sem, head_sem) = refs[:total], refs[total:]
    del after_ref
    sources = [flat[sum(sizes[:s]) : sum(sizes[: s + 1])] for s in range(count)]
    for s in range(count):
        ints[s] = sources[s][0][0:HEAD, :].astype(F32).astype(jnp.int32)
        pltpu.make_async_copy(ints.at[s], asked.at[s], head_sem.at[s]).start()
    zeros[...] = jnp.zeros_like(zeros)
    for s in range(count):
        pltpu.make_async_copy(ints.at[s], asked.at[s], head_sem.at[s]).wait()
    mine = z_ref[0]

    def one(reader, carry):
        column = (reader // C) * (Z * C) + mine * C + lax.rem(reader, C)
        for s, source in enumerate(sources):
            limit = HB if len(source) == 1 else HALF
            for slot in range(CAP):
                block = asked[s, slot, column]
                target = out_ref.at[(reader * count + s) * CAP + slot]
                start = pl.multiple_of(HEAD + jnp.where(block < limit, block, 0) * BS, HEAD)

                @pl.when(block < limit)
                def _(source=source, start=start, target=target):
                    pltpu.make_async_copy(source[0].at[pl.ds(start, BS)], target, sem).start()

                if len(source) == 2:
                    late = jnp.logical_and(block >= HALF, block < HB)
                    begin = pl.multiple_of(jnp.where(late, block - HALF, 0) * BS, BS)

                    @pl.when(late)
                    def _(source=source, begin=begin, target=target):
                        pltpu.make_async_copy(source[1].at[pl.ds(begin, BS)], target, sem).start()

                @pl.when(block >= HB)
                def _(target=target):
                    pltpu.make_async_copy(zeros, target, sem).start()

        return carry

    lax.fori_loop(0, G, one, 0)
    pltpu.make_async_copy(out_ref, out_ref, sem).wait()


def stage(my_z, sources, after):
    count = len(sources)
    sizes = tuple(len(source) for source in sources)
    entries = G * CAP * count
    return call(
        functools.partial(stage_kernel, sizes),
        jax.ShapeDtypeStruct((entries, BS, BS), BF16),
        [SMEM] + [VMEM] * sum(sizes) + [ANY],
        ANY,
        [
            pltpu.VMEM((BS, BS), BF16),
            pltpu.VMEM((count, HEAD, BS), jnp.int32),
            pltpu.SMEM((count, HEAD, BS), jnp.int32),
            pltpu.SemaphoreType.DMA,
            pltpu.SemaphoreType.DMA((count,)),
        ],
        (0, 2 * entries * BS * BS * 2, 0),
        "stage",
    )(my_z, *[part for source in sources for part in source], after)


def aggregate_kernel(count, skip, local_ref, piece_ref, offset_ref, table_ref, *refs):
    halos, refs = refs[:count], refs[count:]
    tiles_ref, after_ref, out_ref, table, halo, tiles, table_sem, halo_sem, tiles_sem = refs
    del after_ref
    copy = pltpu.make_async_copy(table_ref.at[pl.ds(skip, table.shape[0])], table, table_sem)
    copy.start()

    def start(row, carry):
        pltpu.make_async_copy(tiles_ref.at[row], tiles.at[row], tiles_sem.at[row // STEP]).start()
        for slot in range(TPR - 2):
            use = row * (TPR - 2) + slot
            piece = piece_ref[use]
            offset = offset_ref[use]
            for number, source in enumerate(halos):

                @pl.when(piece == number)
                def _(source=source, slot=slot):
                    pltpu.make_async_copy(source.at[offset], halo.at[row, slot], halo_sem.at[row // STEP]).start()

        return carry

    lax.fori_loop(0, NB, start, 0)
    copy.wait()

    def compute(group, carry):
        rows = pl.ds(group * STEP, STEP)
        pltpu.make_async_copy(tiles_ref.at[rows], tiles.at[rows], tiles_sem.at[group]).wait()
        pltpu.make_async_copy(halo.at[rows], halo.at[rows], halo_sem.at[group]).wait()
        for k in range(STEP):
            row = group * STEP + k
            left = jnp.concatenate([tiles[row, t] for t in range(TPR)], axis=1)
            right = jnp.concatenate(
                [table[pl.ds(pl.multiple_of(local_ref[2 * row + t] * BS, BS), BS), :] for t in range(2)]
                + [halo[row, t] for t in range(TPR - 2)],
                axis=0,
            )
            summed = jnp.dot(left, right, preferred_element_type=F32)
            out_ref[pl.ds(pl.multiple_of(row * BS, BS), BS), :] = summed.astype(BF16)
        return carry

    lax.fori_loop(0, NB // STEP, compute, 0)


def aggregate(skip, table, halos, tiles, local, piece, offset, after):
    return call(
        functools.partial(aggregate_kernel, len(halos), skip),
        jax.ShapeDtypeStruct((ROWS, BS), BF16),
        [SMEM] * 3 + [ANY] * (len(halos) + 3),
        VMEM,
        [
            pltpu.VMEM((table.shape[0] - skip, BS), BF16),
            pltpu.VMEM((NB, TPR - 2, BS, BS), BF16),
            pltpu.VMEM((NB, TPR, BS, BS), BF16),
            pltpu.SemaphoreType.DMA,
            pltpu.SemaphoreType.DMA((NB // STEP,)),
            pltpu.SemaphoreType.DMA((NB // STEP,)),
        ],
        (2 * NB * TPR * BS**3, 2 * NB * TPR * BS * BS * 2, 0),
        "aggregate",
    )(local, piece, offset, table, *halos, tiles, after)


def sigmoid(value):
    return 1.0 / (1.0 + jnp.exp(-value))


def first_kernel(s0, s1, s2, far0, far1, weight_ref, hidden_ref, slope_ref):
    weight = weight_ref[...]
    step = 256
    half = ROWS // 2 // step

    def one(far, begin, row, carry):
        rows = pl.ds(pl.multiple_of((row + begin) * step, step), step)
        far_rows = pl.ds(pl.multiple_of(row * step, step), step)
        left = jnp.concatenate([s0[rows, :], s1[rows, :], s2[rows, :], far[far_rows, :]], axis=1)
        pre = jnp.dot(left, weight, preferred_element_type=F32)
        sig = sigmoid(pre)
        hidden_ref[rows, :] = (pre * sig).astype(BF16)
        slope_ref[rows, :] = sig * (1.0 + pre * (1.0 - sig))
        return carry

    lax.fori_loop(0, half, functools.partial(one, far0, 0), 0)
    lax.fori_loop(0, half, functools.partial(one, far1, half), 0)


def first_layer(summed, weight):
    return call(
        first_kernel,
        (jax.ShapeDtypeStruct((ROWS, BS), BF16), jax.ShapeDtypeStruct((ROWS, BS), F32)),
        [VMEM] * 6,
        (VMEM, VMEM),
        [],
        (2 * ROWS * 512 * BS, 6 * 1024 * 1024, ROWS * BS),
        "first_layer",
    )(*summed, weight)


def second_kernel(summed_ref, weight_ref, cot_ref, out_ref, delta_ref, back_ref):
    step = 128

    def one(row, carry):
        rows = pl.ds(pl.multiple_of(row * step, step), step)
        left = jnp.concatenate([summed_ref[k, rows, :] for k in range(X)], axis=1)
        cot = jnp.concatenate([cot_ref[k, rows, :] for k in range(X)], axis=1)
        pre = jnp.dot(left, weight_ref[...], preferred_element_type=F32)
        sig = sigmoid(pre)
        out = (pre * sig).astype(BF16)
        delta = (cot.astype(F32) * (sig * (1.0 + pre * (1.0 - sig)))).astype(BF16)
        back = lax.dot_general(
            delta, weight_ref[...], (((1,), (1,)), ((), ())), preferred_element_type=F32
        ).astype(BF16)
        delta_ref[rows, :] = delta
        for k in range(X):
            out_ref[k, rows, :] = out[:, k * BS : (k + 1) * BS]
            back_ref[k, rows, :] = back[:, k * BS : (k + 1) * BS]
        return carry

    lax.fori_loop(0, QUARTER // step, one, 0)


def second_layer(summed, weight, cot):
    piece = jax.ShapeDtypeStruct((X, QUARTER, BS), BF16)
    return call(
        second_kernel,
        (piece, jax.ShapeDtypeStruct((QUARTER, X * BS), BF16), piece),
        [VMEM] * 3,
        (VMEM,) * 3,
        [],
        (4 * QUARTER * 512 * 512, 5 * 1024 * 1024, QUARTER * 512),
        "second_layer",
    )(summed, weight, cot)


def grad_second_kernel(summed_ref, delta_ref, out_ref):
    for k in range(X):
        out_ref[k * BS : (k + 1) * BS, :] = lax.dot_general(
            summed_ref[k], delta_ref[...], (((0,), (0,)), ((), ())), preferred_element_type=F32
        ).astype(BF16)


def grad_second_part(summed, delta):
    return call(
        grad_second_kernel,
        jax.ShapeDtypeStruct((X * BS, X * BS), BF16),
        [VMEM] * 2,
        VMEM,
        [],
        (2 * QUARTER * 512 * 512, 3 * 1024 * 1024, 0),
        "grad_second",
    )(summed, delta)


def prepare_kernel(x_ref, tiles_ref, s0, s1, s2, far0, far1, turned_ref, summed_ref, tiles, sem):
    def start(row, carry):
        pltpu.make_async_copy(tiles_ref.at[row, pl.ds(0, 2)], tiles.at[row], sem).start()
        return carry

    lax.fori_loop(0, NB, start, 0)
    x = x_ref[0]
    half = ROWS // 2
    for source, step, begin in ((s0, 0, 0), (s1, X - 1, 0), (s2, 1, 0), (far0, 2, 0), (far1, 2, half)):
        place = pl.ds(pl.multiple_of(lax.rem(x + step, X) * BS, BS), BS)

        def one(block, carry, source=source, begin=begin, place=place):
            rows = pl.ds(pl.multiple_of(block * BS, BS), BS)
            columns = pl.ds(pl.multiple_of(begin + block * BS, BS), BS)
            summed_ref[place, columns] = source[rows, :].T
            return carry

        lax.fori_loop(0, source.shape[0] // BS, one, 0, unroll=4)
    pltpu.make_async_copy(tiles, tiles, sem).wait()

    def turn_tiles(row, carry):
        for t in range(2):
            turned_ref[row, pl.ds(t * BS, BS), :] = tiles[row, t].T
        return carry

    lax.fori_loop(0, NB, turn_tiles, 0, unroll=2)


def prepare(my_x, tiles, summed):
    return call(
        prepare_kernel,
        (jax.ShapeDtypeStruct((NB, 2 * BS, BS), BF16), jax.ShapeDtypeStruct((X * BS, ROWS), BF16)),
        [SMEM, ANY] + [VMEM] * 5,
        (VMEM, VMEM),
        [pltpu.VMEM((NB, 2, BS, BS), BF16), pltpu.SemaphoreType.DMA],
        (0, 10 * 1024 * 1024, 0),
        "prepare",
    )(my_x, tiles, *summed)


def last_kernel(other_ref, back_ref, turned_ref, slope_ref, summed_ref, after_ref, out_ref, total, delta):
    del after_ref
    total[...] = jnp.zeros_like(total)

    def spread(group, carry):
        terms = []
        for k in range(STEP):
            row = group * STEP + k
            rows = pl.ds(pl.multiple_of(row * BS, BS), BS)
            terms.append(jnp.dot(turned_ref[row], back_ref[rows, :], preferred_element_type=F32))
        for k in range(STEP):
            row = group * STEP + k
            total[row] += terms[k][:BS]
            total[other_ref[row]] += terms[k][BS:]
        return carry

    lax.fori_loop(0, NB // STEP, spread, 0)

    def scale(row, carry):
        rows = pl.ds(pl.multiple_of(row * BS, BS), BS)
        delta[rows, :] = (total[row] * slope_ref[rows, :]).astype(BF16)
        return carry

    lax.fori_loop(0, NB, scale, 0, unroll=4)
    out_ref[...] = jnp.dot(summed_ref[...], delta[...], preferred_element_type=F32).astype(BF16)


def last_part(other, back, turned, slope, summed, after):
    return call(
        last_kernel,
        jax.ShapeDtypeStruct((X * BS, BS), BF16),
        [SMEM, VMEM, VMEM, VMEM, VMEM, ANY],
        VMEM,
        [pltpu.VMEM((NB, BS, BS), F32), pltpu.VMEM((ROWS, BS), BF16)],
        (2 * NB * 2 * BS**3 + 2 * ROWS * 512 * BS, 8 * 1024 * 1024, 0),
        "last_part",
    )(other, back, turned, slope, summed, after)


def join_kernel(first_ref, second_ref, after_ref, out_ref):
    del after_ref
    out_ref[:, 0:BS] = first_ref[...]
    out_ref[:, BS:] = second_ref[...]


def join(first, second, after):
    return call(
        join_kernel,
        jax.ShapeDtypeStruct((X * BS, (X + 1) * BS), BF16),
        [VMEM, VMEM, ANY],
        VMEM,
        [],
        (0, 1024 * 1024, 0),
        "join",
    )(first, second, after)


def shift(value, step):
    return lax.ppermute(value, "z", [(i, (i + step) % Z) for i in range(Z)])


def turn(value, step):
    return lax.ppermute(value, "mp", [(i, (i + step) % X) for i in range(X)])


def gather_features(value):
    left, right = turn(value, 1), turn(value, -1)
    half = value.shape[0] // 2
    far = [turn(left[:half], 1), turn(right[half:], -1)]
    return value, left, right, far[0], far[1]


def exchange(value, axes):
    return lax.all_to_all(value, axes, split_axis=0, concat_axis=0, tiled=True)


def plane(staged):
    per = staged.shape[0] // G
    got = exchange(staged.reshape(G, per * BS, BS), ("y", "core"))
    return got.reshape(staged.shape)


def ring(table):
    steps = [(table, table)]
    for _ in range(1, Z // 2):
        up, down = steps[-1]
        steps.append((shift(up, 1), shift(down, -1)))
    up, down = steps[-1]
    return steps, (shift(up[:MIDDLE], 1), shift(down[MIDDLE:], -1))


def body(
    input_history,
    hidden_history,
    batch_blocks,
    tile_columns,
    tile_values,
    send_blocks,
    send_counts,
    weight_first,
    weight_second,
    cotangent,
):
    my_z = lax.axis_index("z").astype(jnp.int32)
    my_x = lax.axis_index("mp").astype(jnp.int32)
    blocks = send_blocks[0].T
    table_input = pack(blocks, send_counts, input_history, tile_columns)
    steps, far = ring(table_input)
    table_hidden = pack(blocks, send_counts, hidden_history, far[0])
    steps_hidden, far_hidden = ring(table_hidden)

    def piece_of(sources, after):
        return plane(stage(my_z.reshape(1), [s if isinstance(s, tuple) else (s,) for s in sources], after))

    halo_input = [
        piece_of(steps[1], tile_columns),
        piece_of((table_input,) + steps[2], tile_columns),
        piece_of((far,) + steps[3], steps_hidden[1][0]),
    ]
    halo_hidden = [
        piece_of(steps_hidden[1], tile_columns),
        piece_of((table_hidden,) + steps_hidden[2], tile_columns),
        piece_of(steps_hidden[3], tile_columns),
        piece_of((far_hidden,), tile_columns),
    ]

    use = tile_columns[:, 2:] - NB
    owner, slot = use // CAP, use % CAP
    group = (owner // (Z * C)) * C + owner % C
    distance = ((owner // C) % Z - my_z) % Z
    near = jnp.minimum(distance, Z - distance)
    from_below = (distance < Z // 2).astype(jnp.int32)
    single = jnp.logical_or(distance == 0, distance == Z // 2)
    third = jnp.where(single, 0, 1 + from_below)
    piece_hidden = jnp.where(near == 0, 1, near - 1)
    piece_input = jnp.minimum(piece_hidden, 2)
    even = group * 2 + from_below
    place_input = jnp.where(near == 1, even, group * 3 + third)
    place_hidden = jnp.where(
        jnp.logical_or(near == 1, near == 3), even, jnp.where(near == Z // 2, group, group * 3 + third)
    )
    where_input = (piece_input.reshape(-1), (place_input * CAP + slot).reshape(-1))
    where_hidden = (piece_hidden.reshape(-1), (place_hidden * CAP + slot).reshape(-1))
    other = tile_columns[:, 1]
    mine = jnp.arange(NB, dtype=jnp.int32)
    local_first = batch_blocks[0][jnp.stack([mine, other], axis=1)].reshape(-1)
    local_second = jnp.stack([mine, other], axis=1).reshape(-1)

    weights = gather_features(jnp.concatenate([weight_first, weight_second]))
    weights = [weights[0], weights[1], weights[2], jnp.concatenate(weights[3:])]
    columns = jnp.concatenate([lax.dynamic_slice(w, (0, my_x * BS), (BS, BS)) for w in weights])
    order = jnp.stack([(-my_x) % X, (1 - my_x) % X, (2 - my_x) % X, (3 - my_x) % X])
    order = jnp.array([0, 2, 3, 1], jnp.int32)[order]
    weight_all = jnp.stack([w[BS:] for w in weights])[order].reshape(X * BS, X * BS)
    cot_rows = exchange(cotangent.reshape(X, QUARTER, BS), "mp")

    summed_first = aggregate(HEAD, table_input, halo_input, tile_values, local_first, *where_input, cot_rows)
    all_first = gather_features(summed_first)
    hidden_first, slope_first = first_layer(all_first, columns)
    turned_tiles, turned_first = prepare(my_x.reshape(1), tile_values, all_first)
    summed_second = aggregate(
        0, hidden_first, halo_hidden, tile_values, local_second, *where_hidden, turned_tiles
    )
    rows_second = exchange(summed_second.reshape(X, QUARTER, BS), "mp")
    out_rows, delta_rows, back_rows = second_layer(rows_second, weight_all, cot_rows)
    back_second = exchange(back_rows, "mp").reshape(ROWS, BS)
    part_second = grad_second_part(rows_second, delta_rows)
    part_first = last_part(other, back_second, turned_tiles, slope_first, turned_first, part_second)
    layer_out = exchange(out_rows, "mp").reshape(ROWS, BS)

    dealt = X * G
    got = join(part_first, part_second, layer_out).reshape(dealt, -1, (X + 1) * BS)
    got = exchange(got, ("mp", "y", "core")).astype(F32)
    got_second = got[:, :, BS:].sum(0)
    got_first = got[:, :, :BS].reshape(X, G, -1, BS).sum(1).transpose(1, 0, 2).reshape(-1, X * BS)
    both = jnp.concatenate([got_first, got_second], axis=0).astype(BF16)
    both = exchange(jnp.broadcast_to(both[None], (Z,) + both.shape), "z").astype(F32).sum(0)
    both = exchange(jnp.broadcast_to(both[None], (G,) + both.shape), ("y", "core"))
    both = both.reshape(G, 2, -1, X * BS)
    grad_first = both[:, 0].reshape(BS, X * BS)
    grad_second = both[:, 1].reshape(BS, X * BS)
    return (layer_out, grad_first, grad_second)


def solution(mesh):
    inner = Mesh(mesh.devices.reshape(Y, Z, C, X), ("y", "z", "core", "mp"))
    nodes = ("y", "z", "core")
    placed = (
        P(nodes, "mp"),
        P(nodes, "mp"),
        P(nodes, None),
        P(nodes, None),
        P(nodes, None, None, None),
        P(nodes, None, None),
        P(nodes, None),
        P("mp", None),
        P("mp", None),
        P(nodes, "mp"),
    )
    return jax.shard_map(
        body,
        mesh=inner,
        in_specs=placed,
        out_specs=(P(nodes, "mp"), P("mp", None), P("mp", None)),
        check_vma=False,
    )
```

time: 749 us -> 441 us (0.59)
  waiting for transfers between devices: 612 us -> 193 us
  starting transfers between devices: 19.8 us -> 89.3 us
  blocking collectives: 0 us -> 64.6 us
  Pallas kernels: 0 us -> 49.6 us
  matrix products: 32.8 us -> 0 us
  other arithmetic: 33.3 us -> 0.5 us
  between operations: 14 us -> 1.36 us
    all_to_all x2 -> x10, waiting for transfers between devices: 222 us -> 14.1 us  [exchange(): return lax.all_to_all(value, axes, split_axis=0, concat_axis=0, tiled=True)]
    psum x1 -> x0, waiting for transfers between devices: 182 us -> none  [sum_grad(): return lax.psum(grad_part, 'nodes')]
    ppermute x0 -> x24, waiting for transfers between devices: none -> 179 us  [the longest x16 151 us: shift(): return lax.ppermute(value, 'z', [(i, (i + step) % Z) for i in range(Z)])]
    reduce_scatter x2 -> x0, waiting for transfers between devices: 120 us -> none  [project(): return lax.psum_scatter(term, 'mp', scatter_dimension=1, tiled=True)]
    all_gather x2 -> x0, waiting for transfers between devices: 88 us -> none  [backward_panel(): piece = lax.all_gather(delta, 'mp', axis=1, tiled=True)]
    all_to_all x0 -> x4, blocking collectives: none -> 64.6 us  [exchange(): return lax.all_to_all(value, axes, split_axis=0, concat_axis=0, tiled=True)]
    pallas_call x0 -> x17, Pallas kernels: none -> 49.6 us  [the longest x7 22.6 us: stage(): call(functools.partial(stage_kernel, sizes), jax.ShapeDtypeStruct((entrie...]
    all_to_all x2 -> x10, starting transfers between devices: 19.5 us -> 54.6 us  [exchange(): return lax.all_to_all(value, axes, split_axis=0, concat_axis=0, tiled=True)]
  transfers between devices with their start and end apart: 7 -> 34, of which waited for: 7 -> 18; matrix products, arithmetic and copies ran while one was open for 1% -> 2% of each run, Pallas kernels for 0% -> 9%
where the time goes in v1:
time: 441 us; the launch traced here: 439 us
  waiting for transfers between devices  193 us (44%)
  starting transfers between devices  89.3 us (20%)
  blocking collectives  64.6 us (15%)
  Pallas kernels  49.6 us (11%)
  local copies, waits for them, and re-layouts  40.6 us (9%)
    ppermute x16, waiting for transfers between devices, shift(): return lax.ppermute(value, 'z', [(i, (i + step) % Z) for i in range(Z)])  151 us
    all_to_all x4, blocking collectives, exchange(): return lax.all_to_all(value, axes, split_axis=0, concat_axis=0, tiled=True)  64.6 us
    all_to_all x10, starting transfers between devices, exchange(): return lax.all_to_all(value, axes, split_axis=0, concat_axis=0, tiled=True)  54.6 us
    unnamed x94, local copies, waits for them, and re-layouts  29.9 us
    ppermute x8, waiting for transfers between devices, turn(): return lax.ppermute(value, 'mp', [(i, (i + step) % X) for i in range(X)])  28.4 us
    ppermute x16, starting transfers between devices, shift(): return lax.ppermute(value, 'z', [(i, (i + step) % Z) for i in range(Z)])  25 us
    pallas_call x7, Pallas kernels, stage(): call(functools.partial(stage_kernel, sizes), jax.ShapeDtypeStruct((entrie...  22.6 us
    all_to_all x10, waiting for transfers between devices, exchange(): return lax.all_to_all(value, axes, split_axis=0, concat_axis=0, tiled=True)  14.1 us
  transfers between devices with their start and end apart: 34, of which 18 were waited for; matrix products, arithmetic and copies ran while one was open for 2% of the time, Pallas kernels for 9%

profile of v1, /device:TPU:1, one launch (start us, length us, event | category | flops | bytes accessed | tf_op | source)
XLA Modules:
  0.0 439.0 jit_solution(9482260744710540338)
XLA Ops:
  15.1 19.0 %collective-permute-done.refs_0_ = bf16[4112,128]{1,0:T(8,128)(2,1)} collective-permute-done((bf16[4112,128]{1,0:T(8,128)(2,1)S(1)}, bf16[4112,128]{1,0:T(8,128)(2,1)}, u32[]{:S(2)}, u32[]{:S(2)}) %collective-permute-start) | collective-permute-done | bytes 1052704 | tf_op jit(solution)/shard_map/ppermute | solution.py:391
  41.3 5.7 %all-to-all-start = ((bf16[8,768,128]{2,1,0:T(8,128)(2,1)}), bf16[8,768,128]{2,1,0:T(8,128)(2,1)S(1)}, u32[]{:S(2)}, u32[]{:S(2)}) async-start(bf16[8,768,128]{2,1,0:T(8,128)(2,1)} %bitcast.68), calls=%async_computation | async-start | bytes 3145728 | tf_op jit(solution)/shard_map/all_to_all | solution.py:406
  50.0 9.2 %collective-permute-done.2.refs_1_ = bf16[4112,128]{1,0:T(8,128)(2,1)} collective-permute-done((bf16[4112,128]{1,0:T(8,128)(2,1)}, bf16[4112,128]{1,0:T(8,128)(2,1)}, u32[]{:S(2)}, u32[]{:S(2)}) %collective-permute-start.2) | collective-permute-done | bytes 1052704 | tf_op jit(solution)/shard_map/ppermute | solution.py:391
  59.1 13.8 %collective-permute-done.3.refs_2_ = bf16[4112,128]{1,0:T(8,128)(2,1)} collective-permute-done((bf16[4112,128]{1,0:T(8,128)(2,1)}, bf16[4112,128]{1,0:T(8,128)(2,1)}, u32[]{:S(2)}, u32[]{:S(2)}) %collective-permute-start.3) | collective-permute-done | bytes 1052704 | tf_op jit(solution)/shard_map/ppermute | solution.py:391
  76.9 5.2 %all-to-all-start.1 = ((bf16[8,1152,128]{2,1,0:T(8,128)(2,1)}), bf16[8,1152,128]{2,1,0:T(8,128)(2,1)}, u32[]{:S(2)}, u32[]{:S(2)}) async-start(bf16[8,1152,128]{2,1,0:T(8,128)(2,1)} %bitcast.6), calls=%async_computation.1 | async-start | bytes 4718592 | tf_op jit(solution)/shard_map/all_to_all | solution.py:406
  84.4 11.7 %collective-permute-done.5.after_ref.refs_0_ = bf16[2064,128]{1,0:T(8,128)(2,1)S(1)} collective-permute-done((bf16[2064,128]{1,0:T(8,128)(2,1)S(1)}, bf16[2064,128]{1,0:T(8,128)(2,1)S(1)}, u32[]{:S(2)}, u32[]{:S(2)}) %collective-permute-start.5) | collective-permute-done | bytes 528416 | tf_op jit(solution)/shard_map/ppermute | solution.py:391
  105.4 18.6 %collective-permute-done.8.refs_4_.refs_0_ = bf16[4112,128]{1,0:T(8,128)(2,1)S(1)} collective-permute-done((bf16[4112,128]{1,0:T(8,128)(2,1)S(1)}, bf16[4112,128]{1,0:T(8,128)(2,1)S(1)}, u32[]{:S(2)}, u32[]{:S(2)}) %collective-permute-start.8) | collective-permute-done | bytes 1052704 | tf_op jit(solution)/shard_map/ppermute | solution.py:391
  131.6 9.1 %all-to-all-start.4 = ((bf16[8,768,128]{2,1,0:T(8,128)(2,1)}), bf16[8,768,128]{2,1,0:T(8,128)(2,1)}, u32[]{:S(2)}, u32[]{:S(2)}) async-start(bf16[8,768,128]{2,1,0:T(8,128)(2,1)} %bitcast.67), calls=%async_computation.4 | async-start | bytes 3145728 | tf_op jit(solution)/shard_map/all_to_all | solution.py:406
  140.7 6.9 %collective-permute-done.6.refs_3_ = bf16[4112,128]{1,0:T(8,128)(2,1)} collective-permute-done((bf16[4112,128]{1,0:T(8,128)(2,1)}, bf16[4112,128]{1,0:T(8,128)(2,1)}, u32[]{:S(2)}, u32[]{:S(2)}) %collective-permute-start.6) | collective-permute-done | bytes 1052704 | tf_op jit(solution)/shard_map/ppermute | solution.py:391
  150.2 12.1 %collective-permute-done.7.refs_1_ = bf16[2048,128]{1,0:T(8,128)(2,1)S(1)} collective-permute-done((bf16[2048,128]{1,0:T(8,128)(2,1)S(1)}, bf16[2048,128]{1,0:T(8,128)(2,1)S(1)}, u32[]{:S(2)}, u32[]{:S(2)}) %collective-permute-start.7) | collective-permute-done | bytes 524320 | tf_op jit(solution)/shard_map/ppermute | solution.py:391
  167.4 6.5 %all-to-all-start.2 = ((bf16[8,1152,128]{2,1,0:T(8,128)(2,1)}), bf16[8,1152,128]{2,1,0:T(8,128)(2,1)}, u32[]{:S(2)}, u32[]{:S(2)}) async-start(bf16[8,1152,128]{2,1,0:T(8,128)(2,1)} %bitcast.74), calls=%async_computation.2 | async-start | bytes 4718592 | tf_op jit(solution)/shard_map/all_to_all | solution.py:406
  176.6 23.5 %collective-permute-done.18.refs_1_ = bf16[4112,128]{1,0:T(8,128)(2,1)S(1)} collective-permute-done((bf16[4112,128]{1,0:T(8,128)(2,1)}, bf16[4112,128]{1,0:T(8,128)(2,1)S(1)}, u32[]{:S(2)}, u32[]{:S(2)}) %collective-permute-start.18) | collective-permute-done | bytes 1052704 | tf_op jit(solution)/shard_map/ppermute | solution.py:391
  205.6 5.6 %all-to-all-start.5 = ((bf16[8,1152,128]{2,1,0:T(8,128)(2,1)}), bf16[8,1152,128]{2,1,0:T(8,128)(2,1)}, u32[]{:S(2)}, u32[]{:S(2)}) async-start(bf16[8,1152,128]{2,1,0:T(8,128)(2,1)} %bitcast.13), calls=%async_computation.5 | async-start | bytes 4718592 | tf_op jit(solution)/shard_map/all_to_all | solution.py:406
  213.9 23.6 %collective-permute-done.20.refs_0_ = bf16[4112,128]{1,0:T(8,128)(2,1)S(1)} collective-permute-done((bf16[4112,128]{1,0:T(8,128)(2,1)}, bf16[4112,128]{1,0:T(8,128)(2,1)S(1)}, u32[]{:S(2)}, u32[]{:S(2)}) %collective-permute-start.20) | collective-permute-done | bytes 1052704 | tf_op jit(solution)/shard_map/ppermute | solution.py:391
  242.4 10.1 %collective-permute-done.23.refs_1_ = bf16[2048,128]{1,0:T(8,128)(2,1)S(1)} collective-permute-done((bf16[2048,128]{1,0:T(8,128)(2,1)S(1)}, bf16[2048,128]{1,0:T(8,128)(2,1)S(1)}, u32[]{:S(2)}, u32[]{:S(2)}) %collective-permute-start.23) | collective-permute-done | bytes 524320 | tf_op jit(solution)/shard_map/ppermute | solution.py:391
  254.2 6.0 %all-to-all-start.7 = ((bf16[8,384,128]{2,1,0:T(8,128)(2,1)}), bf16[8,384,128]{2,1,0:T(8,128)(2,1)}, u32[]{:S(2)}, u32[]{:S(2)}) async-start(bf16[8,384,128]{2,1,0:T(8,128)(2,1)} %bitcast.17), calls=%async_computation.7 | async-start | bytes 1572864 | tf_op jit(solution)/shard_map/all_to_all | solution.py:406
  266.8 5.7 %all-to-all-done.7 = bf16[8,384,128]{2,1,0:T(8,128)(2,1)} async-done(((bf16[8,384,128]{2,1,0:T(8,128)(2,1)}), bf16[8,384,128]{2,1,0:T(8,128)(2,1)}, u32[]{:S(2)}, u32[]{:S(2)}) %all-to-all-start.7) | async-done | bytes 786464 | tf_op jit(solution)/shard_map/all_to_all | solution.py:406
  289.8 19.5 %collective-permute-done.14 = bf16[256,512]{1,0:T(8,128)(2,1)S(1)} collective-permute-done((bf16[256,512]{1,0:T(8,128)(2,1)}, bf16[256,512]{1,0:T(8,128)(2,1)S(1)}, u32[]{:S(2)}, u32[]{:S(2)}) %collective-permute-start.14) | collective-permute-done | bytes 262176 | tf_op jit(solution)/shard_map/ppermute | solution.py:395
  318.6 8.2 %collective-permute-done.11.far0 = bf16[1536,128]{1,0:T(8,128)(2,1)S(1)} collective-permute-done((bf16[1536,128]{1,0:T(8,128)(2,1)S(1)}, bf16[1536,128]{1,0:T(8,128)(2,1)S(1)}, u32[]{:S(2)}, u32[]{:S(2)}) %collective-permute-start.11) | collective-permute-done | bytes 393248 | tf_op jit(solution)/shard_map/ppermute | solution.py:395
  347.5 8.3 %all-to-all-done.8.summed_ref = bf16[4,768,128]{2,1,0:T(8,128)(2,1)S(1)} async-done(((bf16[4,768,128]{2,1,0:T(8,128)(2,1)}), bf16[4,768,128]{2,1,0:T(8,128)(2,1)S(1)}, u32[]{:S(2)}, u32[]{:S(2)}) %all-to-all-start.8) | async-done | bytes 786464 | tf_op jit(solution)/shard_map/all_to_all | solution.py:406
  359.5 11.7 %all_to_all.70 = bf16[4,768,128]{2,1,0:T(8,128)(2,1)} all-to-all(bf16[4,768,128]{2,1,0:T(8,128)(2,1)S(1)} %get-tuple-element.13), channel_id=1, replica_groups=mesh['y'=4,'z'=8,'core'=2,'mp'=4] {'mp'}, dimensions={0} | all-to-all | bytes 1572864 | tf_op jit(solution)/shard_map/all_to_all | solution.py:406
  384.1 23.2 %all_to_all.71 = bf16[32,16,640]{2,1,0:T(8,128)(2,1)S(1)} all-to-all(bf16[32,16,640]{2,1,0:T(8,128)(2,1)S(1)} %bitcast.70), channel_id=1, replica_groups=mesh['y'=4,'z'=8,'core'=2,'mp'=4] {'mp','y','core'}, dimensions={0} | all-to-all | bytes 1310720 | tf_op jit(solution)/shard_map/all_to_all | solution.py:406
  407.5 17.5 %all_to_all.72 = bf16[8,32,512]{2,1,0:T(8,128)(2,1)S(1)} all-to-all(bf16[8,32,512]{2,1,0:T(8,128)(2,1)S(1)} %broadcast_in_dim.7), channel_id=1, replica_groups=mesh['y'=4,'z'=8,'core'=2,'mp'=4] {'z'}, dimensions={0} | all-to-all | bytes 524288 | tf_op jit(solution)/shard_map/all_to_all | solution.py:406
  425.1 12.2 %all_to_all.73 = f32[8,32,512]{2,1,0:T(8,128)S(1)} all-to-all(f32[8,32,512]{2,1,0:T(8,128)S(1)} %broadcast_in_dim.8), channel_id=1, replica_groups=mesh['y'=4,'z'=8,'core'=2,'mp'=4] {'y','core'}, dimensions={0} | all-to-all | bytes 1048576 | tf_op jit(solution)/shard_map/all_to_all | solution.py:406
  (210 shorter events, 144.7 us)
Async XLA Ops:
  4.5 29.6 %collective-permute-start = (bf16[4112,128]{1,0:T(8,128)(2,1)S(1)}, bf16[4112,128]{1,0:T(8,128)(2,1)}, u32[]{:S(2)}, u32[]{:S(2)}) collective-permute-start(bf16[4112,128]{1,0:T(8,128)(2,1)S(1)} %pack.2.refs_0_.table_ref), channel_id=1, source_target_pairs={{0,8},{8,16},{16,24},{24,32},{32,40},{40,48},{48,56},{56,0},{1,9},... | collective-permute-start | bytes 3158024 | tf_op jit(solution)/shard_map/ppermute | solution.py:391
  7.1 27.0 %collective-permute-start.1 = (bf16[4112,128]{1,0:T(8,128)(2,1)S(1)}, bf16[4112,128]{1,0:T(8,128)(2,1)S(1)}, u32[]{:S(2)}, u32[]{:S(2)}) collective-permute-start(bf16[4112,128]{1,0:T(8,128)(2,1)S(1)} %pack.2.refs_0_.table_ref), channel_id=1, source_target_pairs={{0,56},{8,0},{16,8},{24,16},{32,24},{40,32},{48,40},{56,48},{1,57}... | collective-permute-start | bytes 3158024 | tf_op jit(solution)/shard_map/ppermute | solution.py:391
  11.1 29.3 %all-to-all-start.3 = ((bf16[4,768,128]{2,1,0:T(8,128)(2,1)}), bf16[4,768,128]{2,1,0:T(8,128)(2,1)S(1)}, u32[]{:S(2)}, u32[]{:S(2)}) async-start(bf16[4,768,128]{2,1,0:T(8,128)(2,1)} %bitcast.76), calls=%async_computation.3 | async-start | bytes 1572864 | tf_op jit(solution)/shard_map/all_to_all | solution.py:406
  34.1 25.0 %collective-permute-start.2 = (bf16[4112,128]{1,0:T(8,128)(2,1)}, bf16[4112,128]{1,0:T(8,128)(2,1)}, u32[]{:S(2)}, u32[]{:S(2)}) collective-permute-start(bf16[4112,128]{1,0:T(8,128)(2,1)} %collective-permute-done.refs_0_), channel_id=1, source_target_pairs={{0,8},{8,16},{16,24},{24,32},{32,40},{40,48},{48,56},{56,0},{1,9},... | collective-permute-start | bytes 3158024 | tf_op jit(solution)/shard_map/ppermute | solution.py:391
  41.3 35.6 %all-to-all-start = ((bf16[8,768,128]{2,1,0:T(8,128)(2,1)}), bf16[8,768,128]{2,1,0:T(8,128)(2,1)S(1)}, u32[]{:S(2)}, u32[]{:S(2)}) async-start(bf16[8,768,128]{2,1,0:T(8,128)(2,1)} %bitcast.68), calls=%async_computation | async-start | bytes 3145728 | tf_op jit(solution)/shard_map/all_to_all | solution.py:406
  47.0 25.9 %collective-permute-start.3 = (bf16[4112,128]{1,0:T(8,128)(2,1)}, bf16[4112,128]{1,0:T(8,128)(2,1)}, u32[]{:S(2)}, u32[]{:S(2)}) collective-permute-start(bf16[4112,128]{1,0:T(8,128)(2,1)} %copy-done.29), channel_id=1, source_target_pairs={{0,56},{8,0},{16,8},{24,16},{32,24},{40,32},{48,40},{56,48},{1,57}... | collective-permute-start | bytes 3158024 | tf_op jit(solution)/shard_map/ppermute | solution.py:391
  59.1 24.1 %collective-permute-start.4 = (bf16[4112,128]{1,0:T(8,128)(2,1)}, bf16[4112,128]{1,0:T(8,128)(2,1)}, u32[]{:S(2)}, u32[]{:S(2)}) collective-permute-start(bf16[4112,128]{1,0:T(8,128)(2,1)} %collective-permute-done.2.refs_1_), channel_id=1, source_target_pairs={{0,8},{8,16},{16,24},{24,32},{32,40},{40,48},{48,56},{56,0},{1,9},... | collective-permute-start | bytes 3158024 | tf_op jit(solution)/shard_map/ppermute | solution.py:391
  76.9 54.6 %all-to-all-start.1 = ((bf16[8,1152,128]{2,1,0:T(8,128)(2,1)}), bf16[8,1152,128]{2,1,0:T(8,128)(2,1)}, u32[]{:S(2)}, u32[]{:S(2)}) async-start(bf16[8,1152,128]{2,1,0:T(8,128)(2,1)} %bitcast.6), calls=%async_computation.1 | async-start | bytes 4718592 | tf_op jit(solution)/shard_map/all_to_all | solution.py:406
  98.6 25.4 %collective-permute-start.8 = (bf16[4112,128]{1,0:T(8,128)(2,1)S(1)}, bf16[4112,128]{1,0:T(8,128)(2,1)S(1)}, u32[]{:S(2)}, u32[]{:S(2)}) collective-permute-start(bf16[4112,128]{1,0:T(8,128)(2,1)S(1)} %pack.3.refs_0_), channel_id=1, source_target_pairs={{0,8},{8,16},{16,24},{24,32},{32,40},{40,48},{48,56},{56,0},{1,9},... | collective-permute-start | bytes 3158024 | tf_op jit(solution)/shard_map/ppermute | solution.py:391
  100.1 24.8 %collective-permute-start.17 = (bf16[4112,128]{1,0:T(8,128)(2,1)S(1)}, bf16[4112,128]{1,0:T(8,128)(2,1)S(1)}, u32[]{:S(2)}, u32[]{:S(2)}) collective-permute-start(bf16[4112,128]{1,0:T(8,128)(2,1)S(1)} %pack.3.refs_0_), channel_id=1, source_target_pairs={{0,56},{8,0},{16,8},{24,16},{32,24},{40,32},{48,40},{56,48},{1,57}... | collective-permute-start | bytes 3158024 | tf_op jit(solution)/shard_map/ppermute | solution.py:391
  103.9 43.6 %collective-permute-start.6 = (bf16[4112,128]{1,0:T(8,128)(2,1)}, bf16[4112,128]{1,0:T(8,128)(2,1)}, u32[]{:S(2)}, u32[]{:S(2)}) collective-permute-start(bf16[4112,128]{1,0:T(8,128)(2,1)} %collective-permute-done.3.refs_2_), channel_id=1, source_target_pairs={{0,56},{8,0},{16,8},{24,16},{32,24},{40,32},{48,40},{56,48},{1,57}... | collective-permute-start | bytes 3158024 | tf_op jit(solution)/shard_map/ppermute | solution.py:391
  131.6 35.8 %all-to-all-start.4 = ((bf16[8,768,128]{2,1,0:T(8,128)(2,1)}), bf16[8,768,128]{2,1,0:T(8,128)(2,1)}, u32[]{:S(2)}, u32[]{:S(2)}) async-start(bf16[8,768,128]{2,1,0:T(8,128)(2,1)} %bitcast.67), calls=%async_computation.4 | async-start | bytes 3145728 | tf_op jit(solution)/shard_map/all_to_all | solution.py:406
  167.4 38.2 %all-to-all-start.2 = ((bf16[8,1152,128]{2,1,0:T(8,128)(2,1)}), bf16[8,1152,128]{2,1,0:T(8,128)(2,1)}, u32[]{:S(2)}, u32[]{:S(2)}) async-start(bf16[8,1152,128]{2,1,0:T(8,128)(2,1)} %bitcast.74), calls=%async_computation.2 | async-start | bytes 4718592 | tf_op jit(solution)/shard_map/all_to_all | solution.py:406
  173.9 26.2 %collective-permute-start.18 = (bf16[4112,128]{1,0:T(8,128)(2,1)}, bf16[4112,128]{1,0:T(8,128)(2,1)S(1)}, u32[]{:S(2)}, u32[]{:S(2)}) collective-permute-start(bf16[4112,128]{1,0:T(8,128)(2,1)} %copy-done.8), channel_id=1, source_target_pairs={{0,8},{8,16},{16,24},{24,32},{32,40},{40,48},{48,56},{56,0},{1,9},... | collective-permute-start | bytes 3158024 | tf_op jit(solution)/shard_map/ppermute | solution.py:391
  175.3 24.7 %collective-permute-start.19 = (bf16[4112,128]{1,0:T(8,128)(2,1)}, bf16[4112,128]{1,0:T(8,128)(2,1)S(1)}, u32[]{:S(2)}, u32[]{:S(2)}) collective-permute-start(bf16[4112,128]{1,0:T(8,128)(2,1)} %copy-done.28), channel_id=1, source_target_pairs={{0,56},{8,0},{16,8},{24,16},{32,24},{40,32},{48,40},{56,48},{1,57}... | collective-permute-start | bytes 3158024 | tf_op jit(solution)/shard_map/ppermute | solution.py:391
  205.6 48.6 %all-to-all-start.5 = ((bf16[8,1152,128]{2,1,0:T(8,128)(2,1)}), bf16[8,1152,128]{2,1,0:T(8,128)(2,1)}, u32[]{:S(2)}, u32[]{:S(2)}) async-start(bf16[8,1152,128]{2,1,0:T(8,128)(2,1)} %bitcast.13), calls=%async_computation.5 | async-start | bytes 4718592 | tf_op jit(solution)/shard_map/all_to_all | solution.py:406
  211.2 26.3 %collective-permute-start.20 = (bf16[4112,128]{1,0:T(8,128)(2,1)}, bf16[4112,128]{1,0:T(8,128)(2,1)S(1)}, u32[]{:S(2)}, u32[]{:S(2)}) collective-permute-start(bf16[4112,128]{1,0:T(8,128)(2,1)} %copy-done.27), channel_id=1, source_target_pairs={{0,8},{8,16},{16,24},{24,32},{32,40},{40,48},{48,56},{56,0},{1,9},... | collective-permute-start | bytes 3158024 | tf_op jit(solution)/shard_map/ppermute | solution.py:391
  212.4 26.2 %collective-permute-start.21 = (bf16[4112,128]{1,0:T(8,128)(2,1)}, bf16[4112,128]{1,0:T(8,128)(2,1)S(1)}, u32[]{:S(2)}, u32[]{:S(2)}) collective-permute-start(bf16[4112,128]{1,0:T(8,128)(2,1)} %copy-done.26), channel_id=1, source_target_pairs={{0,56},{8,0},{16,8},{24,16},{32,24},{40,32},{48,40},{56,48},{1,57}... | collective-permute-start | bytes 3158024 | tf_op jit(solution)/shard_map/ppermute | solution.py:391
  254.2 18.4 %all-to-all-start.7 = ((bf16[8,384,128]{2,1,0:T(8,128)(2,1)}), bf16[8,384,128]{2,1,0:T(8,128)(2,1)}, u32[]{:S(2)}, u32[]{:S(2)}) async-start(bf16[8,384,128]{2,1,0:T(8,128)(2,1)} %bitcast.17), calls=%async_computation.7 | async-start | bytes 1572864 | tf_op jit(solution)/shard_map/all_to_all | solution.py:406
  272.6 64.5 %all-to-all-start.6 = ((bf16[8,768,128]{2,1,0:T(8,128)(2,1)}), bf16[8,768,128]{2,1,0:T(8,128)(2,1)}, u32[]{:S(2)}, u32[]{:S(2)}) async-start(bf16[8,768,128]{2,1,0:T(8,128)(2,1)} %bitcast.15), calls=%async_computation.6 | async-start | bytes 3145728 | tf_op jit(solution)/shard_map/all_to_all | solution.py:406
  283.4 30.0 %collective-permute-start.9 = (bf16[3072,128]{1,0:T(8,128)(2,1)S(1)}, bf16[3072,128]{1,0:T(8,128)(2,1)S(1)}, u32[]{:S(2)}, u32[]{:S(2)}) collective-permute-start(bf16[3072,128]{1,0:T(8,128)(2,1)S(1)} %aggregate.2.s0), channel_id=1, source_target_pairs={{0,1},{1,2},{2,3},{3,0},{4,5},{5,6},{6,7},{7,4},{8,9},{9,10},{10,1... | collective-permute-start | bytes 2359304 | tf_op jit(solution)/shard_map/ppermute | solution.py:395
  284.7 28.9 %collective-permute-start.10 = (bf16[3072,128]{1,0:T(8,128)(2,1)S(1)}, bf16[3072,128]{1,0:T(8,128)(2,1)S(1)}, u32[]{:S(2)}, u32[]{:S(2)}) collective-permute-start(bf16[3072,128]{1,0:T(8,128)(2,1)S(1)} %aggregate.2.s0), channel_id=1, source_target_pairs={{0,3},{1,0},{2,1},{3,2},{4,7},{5,4},{6,5},{7,6},{8,11},{9,8},{10,9... | collective-permute-start | bytes 2359304 | tf_op jit(solution)/shard_map/ppermute | solution.py:395
  286.9 22.5 %collective-permute-start.14 = (bf16[256,512]{1,0:T(8,128)(2,1)}, bf16[256,512]{1,0:T(8,128)(2,1)S(1)}, u32[]{:S(2)}, u32[]{:S(2)}) collective-permute-start(bf16[256,512]{1,0:T(8,128)(2,1)} %constant_dynamic-update-slice_fusion), channel_id=1, source_target_pairs={{0,3},{1,0},{2,1},{3,2},{4,7},{5,4},{6,5},{7,6},{8,11},{9,8},{10,9... | collective-permute-start | bytes 786440 | tf_op jit(solution)/shard_map/ppermute | solution.py:395
  288.1 24.6 %collective-permute-start.13 = (bf16[256,512]{1,0:T(8,128)(2,1)}, bf16[256,512]{1,0:T(8,128)(2,1)S(1)}, u32[]{:S(2)}, u32[]{:S(2)}) collective-permute-start(bf16[256,512]{1,0:T(8,128)(2,1)} %constant_dynamic-update-slice_fusion), channel_id=1, source_target_pairs={{0,1},{1,2},{2,3},{3,0},{4,5},{5,6},{6,7},{7,4},{8,9},{9,10},{10,1... | collective-permute-start | bytes 786440 | tf_op jit(solution)/shard_map/ppermute | solution.py:395
  (55 other events, 587.2 us)

commit v2 on v1

--- a/solution.py
+++ b/solution.py
@@ -75,87 +75,77 @@
 def stage_kernel(sizes, z_ref, *refs):
     count = len(sizes)
     total = sum(sizes)
-    flat, (after_ref, out_ref, zeros, ints, asked, sem, head_sem) = refs[:total], refs[total:]
-    del after_ref
+    flat, (out_ref, ints, asked, sem) = refs[:total], refs[-4:]
     sources = [flat[sum(sizes[:s]) : sum(sizes[: s + 1])] for s in range(count)]
+    copies = [pltpu.make_async_copy(ints.at[s], asked.at[s], sem.at[s]) for s in range(count)]
     for s in range(count):
         ints[s] = sources[s][0][0:HEAD, :].astype(F32).astype(jnp.int32)
-        pltpu.make_async_copy(ints.at[s], asked.at[s], head_sem.at[s]).start()
-    zeros[...] = jnp.zeros_like(zeros)
-    for s in range(count):
-        pltpu.make_async_copy(ints.at[s], asked.at[s], head_sem.at[s]).wait()
+        copies[s].start()
+    for copy in copies:
+        copy.wait()
     mine = z_ref[0]
+    zeros = jnp.zeros((BS, BS), BF16)
 
     def one(reader, carry):
         column = (reader // C) * (Z * C) + mine * C + lax.rem(reader, C)
         for s, source in enumerate(sources):
-            limit = HB if len(source) == 1 else HALF
             for slot in range(CAP):
                 block = asked[s, slot, column]
-                target = out_ref.at[(reader * count + s) * CAP + slot]
-                start = pl.multiple_of(HEAD + jnp.where(block < limit, block, 0) * BS, HEAD)
-
-                @pl.when(block < limit)
-                def _(source=source, start=start, target=target):
-                    pltpu.make_async_copy(source[0].at[pl.ds(start, BS)], target, sem).start()
-
-                if len(source) == 2:
-                    late = jnp.logical_and(block >= HALF, block < HB)
-                    begin = pl.multiple_of(jnp.where(late, block - HALF, 0) * BS, BS)
-
-                    @pl.when(late)
-                    def _(source=source, begin=begin, target=target):
-                        pltpu.make_async_copy(source[1].at[pl.ds(begin, BS)], target, sem).start()
-
-                @pl.when(block >= HB)
-                def _(target=target):
-                    pltpu.make_async_copy(zeros, target, sem).start()
-
+                entry = (reader * count + s) * CAP + slot
+                if len(source) == 1:
+                    start = pl.multiple_of(HEAD + jnp.minimum(block, HB - 1) * BS, HEAD)
+                    out_ref[entry] = jnp.where(block < HB, source[0][pl.ds(start, BS), :], zeros)
+                else:
+                    first = pl.multiple_of(HEAD + jnp.minimum(block, HALF - 1) * BS, HEAD)
+                    second = pl.multiple_of(jnp.clip(block - HALF, 0, HALF - 1) * BS, BS)
+                    late = jnp.where(block < HB, source[1][pl.ds(second, BS), :], zeros)
+                    out_ref[entry] = jnp.where(block < HALF, source[0][pl.ds(first, BS), :], late)
         return carry
 
     lax.fori_loop(0, G, one, 0)
-    pltpu.make_async_copy(out_ref, out_ref, sem).wait()
-
-
-def stage(my_z, sources, after):
+
+
+def stage(my_z, sources, after=()):
     count = len(sources)
     sizes = tuple(len(source) for source in sources)
     entries = G * CAP * count
     return call(
         functools.partial(stage_kernel, sizes),
         jax.ShapeDtypeStruct((entries, BS, BS), BF16),
-        [SMEM] + [VMEM] * sum(sizes) + [ANY],
-        ANY,
+        [SMEM] + [VMEM] * sum(sizes) + [ANY] * len(after),
+        VMEM,
         [
-            pltpu.VMEM((BS, BS), BF16),
             pltpu.VMEM((count, HEAD, BS), jnp.int32),
             pltpu.SMEM((count, HEAD, BS), jnp.int32),
-            pltpu.SemaphoreType.DMA,
             pltpu.SemaphoreType.DMA((count,)),
         ],
         (0, 2 * entries * BS * BS * 2, 0),
         "stage",
-    )(my_z, *[part for source in sources for part in source], after)
-
-
-def aggregate_kernel(count, skip, local_ref, piece_ref, offset_ref, table_ref, *refs):
+    )(my_z, *[part for source in sources for part in source], *after)
+
+
+def aggregate_kernel(sides, count, skip, code_ref, other_ref, blocks_ref, table_ref, *refs):
     halos, refs = refs[:count], refs[count:]
-    tiles_ref, after_ref, out_ref, table, halo, tiles, table_sem, halo_sem, tiles_sem = refs
-    del after_ref
+    tiles_ref, out_ref, table, halo, tiles, table_sem, halo_sem, tiles_sem = refs
+
+    def local(row):
+        pair = (row, other_ref[row])
+        return [blocks_ref[block] for block in pair] if skip else pair
+
     copy = pltpu.make_async_copy(table_ref.at[pl.ds(skip, table.shape[0])], table, table_sem)
     copy.start()
 
     def start(row, carry):
         pltpu.make_async_copy(tiles_ref.at[row], tiles.at[row], tiles_sem.at[row // STEP]).start()
         for slot in range(TPR - 2):
-            use = row * (TPR - 2) + slot
-            piece = piece_ref[use]
-            offset = offset_ref[use]
-            for number, source in enumerate(halos):
-
-                @pl.when(piece == number)
-                def _(source=source, slot=slot):
-                    pltpu.make_async_copy(source.at[offset], halo.at[row, slot], halo_sem.at[row // STEP]).start()
+            code = code_ref[row * (TPR - 2) + slot]
+            distance, group, number = code // 256, lax.rem(code // 8, 32), lax.rem(code, 8)
+            for side, (piece, source, sources) in enumerate(sides):
+
+                @pl.when(distance == side)
+                def _(piece=piece, source=source, sources=sources, group=group, number=number, slot=slot):
+                    place = (group * sources + source) * CAP + number
+                    pltpu.make_async_copy(halos[piece].at[place], halo.at[row, slot], halo_sem.at[row // STEP]).start()
 
         return carry
 
@@ -170,7 +160,7 @@
             row = group * STEP + k
             left = jnp.concatenate([tiles[row, t] for t in range(TPR)], axis=1)
             right = jnp.concatenate(
-                [table[pl.ds(pl.multiple_of(local_ref[2 * row + t] * BS, BS), BS), :] for t in range(2)]
+                [table[pl.ds(pl.multiple_of(block * BS, BS), BS), :] for block in local(row)]
                 + [halo[row, t] for t in range(TPR - 2)],
                 axis=0,
             )
@@ -181,11 +171,11 @@
     lax.fori_loop(0, NB // STEP, compute, 0)
 
 
-def aggregate(skip, table, halos, tiles, local, piece, offset, after):
-    return call(
-        functools.partial(aggregate_kernel, len(halos), skip),
+def aggregate(sides, skip, table, halos, tiles, code, other, blocks):
+    return call(
+        functools.partial(aggregate_kernel, sides, len(halos), skip),
         jax.ShapeDtypeStruct((ROWS, BS), BF16),
-        [SMEM] * 3 + [ANY] * (len(halos) + 3),
+        [SMEM] * 3 + [ANY] * (len(halos) + 2),
         VMEM,
         [
             pltpu.VMEM((table.shape[0] - skip, BS), BF16),
@@ -197,7 +187,7 @@
         ],
         (2 * NB * TPR * BS**3, 2 * NB * TPR * BS * BS * 2, 0),
         "aggregate",
-    )(local, piece, offset, table, *halos, tiles, after)
+    )(code, other, blocks, table, *halos, tiles)
 
 
 def sigmoid(value):
@@ -235,7 +225,7 @@
     )(*summed, weight)
 
 
-def second_kernel(summed_ref, weight_ref, cot_ref, out_ref, delta_ref, back_ref):
+def second_kernel(x_ref, summed_ref, weight_ref, cot_ref, out_ref, delta_ref, back_ref):
     step = 128
 
     def one(row, carry):
@@ -251,24 +241,24 @@
         ).astype(BF16)
         delta_ref[rows, :] = delta
         for k in range(X):
-            out_ref[k, rows, :] = out[:, k * BS : (k + 1) * BS]
+            out_ref[lax.rem(k + X - x_ref[0], X), rows, :] = out[:, k * BS : (k + 1) * BS]
             back_ref[k, rows, :] = back[:, k * BS : (k + 1) * BS]
         return carry
 
     lax.fori_loop(0, QUARTER // step, one, 0)
 
 
-def second_layer(summed, weight, cot):
+def second_layer(my_x, summed, weight, cot):
     piece = jax.ShapeDtypeStruct((X, QUARTER, BS), BF16)
     return call(
         second_kernel,
         (piece, jax.ShapeDtypeStruct((QUARTER, X * BS), BF16), piece),
-        [VMEM] * 3,
+        [SMEM] + [VMEM] * 3,
         (VMEM,) * 3,
         [],
         (4 * QUARTER * 512 * 512, 5 * 1024 * 1024, QUARTER * 512),
         "second_layer",
-    )(summed, weight, cot)
+    )(my_x, summed, weight, cot)
 
 
 def grad_second_kernel(summed_ref, delta_ref, out_ref):
@@ -330,8 +320,8 @@
     )(my_x, tiles, *summed)
 
 
-def last_kernel(other_ref, back_ref, turned_ref, slope_ref, summed_ref, after_ref, out_ref, total, delta):
-    del after_ref
+def last_kernel(other_ref, back_ref, turned_ref, slope_ref, summed_ref, second_ref, out_ref, total, delta):
+    out_ref[:, BS:] = second_ref[...]
     total[...] = jnp.zeros_like(total)
 
     def spread(group, carry):
@@ -354,37 +344,71 @@
         return carry
 
     lax.fori_loop(0, NB, scale, 0, unroll=4)
-    out_ref[...] = jnp.dot(summed_ref[...], delta[...], preferred_element_type=F32).astype(BF16)
-
-
-def last_part(other, back, turned, slope, summed, after):
+    out_ref[:, 0:BS] = jnp.dot(summed_ref[...], delta[...], preferred_element_type=F32).astype(BF16)
+
+
+def last_part(other, back, turned, slope, summed, second):
     return call(
         last_kernel,
-        jax.ShapeDtypeStruct((X * BS, BS), BF16),
-        [SMEM, VMEM, VMEM, VMEM, VMEM, ANY],
+        jax.ShapeDtypeStruct((X * BS, (X + 1) * BS), BF16),
+        [SMEM] + [VMEM] * 5,
         VMEM,
         [pltpu.VMEM((NB, BS, BS), F32), pltpu.VMEM((ROWS, BS), BF16)],
         (2 * NB * 2 * BS**3 + 2 * ROWS * 512 * BS, 8 * 1024 * 1024, 0),
         "last_part",
-    )(other, back, turned, slope, summed, after)
-
-
-def join_kernel(first_ref, second_ref, after_ref, out_ref):
-    del after_ref
-    out_ref[:, 0:BS] = first_ref[...]
-    out_ref[:, BS:] = second_ref[...]
-
-
-def join(first, second, after):
-    return call(
-        join_kernel,
-        jax.ShapeDtypeStruct((X * BS, (X + 1) * BS), BF16),
-        [VMEM, VMEM, ANY],
-        VMEM,
-        [],
-        (0, 1024 * 1024, 0),
-        "join",
-    )(first, second, after)
+    )(other, back, turned, slope, summed, second)
+
+
+def sum_kernel(got_ref, held_ref, out_ref, passed_ref):
+    del held_ref, passed_ref
+    rows = got_ref.shape[1]
+    second = got_ref[0, :, BS:].astype(F32)
+    for k in range(1, X * G):
+        second += got_ref[k, :, BS:].astype(F32)
+    for x in range(X):
+        first = got_ref[x * G, :, :BS].astype(F32)
+        for k in range(1, G):
+            first += got_ref[x * G + k, :, :BS].astype(F32)
+        for z in range(Z):
+            out_ref[z, :rows, x * BS : (x + 1) * BS] = first.astype(BF16)
+    for z in range(Z):
+        out_ref[z, rows:, :] = second.astype(BF16)
+
+
+def sum_parts(got, held):
+    return pl.pallas_call(
+        sum_kernel,
+        out_shape=(
+            jax.ShapeDtypeStruct((Z, 2 * got.shape[1], X * BS), BF16),
+            jax.ShapeDtypeStruct(held.shape, held.dtype),
+        ),
+        in_specs=[VMEM, ANY],
+        out_specs=(VMEM, ANY),
+        input_output_aliases={1: 1},
+        compiler_params=pltpu.CompilerParams(vmem_limit_bytes=LIMIT),
+        cost_estimate=pl.CostEstimate(flops=0, bytes_accessed=1024 * 1024, transcendentals=0),
+        name="sum_parts",
+    )(got, held)
+
+
+def assemble_kernel(x_ref, *refs):
+    quarters, (out_ref, sem) = refs[:X], refs[X:]
+    for k in range(X):
+        rows = pl.ds(pl.multiple_of(lax.rem(x_ref[0] + X - k, X) * QUARTER, QUARTER), QUARTER)
+        pltpu.make_async_copy(quarters[k], out_ref.at[rows], sem).start()
+    pltpu.make_async_copy(out_ref, out_ref, sem).wait()
+
+
+def assemble(my_x, quarters):
+    return call(
+        assemble_kernel,
+        jax.ShapeDtypeStruct((ROWS, BS), BF16),
+        [SMEM] + [VMEM] * X,
+        ANY,
+        [pltpu.SemaphoreType.DMA],
+        (0, 2 * 1024 * 1024, 0),
+        "assemble",
+    )(my_x, *quarters)
 
 
 def shift(value, step):
@@ -412,13 +436,12 @@
     return got.reshape(staged.shape)
 
 
-def ring(table):
-    steps = [(table, table)]
-    for _ in range(1, Z // 2):
-        up, down = steps[-1]
-        steps.append((shift(up, 1), shift(down, -1)))
-    up, down = steps[-1]
-    return steps, (shift(up[:MIDDLE], 1), shift(down[MIDDLE:], -1))
+def apart(work, my_z, *args):
+    def skip(*args):
+        return jax.tree.map(lambda leaf: jnp.zeros(leaf.shape, leaf.dtype), shapes)
+
+    shapes = jax.eval_shape(work, *args)
+    return lax.cond(my_z < Z, work, skip, *args)
 
 
 def body(
@@ -436,79 +459,81 @@
     my_z = lax.axis_index("z").astype(jnp.int32)
     my_x = lax.axis_index("mp").astype(jnp.int32)
     blocks = send_blocks[0].T
+    other = tile_columns[:, 1]
     table_input = pack(blocks, send_counts, input_history, tile_columns)
-    steps, far = ring(table_input)
-    table_hidden = pack(blocks, send_counts, hidden_history, far[0])
-    steps_hidden, far_hidden = ring(table_hidden)
-
-    def piece_of(sources, after):
+
+    def hop(pair):
+        return shift(pair[0], 1), shift(pair[1], -1)
+
+    def far_hop(pair):
+        return shift(pair[0][:MIDDLE], 1), shift(pair[1][MIDDLE:], -1)
+
+    def send(*sources, after=()):
         return plane(stage(my_z.reshape(1), [s if isinstance(s, tuple) else (s,) for s in sources], after))
 
-    halo_input = [
-        piece_of(steps[1], tile_columns),
-        piece_of((table_input,) + steps[2], tile_columns),
-        piece_of((far,) + steps[3], steps_hidden[1][0]),
-    ]
-    halo_hidden = [
-        piece_of(steps_hidden[1], tile_columns),
-        piece_of((table_hidden,) + steps_hidden[2], tile_columns),
-        piece_of(steps_hidden[3], tile_columns),
-        piece_of((far_hidden,), tile_columns),
-    ]
-
+    def beside(*sources, after=()):
+        return apart(lambda sources, after: send(*sources, after=after), my_z, sources, after)
+
+    def step_zero(table, blocks, counts, history):
+        return hop((table, table)), beside(table), pack(blocks, counts, history, table)
+
+    def step_one(pair, other):
+        return hop(pair), hop((other, other)), beside(*pair, other)
+
+    def step_two(pair, other):
+        return hop(pair), hop(other), beside(*pair, *other)
+
+    def step_three(pair, other):
+        return far_hop(pair), hop(other), beside(*pair, other[0])
+
+    def step_four(far, other, after):
+        return far_hop(other), beside(far, after=after)
+
+    weights = lax.all_gather(jnp.concatenate([weight_first, weight_second]), "mp", axis=0, tiled=False)
+    cot = lax.all_gather(cotangent, "mp", axis=0, tiled=False)
+    cot_rows = lax.dynamic_slice(cot, (0, my_x * QUARTER, 0), (X, QUARTER, BS))
+    order = jnp.stack([my_x, (my_x - 1) % X, (my_x + 1) % X, (my_x + 2) % X])
+    columns = lax.dynamic_slice(weights, (0, 0, my_x * BS), (X, BS, BS))[order].reshape(X * BS, BS)
+    weight_all = weights[:, BS:].reshape(X * BS, X * BS)
+
+    one, piece0, table_hidden = apart(step_zero, my_z, table_input, blocks, send_counts, hidden_history)
+    two, one_hidden, piece1 = apart(step_one, my_z, one, table_hidden)
+    three, two_hidden, piece2 = apart(step_two, my_z, two, one_hidden)
+    far, three_hidden, piece3 = apart(step_three, my_z, three, two_hidden)
+    far_hidden, piece4 = apart(step_four, my_z, far, three_hidden, (columns, weight_all, cot_rows))
+    piece5 = send(far_hidden, *three_hidden, two_hidden[1])
+
+    sides_input = ((0, 0, 1), (1, 1, 3), (2, 1, 4), (3, 1, 3), (4, 0, 1), (3, 0, 3), (2, 0, 4), (1, 0, 3))
+    sides_hidden = ((0, 2, 3), (1, 3, 4), (3, 3, 4), (3, 2, 4), (3, 0, 4), (3, 1, 4), (2, 2, 3), (1, 2, 4))
     use = tile_columns[:, 2:] - NB
     owner, slot = use // CAP, use % CAP
     group = (owner // (Z * C)) * C + owner % C
-    distance = ((owner // C) % Z - my_z) % Z
-    near = jnp.minimum(distance, Z - distance)
-    from_below = (distance < Z // 2).astype(jnp.int32)
-    single = jnp.logical_or(distance == 0, distance == Z // 2)
-    third = jnp.where(single, 0, 1 + from_below)
-    piece_hidden = jnp.where(near == 0, 1, near - 1)
-    piece_input = jnp.minimum(piece_hidden, 2)
-    even = group * 2 + from_below
-    place_input = jnp.where(near == 1, even, group * 3 + third)
-    place_hidden = jnp.where(
-        jnp.logical_or(near == 1, near == 3), even, jnp.where(near == Z // 2, group, group * 3 + third)
-    )
-    where_input = (piece_input.reshape(-1), (place_input * CAP + slot).reshape(-1))
-    where_hidden = (piece_hidden.reshape(-1), (place_hidden * CAP + slot).reshape(-1))
-    other = tile_columns[:, 1]
-    mine = jnp.arange(NB, dtype=jnp.int32)
-    local_first = batch_blocks[0][jnp.stack([mine, other], axis=1)].reshape(-1)
-    local_second = jnp.stack([mine, other], axis=1).reshape(-1)
-
-    weights = gather_features(jnp.concatenate([weight_first, weight_second]))
-    weights = [weights[0], weights[1], weights[2], jnp.concatenate(weights[3:])]
-    columns = jnp.concatenate([lax.dynamic_slice(w, (0, my_x * BS), (BS, BS)) for w in weights])
-    order = jnp.stack([(-my_x) % X, (1 - my_x) % X, (2 - my_x) % X, (3 - my_x) % X])
-    order = jnp.array([0, 2, 3, 1], jnp.int32)[order]
-    weight_all = jnp.stack([w[BS:] for w in weights])[order].reshape(X * BS, X * BS)
-    cot_rows = exchange(cotangent.reshape(X, QUARTER, BS), "mp")
-
-    summed_first = aggregate(HEAD, table_input, halo_input, tile_values, local_first, *where_input, cot_rows)
+    code = (((owner // C) % Z - my_z) % Z * 256 + group * 8 + slot).reshape(-1)
+
+    batch = batch_blocks.reshape(-1)
+    halo_input = (piece0, piece1, piece2, piece3, piece4)
+    halo_hidden = (piece1, piece2, piece3, piece5)
+    summed_first = aggregate(sides_input, HEAD, table_input, halo_input, tile_values, code, other, batch)
     all_first = gather_features(summed_first)
     hidden_first, slope_first = first_layer(all_first, columns)
     turned_tiles, turned_first = prepare(my_x.reshape(1), tile_values, all_first)
-    summed_second = aggregate(
-        0, hidden_first, halo_hidden, tile_values, local_second, *where_hidden, turned_tiles
+    summed_second = aggregate(sides_hidden, 0, hidden_first, halo_hidden, tile_values, code, other, batch)
+    rows_second = exchange(summed_second.reshape(X, QUARTER, BS), "mp")
+    out_rows, delta_rows, back_rows = second_layer(
+        my_x.reshape(1), rows_second, weight_all, cot_rows
     )
-    rows_second = exchange(summed_second.reshape(X, QUARTER, BS), "mp")
-    out_rows, delta_rows, back_rows = second_layer(rows_second, weight_all, cot_rows)
     back_second = exchange(back_rows, "mp").reshape(ROWS, BS)
     part_second = grad_second_part(rows_second, delta_rows)
-    part_first = last_part(other, back_second, turned_tiles, slope_first, turned_first, part_second)
-    layer_out = exchange(out_rows, "mp").reshape(ROWS, BS)
+    got = last_part(other, back_second, turned_tiles, slope_first, turned_first, part_second)
 
     dealt = X * G
-    got = join(part_first, part_second, layer_out).reshape(dealt, -1, (X + 1) * BS)
-    got = exchange(got, ("mp", "y", "core")).astype(F32)
-    got_second = got[:, :, BS:].sum(0)
-    got_first = got[:, :, :BS].reshape(X, G, -1, BS).sum(1).transpose(1, 0, 2).reshape(-1, X * BS)
-    both = jnp.concatenate([got_first, got_second], axis=0).astype(BF16)
-    both = exchange(jnp.broadcast_to(both[None], (Z,) + both.shape), "z").astype(F32).sum(0)
+    got = exchange(got.reshape(dealt, -1, (X + 1) * BS), ("mp", "y", "core"))
+    parts, out_rows = sum_parts(got, out_rows)
+    quarters = [out_rows[0]] + [turn(out_rows[k], k) for k in range(1, X)]
+    layer_out = assemble(my_x.reshape(1), quarters)
+    both = exchange(parts, "z").astype(F32).sum(0).astype(BF16)
     both = exchange(jnp.broadcast_to(both[None], (G,) + both.shape), ("y", "core"))
-    both = both.reshape(G, 2, -1, X * BS)
+    both = both.reshape(G, 2, -1, X * BS).astype(F32)
     grad_first = both[:, 0].reshape(BS, X * BS)
     grad_second = both[:, 1].reshape(BS, X * BS)
     return (layer_out, grad_first, grad_second)

time: 441 us -> 397 us (0.900)
  waiting for transfers between devices: 193 us -> 42 us
  blocking collectives: 64.6 us -> 205 us
  starting transfers between devices: 89.3 us -> 46.6 us
  between operations: 1.36 us -> 14.5 us
  local copies, waits for them, and re-layouts: 40.6 us -> 30.2 us
  Pallas kernels: 49.6 us -> 55.6 us
    ppermute x16, waiting for transfers between devices: 151 us -> 5.94 us  [shift(): return lax.ppermute(value, 'z', [(i, (i + step) % Z) for i in range(Z)])]
    all_to_all x4 -> x8, blocking collectives: 64.6 us -> 205 us  [exchange(): return lax.all_to_all(value, axes, split_axis=0, concat_axis=0, tiled=True)]
    all_to_all x10 -> x3, starting transfers between devices: 54.6 us -> 12.1 us  [exchange(): return lax.all_to_all(value, axes, split_axis=0, concat_axis=0, tiled=True)]
    all_to_all x10 -> x3, waiting for transfers between devices: 14.1 us -> 0.76 us  [exchange(): return lax.all_to_all(value, axes, split_axis=0, concat_axis=0, tiled=True)]
    unnamed x94 -> x70, local copies, waits for them, and re-layouts: 29.9 us -> 19.1 us
    pallas_call x4 -> x5, Pallas kernels: 14.5 us -> 22.1 us  [the longest x2 16.5 us: aggregate(): call(functools.partial(aggregate_kernel, sides, len(halos), skip), jax.Sh...]
    ppermute x8 -> x7, waiting for transfers between devices: 28.4 us -> 34.6 us  [turn(): return lax.ppermute(value, 'mp', [(i, (i + step) % X) for i in range(X)])]
    pallas_call x7 -> x6, Pallas kernels: 22.6 us -> 19.1 us  [stage(): call(functools.partial(stage_kernel, sizes), jax.ShapeDtypeStruct((entrie...]
  transfers between devices with their start and end apart: 34 -> 28, of which waited for: 18 -> 7; matrix products, arithmetic and copies ran while one was open for 2% -> 2% of each run, Pallas kernels for 9% -> 9%
where the time goes in v2:
time: 397 us; the launch traced here: 396 us
  blocking collectives  205 us (52%)
  Pallas kernels  55.6 us (14%)
  starting transfers between devices  46.6 us (12%)
  waiting for transfers between devices  42 us (11%)
  local copies, waits for them, and re-layouts  30.2 us (8%)
  between operations  14.5 us (4%)
    all_to_all x8, blocking collectives, exchange(): return lax.all_to_all(value, axes, split_axis=0, concat_axis=0, tiled=True)  205 us
    ppermute x7, waiting for transfers between devices, turn(): return lax.ppermute(value, 'mp', [(i, (i + step) % X) for i in range(X)])  34.6 us
    ppermute x16, starting transfers between devices, shift(): return lax.ppermute(value, 'z', [(i, (i + step) % Z) for i in range(Z)])  25.5 us
    unnamed x70, local copies, waits for them, and re-layouts  19.1 us
    pallas_call x6, Pallas kernels, stage(): call(functools.partial(stage_kernel, sizes), jax.ShapeDtypeStruct((entrie...  19.1 us
    pallas_call x2, Pallas kernels, aggregate(): call(functools.partial(aggregate_kernel, sides, len(halos), skip), jax.Sh...  16.5 us
    all_to_all x3, starting transfers between devices, exchange(): return lax.all_to_all(value, axes, split_axis=0, concat_axis=0, tiled=True)  12.1 us
    ppermute x7, starting transfers between devices, turn(): return lax.ppermute(value, 'mp', [(i, (i + step) % X) for i in range(X)])  8.9 us
  transfers between devices with their start and end apart: 28, of which 7 were waited for; matrix products, arithmetic and copies ran while one was open for 2% of the time, Pallas kernels for 9%

profile of v2, /device:TPU:1, one launch (start us, length us, event | category | flops | bytes accessed | tf_op | source)
XLA Modules:
  0.0 395.6 jit_solution(10874082455385734406)
XLA Ops:
  14.1 29.5 %conditional.10 = (bf16[4112,128]{1,0:T(8,128)(2,1)}, bf16[4112,128]{1,0:T(8,128)(2,1)}, bf16[24,128,128]{2,1,0:T(8,128)(2,1)}, bf16[4112,128]{1,0:T(8,128)(2,1)}) conditional(s32[]{:T(128)} %convert_element_type.30, () %tuple.78, (bf16[4112,128]{1,0:T(8,128)(2,1)S(1)}, s32[]{:T(128)}, s32[3,64]{1,0:T(4,128)S(1)}, s32[1,64]{1,0:T(1,128)S(1)}, ...), branch_computations={%region_0.1_spmd, %region_1.4_spmd} | conditional | flops 2 | bytes 14712982 | solution.py:444
  20.5 18.6 %conditional = (bf16[24,128,128]{2,1,0:T(8,128)(2,1)}) conditional(s32[]{:T(128)} %convert_element_type.9, () %tuple.47, (s32[]{:T(128)}, bf16[4112,128]{1,0:T(8,128)(2,1)S(1)}) %tuple.48), branch_computations={%region_2.2_spmd, %region_3.3_spmd} | conditional | bytes 3145736 | solution.py:444
  21.5 17.5 %all_to_all.50 = bf16[8,384,128]{2,1,0:T(8,128)(2,1)} all-to-all(bf16[8,384,128]{2,1,0:T(8,128)(2,1)S(1)} %bitcast.59), channel_id=1, replica_groups=mesh['y'=4,'z'=8,'core'=2,'mp'=4] {'y','core'}, dimensions={0} | all-to-all | bytes 1572864 | tf_op jit(solution)/shard_map/cond/branch_1_fun/cond/branch_1_fun/all_to_all | solution.py:430
  43.6 47.6 %conditional.11 = (bf16[4112,128]{1,0:T(8,128)(2,1)}, bf16[4112,128]{1,0:T(8,128)(2,1)}, bf16[4112,128]{1,0:T(8,128)(2,1)}, bf16[4112,128]{1,0:T(8,128)(2,1)}, bf16[72,128,128]{2,1,0:T(8,128)(2,1)}) conditional(s32[]{:T(128)} %convert_element_type.30, () %tuple.80, (bf16[4112,128]{1,0:T(8,128)(2,1)}, bf16[4112,128]{1,0:T(8,128)(2,1)}, ...), branch_computations={%region_4.5_spmd, %region_5.8_spmd} | conditional | flops 2 | bytes 26280188 | solution.py:444
  48.9 39.6 %conditional.1 = (bf16[72,128,128]{2,1,0:T(8,128)(2,1)}) conditional(s32[]{:T(128)} %convert_element_type.12, () %tuple.51, (s32[]{:T(128)}, bf16[4112,128]{1,0:T(8,128)(2,1)}, bf16[4112,128]{1,0:T(8,128)(2,1)}, bf16[4112,128]{1,0:T(8,128)(2,1)}) %tuple.52), branch_computations={%region_6.6_spmd, %region_7.7_spmd} | conditional | bytes 9437192 | solution.py:444
  52.5 36.0 %all_to_all.51 = bf16[8,1152,128]{2,1,0:T(8,128)(2,1)} all-to-all(bf16[8,1152,128]{2,1,0:T(8,128)(2,1)S(1)} %bitcast.55), channel_id=1, replica_groups=mesh['y'=4,'z'=8,'core'=2,'mp'=4] {'y','core'}, dimensions={0} | all-to-all | bytes 4718592 | tf_op jit(solution)/shard_map/cond/branch_1_fun/cond/branch_1_fun/all_to_all | solution.py:430
  91.2 55.2 %conditional.12 = (bf16[4112,128]{1,0:T(8,128)(2,1)}, bf16[4112,128]{1,0:T(8,128)(2,1)}, bf16[4112,128]{1,0:T(8,128)(2,1)}, bf16[4112,128]{1,0:T(8,128)(2,1)}, bf16[96,128,128]{2,1,0:T(8,128)(2,1)}) conditional(s32[]{:T(128)} %convert_element_type.30, () %tuple.82, (bf16[4112,128]{1,0:T(8,128)(2,1)}, bf16[4112,128]{1,0:T(8,128)(2,1)}, ...), branch_computations={%region_8.9_spmd, %region_9.12_spmd} | conditional | flops 2 | bytes 29425924 | solution.py:444
  96.5 49.8 %conditional.2 = (bf16[96,128,128]{2,1,0:T(8,128)(2,1)}) conditional(s32[]{:T(128)} %convert_element_type.16, () %tuple.55, (s32[]{:T(128)}, bf16[4112,128]{1,0:T(8,128)(2,1)}, bf16[4112,128]{1,0:T(8,128)(2,1)}, bf16[4112,128]{1,0:T(8,128)(2,1)}, bf16[4112,128]{1,0:T(8,128)(2,1)}) %tuple.56), branch_computations={%region_10.10_spmd, %region_11.11_spmd} | conditional | bytes 12582920 | solution.py:444
  100.8 45.5 %all_to_all.52 = bf16[8,1536,128]{2,1,0:T(8,128)(2,1)} all-to-all(bf16[8,1536,128]{2,1,0:T(8,128)(2,1)S(1)} %bitcast.54), channel_id=1, replica_groups=mesh['y'=4,'z'=8,'core'=2,'mp'=4] {'y','core'}, dimensions={0} | all-to-all | bytes 6291456 | tf_op jit(solution)/shard_map/cond/branch_1_fun/cond/branch_1_fun/all_to_all | solution.py:430
  146.4 46.2 %conditional.13 = (bf16[2064,128]{1,0:T(8,128)(2,1)}, bf16[2048,128]{1,0:T(8,128)(2,1)}, bf16[4112,128]{1,0:T(8,128)(2,1)}, bf16[4112,128]{1,0:T(8,128)(2,1)}, bf16[72,128,128]{2,1,0:T(8,128)(2,1)}) conditional(s32[]{:T(128)} %convert_element_type.30, () %tuple.84, (bf16[4112,128]{1,0:T(8,128)(2,1)}, bf16[4112,128]{1,0:T(8,128)(2,1)}, ...), branch_computations={%region_12.13_spmd, %region_13.16_spmd} | conditional | flops 2 | bytes 24174846 | solution.py:444
  154.1 38.5 %conditional.3 = (bf16[72,128,128]{2,1,0:T(8,128)(2,1)}) conditional(s32[]{:T(128)} %convert_element_type.17, () %tuple.59, (s32[]{:T(128)}, bf16[4112,128]{1,0:T(8,128)(2,1)}, bf16[4112,128]{1,0:T(8,128)(2,1)}, bf16[4112,128]{1,0:T(8,128)(2,1)}) %tuple.60), branch_computations={%region_14.14_spmd, %region_15.15_spmd} | conditional | bytes 9437192 | solution.py:444
  157.7 34.9 %all_to_all.53 = bf16[8,1152,128]{2,1,0:T(8,128)(2,1)} all-to-all(bf16[8,1152,128]{2,1,0:T(8,128)(2,1)S(1)} %bitcast.56), channel_id=1, replica_groups=mesh['y'=4,'z'=8,'core'=2,'mp'=4] {'y','core'}, dimensions={0} | all-to-all | bytes 4718592 | tf_op jit(solution)/shard_map/cond/branch_1_fun/cond/branch_1_fun/all_to_all | solution.py:430
  197.7 24.2 %conditional.14 = (bf16[2064,128]{1,0:T(8,128)(2,1)}, bf16[2048,128]{1,0:T(8,128)(2,1)}, bf16[24,128,128]{2,1,0:T(8,128)(2,1)}) conditional(s32[]{:T(128)} %convert_element_type.30, () %tuple.86, (bf16[4112,128]{1,0:T(8,128)(2,1)}, bf16[4112,128]{1,0:T(8,128)(2,1)}, s32[]{:T(128)}, bf16[2064,128]{1,0:T(8,128)(2,1)}, bf16[2048,128]{1,0:T(8,128)(2,1)}, ...), branch_computations={%region_16.17_spmd, %region_17.20_spmd} | conditional | flops 2 | bytes 9461934 | solution.py:444
  202.7 19.2 %conditional.4 = (bf16[24,128,128]{2,1,0:T(8,128)(2,1)}) conditional(s32[]{:T(128)} %convert_element_type.26, () %tuple.63, (s32[]{:T(128)}, bf16[2064,128]{1,0:T(8,128)(2,1)}, bf16[2048,128]{1,0:T(8,128)(2,1)}, bf16[512,128]{1,0:T(8,128)(2,1)S(1)}, bf16[512,512]{1,0:T(8,128)(2,1)S(1)}, /*index=5*/bf16[4,768,128]{2,1,0:T(8,128)(2,1)}) %tuple.64), branch_computations={%region_18.18_spmd, %region_19.19_spmd} | conditional | bytes 3145736 | solution.py:444
  205.0 16.9 %all_to_all.54 = bf16[8,384,128]{2,1,0:T(8,128)(2,1)} all-to-all(bf16[8,384,128]{2,1,0:T(8,128)(2,1)S(1)} %bitcast.60), channel_id=1, replica_groups=mesh['y'=4,'z'=8,'core'=2,'mp'=4] {'y','core'}, dimensions={0} | all-to-all | bytes 1572864 | tf_op jit(solution)/shard_map/cond/branch_1_fun/cond/branch_1_fun/all_to_all | solution.py:430
  235.0 9.4 %aggregate.2.s0 = bf16[3072,128]{1,0:T(8,128)(2,1)S(1)} custom-call(s32[72]{0:T(128)S(1)} %reshape.252.code_ref, s32[24]{0:T(128)S(1)} %slice_bitcast_fusion.4.other_ref, s32[24]{0:T(128)S(1)} %bitcast.62, bf16[4112,128]{1,0:T(8,128)(2,1)} %copy-done.25, bf16[24,128,128]{2,1,0:T(8,128)(2,1)} %get-tuple-element.193.refs_0_, ...), custom_call_target="tpu_custom_call" | custom-call | flops 503316480 | bytes 7864320 | tf_op jit(solution)/shard_map/aggregate/pallas_call | solution.py:175
  247.2 17.5 %collective-permute-done.16.s1 = bf16[3072,128]{1,0:T(8,128)(2,1)S(1)} collective-permute-done((bf16[3072,128]{1,0:T(8,128)(2,1)S(1)}, bf16[3072,128]{1,0:T(8,128)(2,1)S(1)}, u32[]{:S(2)}, u32[]{:S(2)}) %collective-permute-start.16) | collective-permute-done | bytes 786464 | tf_op jit(solution)/shard_map/ppermute | solution.py:419
  267.6 8.1 %collective-permute-done.18.far0 = bf16[1536,128]{1,0:T(8,128)(2,1)S(1)} collective-permute-done((bf16[1536,128]{1,0:T(8,128)(2,1)S(1)}, bf16[1536,128]{1,0:T(8,128)(2,1)S(1)}, u32[]{:S(2)}, u32[]{:S(2)}) %collective-permute-start.18) | collective-permute-done | bytes 393248 | tf_op jit(solution)/shard_map/ppermute | solution.py:419
  283.5 7.1 %aggregate.3 = bf16[3072,128]{1,0:T(8,128)(2,1)S(1)} custom-call(s32[72]{0:T(128)S(1)} %reshape.252.code_ref, s32[24]{0:T(128)S(1)} %slice_bitcast_fusion.4.other_ref, s32[24]{0:T(128)S(1)} %bitcast.63, bf16[3072,128]{1,0:T(8,128)(2,1)S(1)} %copy-done.20, bf16[72,128,128]{2,1,0:T(8,128)(2,1)} %get-tuple-element.197.refs_1_.refs_0_, ...), custom_call_target="tpu_custom_call" | custom-call | flops 503316480 | bytes 7864320 | tf_op jit(solution)/shard_map/aggregate/pallas_call | solution.py:175
  290.6 13.6 %all_to_all.55.summed_ref = bf16[4,768,128]{2,1,0:T(8,128)(2,1)S(1)} all-to-all(bf16[4,768,128]{2,1,0:T(8,128)(2,1)S(1)} %bitcast.57), channel_id=1, replica_groups=mesh['y'=4,'z'=8,'core'=2,'mp'=4] {'mp'}, dimensions={0} | all-to-all | bytes 1572864 | tf_op jit(solution)/shard_map/all_to_all | solution.py:430
  316.0 5.1 %prepare.1 = (bf16[24,256,128]{2,1,0:T(8,128)(2,1)S(1)}, bf16[512,3072]{1,0:T(8,128)(2,1)}) custom-call(s32[1]{0:T(128)} %bitcast.15.x_ref, bf16[24,5,128,128]{3,2,1,0:T(8,128)(2,1)} %tiles_ref.1, bf16[3072,128]{1,0:T(8,128)(2,1)S(1)} %copy-done.3, bf16[3072,128]{1,0:T(8,128)(2,1)S(1)} %copy-done.5, bf16[3072,128]{1,0:T(8,128)(2,1)S(1)} %copy-done.7, ...), custom_call_target="tpu_custom_call" | custom-call | bytes 10485760 | tf_op jit(solution)/shard_map/prepare/pallas_call | solution.py:312
  329.8 23.4 %all_to_all.56.got_ref = bf16[32,16,640]{2,1,0:T(8,128)(2,1)S(1)} all-to-all(bf16[32,16,640]{2,1,0:T(8,128)(2,1)S(1)} %bitcast.61), channel_id=1, replica_groups=mesh['y'=4,'z'=8,'core'=2,'mp'=4] {'mp','y','core'}, dimensions={0} | all-to-all | bytes 1310720 | tf_op jit(solution)/shard_map/all_to_all | solution.py:430
  353.2 16.9 %all_to_all.57 = bf16[8,32,512]{2,1,0:T(8,128)(2,1)S(1)} all-to-all(bf16[8,32,512]{2,1,0:T(8,128)(2,1)S(1)} %get-tuple-element.223), channel_id=1, replica_groups=mesh['y'=4,'z'=8,'core'=2,'mp'=4] {'z'}, dimensions={0} | all-to-all | bytes 524288 | tf_op jit(solution)/shard_map/all_to_all | solution.py:430
  378.0 8.7 %collective-permute-done.20.refs_1_ = bf16[768,128]{1,0:T(8,128)(2,1)S(1)} collective-permute-done((bf16[768,128]{1,0:T(8,128)(2,1)S(1)}, bf16[768,128]{1,0:T(8,128)(2,1)S(1)}, u32[]{:S(2)}, u32[]{:S(2)}) %collective-permute-start.20) | collective-permute-done | bytes 196640 | tf_op jit(solution)/shard_map/ppermute | solution.py:419
  (160 shorter events, 120.4 us)
Async XLA Ops:
  7.2 185.5 %all-gather.5.cloned.1.call-start = ((), (), s32[]{:S(2)}) async-start(), calls=%async_computation.11 | async-start | bytes 1310720 | tf_op jit(solution)/shard_map/all_gather | solution.py:492
  9.0 186.6 %all-gather.7.cloned.1.call-start = ((), (), s32[]{:S(2)}) async-start(), calls=%async_computation.12 | async-start | bytes 3932160 | tf_op jit(solution)/shard_map/all_gather | solution.py:493
  14.1 29.5 %collective-permute-start = (bf16[4112,128]{1,0:T(8,128)(2,1)S(1)}, bf16[4112,128]{1,0:T(8,128)(2,1)}, u32[]{:S(2)}, u32[]{:S(2)}) collective-permute-start(bf16[4112,128]{1,0:T(8,128)(2,1)S(1)} %get-tuple-element.98.after_ref), channel_id=1, source_target_pairs={{0,8},{8,16},{16,24},{24,32},{32,40},{40,48},{48,56},{56,0},{1,9},... | collective-permute-start | bytes 3158024 | tf_op jit(solution)/shard_map/cond/branch_1_fun/ppermute | solution.py:415
  16.6 27.0 %collective-permute-start.1 = (bf16[4112,128]{1,0:T(8,128)(2,1)S(1)}, bf16[4112,128]{1,0:T(8,128)(2,1)}, u32[]{:S(2)}, u32[]{:S(2)}) collective-permute-start(bf16[4112,128]{1,0:T(8,128)(2,1)S(1)} %get-tuple-element.98.after_ref), channel_id=1, source_target_pairs={{0,56},{8,0},{16,8},{24,16},{32,24},{40,32},{48,40},{56,48},{1,57}... | collective-permute-start | bytes 3158024 | tf_op jit(solution)/shard_map/cond/branch_1_fun/ppermute | solution.py:415
  43.6 45.0 %collective-permute-start.4 = (bf16[4112,128]{1,0:T(8,128)(2,1)}, bf16[4112,128]{1,0:T(8,128)(2,1)}, u32[]{:S(2)}, u32[]{:S(2)}) collective-permute-start(bf16[4112,128]{1,0:T(8,128)(2,1)} %get-tuple-element.124), channel_id=1, source_target_pairs={{0,8},{8,16},{16,24},{24,32},{32,40},{40,48},{48,56},{56,0},{1,9},... | collective-permute-start | bytes 3158024 | tf_op jit(solution)/shard_map/cond/branch_1_fun/ppermute | solution.py:415
  43.6 45.0 %collective-permute-start.5 = (bf16[4112,128]{1,0:T(8,128)(2,1)}, bf16[4112,128]{1,0:T(8,128)(2,1)}, u32[]{:S(2)}, u32[]{:S(2)}) collective-permute-start(bf16[4112,128]{1,0:T(8,128)(2,1)} %get-tuple-element.124), channel_id=1, source_target_pairs={{0,56},{8,0},{16,8},{24,16},{32,24},{40,32},{48,40},{56,48},{1,57}... | collective-permute-start | bytes 3158024 | tf_op jit(solution)/shard_map/cond/branch_1_fun/ppermute | solution.py:415
  46.3 44.9 %collective-permute-start.2 = (bf16[4112,128]{1,0:T(8,128)(2,1)}, bf16[4112,128]{1,0:T(8,128)(2,1)}, u32[]{:S(2)}, u32[]{:S(2)}) collective-permute-start(bf16[4112,128]{1,0:T(8,128)(2,1)} %get-tuple-element.122), channel_id=1, source_target_pairs={{0,8},{8,16},{16,24},{24,32},{32,40},{40,48},{48,56},{56,0},{1,9},... | collective-permute-start | bytes 3158024 | tf_op jit(solution)/shard_map/cond/branch_1_fun/ppermute | solution.py:415
  46.3 44.9 %collective-permute-start.3 = (bf16[4112,128]{1,0:T(8,128)(2,1)}, bf16[4112,128]{1,0:T(8,128)(2,1)}, u32[]{:S(2)}, u32[]{:S(2)}) collective-permute-start(bf16[4112,128]{1,0:T(8,128)(2,1)} %get-tuple-element.123), channel_id=1, source_target_pairs={{0,56},{8,0},{16,8},{24,16},{32,24},{40,32},{48,40},{56,48},{1,57}... | collective-permute-start | bytes 3158024 | tf_op jit(solution)/shard_map/cond/branch_1_fun/ppermute | solution.py:415
  91.2 55.2 %collective-permute-start.6 = (bf16[4112,128]{1,0:T(8,128)(2,1)}, bf16[4112,128]{1,0:T(8,128)(2,1)}, u32[]{:S(2)}, u32[]{:S(2)}) collective-permute-start(bf16[4112,128]{1,0:T(8,128)(2,1)} %get-tuple-element.131), channel_id=1, source_target_pairs={{0,8},{8,16},{16,24},{24,32},{32,40},{40,48},{48,56},{56,0},{1,9},... | collective-permute-start | bytes 3158024 | tf_op jit(solution)/shard_map/cond/branch_1_fun/ppermute | solution.py:415
  92.1 54.2 %collective-permute-start.7 = (bf16[4112,128]{1,0:T(8,128)(2,1)}, bf16[4112,128]{1,0:T(8,128)(2,1)}, u32[]{:S(2)}, u32[]{:S(2)}) collective-permute-start(bf16[4112,128]{1,0:T(8,128)(2,1)} %get-tuple-element.132), channel_id=1, source_target_pairs={{0,56},{8,0},{16,8},{24,16},{32,24},{40,32},{48,40},{56,48},{1,57}... | collective-permute-start | bytes 3158024 | tf_op jit(solution)/shard_map/cond/branch_1_fun/ppermute | solution.py:415
  93.9 52.5 %collective-permute-start.8 = (bf16[4112,128]{1,0:T(8,128)(2,1)}, bf16[4112,128]{1,0:T(8,128)(2,1)}, u32[]{:S(2)}, u32[]{:S(2)}) collective-permute-start(bf16[4112,128]{1,0:T(8,128)(2,1)} %get-tuple-element.133), channel_id=1, source_target_pairs={{0,8},{8,16},{16,24},{24,32},{32,40},{40,48},{48,56},{56,0},{1,9},... | collective-permute-start | bytes 3158024 | tf_op jit(solution)/shard_map/cond/branch_1_fun/ppermute | solution.py:415
  93.9 52.5 %collective-permute-start.9 = (bf16[4112,128]{1,0:T(8,128)(2,1)}, bf16[4112,128]{1,0:T(8,128)(2,1)}, u32[]{:S(2)}, u32[]{:S(2)}) collective-permute-start(bf16[4112,128]{1,0:T(8,128)(2,1)} %get-tuple-element.134), channel_id=1, source_target_pairs={{0,56},{8,0},{16,8},{24,16},{32,24},{40,32},{48,40},{56,48},{1,57}... | collective-permute-start | bytes 3158024 | tf_op jit(solution)/shard_map/cond/branch_1_fun/ppermute | solution.py:415
  146.4 46.2 %collective-permute-start.12 = (bf16[4112,128]{1,0:T(8,128)(2,1)}, bf16[4112,128]{1,0:T(8,128)(2,1)}, u32[]{:S(2)}, u32[]{:S(2)}) collective-permute-start(bf16[4112,128]{1,0:T(8,128)(2,1)} %get-tuple-element.142), channel_id=1, source_target_pairs={{0,8},{8,16},{16,24},{24,32},{32,40},{40,48},{48,56},{56,0},{1,9},... | collective-permute-start | bytes 3158024 | tf_op jit(solution)/shard_map/cond/branch_1_fun/ppermute | solution.py:415
  146.5 46.1 %collective-permute-start.13 = (bf16[4112,128]{1,0:T(8,128)(2,1)}, bf16[4112,128]{1,0:T(8,128)(2,1)}, u32[]{:S(2)}, u32[]{:S(2)}) collective-permute-start(bf16[4112,128]{1,0:T(8,128)(2,1)} %get-tuple-element.143), channel_id=1, source_target_pairs={{0,56},{8,0},{16,8},{24,16},{32,24},{40,32},{48,40},{56,48},{1,57}... | collective-permute-start | bytes 3158024 | tf_op jit(solution)/shard_map/cond/branch_1_fun/ppermute | solution.py:415
  150.2 42.4 %collective-permute-start.10 = (bf16[2064,128]{1,0:T(8,128)(2,1)S(1)}, bf16[2064,128]{1,0:T(8,128)(2,1)}, u32[]{:S(2)}, u32[]{:S(2)}) collective-permute-start(bf16[2064,128]{1,0:T(8,128)(2,1)S(1)} %slice.30), channel_id=1, source_target_pairs={{0,8},{8,16},{16,24},{24,32},{32,40},{40,48},{48,56},{56,0},{1,9},... | collective-permute-start | bytes 1585160 | tf_op jit(solution)/shard_map/cond/branch_1_fun/ppermute | solution.py:415
  151.4 41.2 %collective-permute-start.11 = (bf16[2048,128]{1,0:T(8,128)(2,1)S(1)}, bf16[2048,128]{1,0:T(8,128)(2,1)}, u32[]{:S(2)}, u32[]{:S(2)}) collective-permute-start(bf16[2048,128]{1,0:T(8,128)(2,1)S(1)} %slice.31), channel_id=1, source_target_pairs={{0,56},{8,0},{16,8},{24,16},{32,24},{40,32},{48,40},{56,48},{1,57}... | collective-permute-start | bytes 1572872 | tf_op jit(solution)/shard_map/cond/branch_1_fun/ppermute | solution.py:415
  198.8 23.1 %collective-permute-start.14 = (bf16[2064,128]{1,0:T(8,128)(2,1)S(1)}, bf16[2064,128]{1,0:T(8,128)(2,1)}, u32[]{:S(2)}, u32[]{:S(2)}) collective-permute-start(bf16[2064,128]{1,0:T(8,128)(2,1)S(1)} %slice.32), channel_id=1, source_target_pairs={{0,8},{8,16},{16,24},{24,32},{32,40},{40,48},{48,56},{56,0},{1,9},... | collective-permute-start | bytes 1585160 | tf_op jit(solution)/shard_map/cond/branch_1_fun/ppermute | solution.py:415
  199.9 22.0 %collective-permute-start.15 = (bf16[2048,128]{1,0:T(8,128)(2,1)S(1)}, bf16[2048,128]{1,0:T(8,128)(2,1)}, u32[]{:S(2)}, u32[]{:S(2)}) collective-permute-start(bf16[2048,128]{1,0:T(8,128)(2,1)S(1)} %slice.33), channel_id=1, source_target_pairs={{0,56},{8,0},{16,8},{24,16},{32,24},{40,32},{48,40},{56,48},{1,57}... | collective-permute-start | bytes 1572872 | tf_op jit(solution)/shard_map/cond/branch_1_fun/ppermute | solution.py:415
  227.9 54.5 %all-to-all-start.5 = ((bf16[8,1536,128]{2,1,0:T(8,128)(2,1)}), bf16[8,1536,128]{2,1,0:T(8,128)(2,1)S(1)}, u32[]{:S(2)}, u32[]{:S(2)}) async-start(bf16[8,1536,128]{2,1,0:T(8,128)(2,1)} %bitcast.53), calls=%async_computation.5 | async-start | bytes 6291456 | tf_op jit(solution)/shard_map/all_to_all | solution.py:430
  244.4 20.3 %collective-permute-start.16 = (bf16[3072,128]{1,0:T(8,128)(2,1)S(1)}, bf16[3072,128]{1,0:T(8,128)(2,1)S(1)}, u32[]{:S(2)}, u32[]{:S(2)}) collective-permute-start(bf16[3072,128]{1,0:T(8,128)(2,1)S(1)} %aggregate.2.s0), channel_id=1, source_target_pairs={{0,1},{1,2},{2,3},{3,0},{4,5},{5,6},{6,7},{7,4},{8,9},{9,10},{10,1... | collective-permute-start | bytes 2359304 | tf_op jit(solution)/shard_map/ppermute | solution.py:419
  245.8 19.2 %collective-permute-start.17 = (bf16[3072,128]{1,0:T(8,128)(2,1)S(1)}, bf16[3072,128]{1,0:T(8,128)(2,1)S(1)}, u32[]{:S(2)}, u32[]{:S(2)}) collective-permute-start(bf16[3072,128]{1,0:T(8,128)(2,1)S(1)} %aggregate.2.s0), channel_id=1, source_target_pairs={{0,3},{1,0},{2,1},{3,2},{4,7},{5,4},{6,5},{7,6},{8,11},{9,8},{10,9... | collective-permute-start | bytes 2359304 | tf_op jit(solution)/shard_map/ppermute | solution.py:419
  311.3 12.3 %all-to-all-start.7 = ((bf16[4,768,128]{2,1,0:T(8,128)(2,1)}), bf16[4,768,128]{2,1,0:T(8,128)(2,1)S(1)}, u32[]{:S(2)}, u32[]{:S(2)}) async-start(bf16[4,768,128]{2,1,0:T(8,128)(2,1)} %copy-done.21), calls=%async_computation.7 | async-start | bytes 1572864 | tf_op jit(solution)/shard_map/all_to_all | solution.py:430
  370.9 17.0 %all-to-all-start.10 = ((bf16[8,32,512]{2,1,0:T(8,128)(2,1)}), bf16[8,32,512]{2,1,0:T(8,128)(2,1)S(1)}, u32[]{:S(2)}, u32[]{:S(2)}) async-start(bf16[8,32,512]{2,1,0:T(8,128)(2,1)} %broadcast_in_dim.2), calls=%async_computation.10 | async-start | bytes 524288 | tf_op jit(solution)/shard_map/all_to_all | solution.py:430
  374.7 12.0 %collective-permute-start.20 = (bf16[768,128]{1,0:T(8,128)(2,1)S(1)}, bf16[768,128]{1,0:T(8,128)(2,1)S(1)}, u32[]{:S(2)}, u32[]{:S(2)}) collective-permute-start(bf16[768,128]{1,0:T(8,128)(2,1)S(1)} %get-tuple-element.228), channel_id=1, source_target_pairs={{0,1},{1,2},{2,3},{3,0},{4,5},{5,6},{6,7},{7,4},{8,9},{9,10},{10,1... | collective-permute-start | bytes 589832 | tf_op jit(solution)/shard_map/ppermute | solution.py:419
  (38 other events, 229.2 us)
Sparse Core Ops, SparseCore 0:
  10.4 29.3 all-gather.4
  41.6 43.3 all-gather.6

commit v3 on v2

--- a/solution.py
+++ b/solution.py
@@ -44,32 +44,45 @@
 MIDDLE = HEAD + HALF * BS
 
 
-def pack_kernel(blocks_ref, counts_ref, history_ref, after_ref, out_ref, wanted):
-    del after_ref
+def pack_kernel(blocks_ref, counts_ref, history_ref, out_ref, wanted, rows_in, sem):
+    parts = sem.shape[0]
+    size = HB * BS // parts
+    copies = [
+        pltpu.make_async_copy(history_ref.at[pl.ds(k * size, size)], rows_in.at[pl.ds(k * size, size)], sem.at[k])
+        for k in range(parts)
+    ]
+    for copy in copies:
+        copy.start()
     wanted[...] = jnp.zeros_like(wanted)
     blocks = blocks_ref[...]
     slot = lax.broadcasted_iota(jnp.int32, blocks.shape, 0)
     wanted[0:CAP, 0 : blocks.shape[1]] = jnp.where(slot < counts_ref[...], blocks, HB)
     out_ref[0:HEAD, :] = wanted[...].astype(F32).astype(BF16)
-
-    def one(block, carry):
-        rows = pl.multiple_of(block * BS, BS)
-        out_ref[pl.ds(pl.multiple_of(HEAD + rows, HEAD), BS), :] = history_ref[pl.ds(rows, BS), :].astype(BF16)
-        return carry
-
-    lax.fori_loop(0, HB, one, 0)
-
-
-def pack(blocks, counts, history, after):
+    for k in range(parts):
+        copies[k].wait()
+
+        def one(block, carry, k=k):
+            rows = pl.multiple_of(k * size + block * BS, BS)
+            out_ref[pl.ds(pl.multiple_of(HEAD + rows, HEAD), BS), :] = rows_in[pl.ds(rows, BS), :].astype(BF16)
+            return carry
+
+        lax.fori_loop(0, size // BS, one, 0, unroll=2)
+
+
+def pack(blocks, counts, history):
     return call(
         pack_kernel,
         jax.ShapeDtypeStruct((HEAD + HB * BS, BS), BF16),
-        [VMEM, VMEM, VMEM, ANY],
+        [VMEM, VMEM, ANY],
         VMEM,
-        [pltpu.VMEM((HEAD, BS), jnp.int32)],
+        [
+            pltpu.VMEM((HEAD, BS), jnp.int32),
+            pltpu.VMEM(history.shape, F32),
+            pltpu.SemaphoreType.DMA((4,)),
+        ],
         (0, 3 * 1024 * 1024, 0),
         "pack",
-    )(blocks, counts, history, after)
+    )(blocks, counts, history)
 
 
 def stage_kernel(sizes, z_ref, *refs):
@@ -86,20 +99,21 @@
     mine = z_ref[0]
     zeros = jnp.zeros((BS, BS), BF16)
 
+    def block_of(source, block):
+        if len(source) == 1:
+            start = pl.multiple_of(HEAD + jnp.minimum(block, HB - 1) * BS, HEAD)
+            return jnp.where(block < HB, source[0][pl.ds(start, BS), :], zeros)
+        first = pl.multiple_of(HEAD + jnp.minimum(block, HALF - 1) * BS, HEAD)
+        second = pl.multiple_of(jnp.clip(block - HALF, 0, HALF - 1) * BS, BS)
+        late = jnp.where(block < HB, source[1][pl.ds(second, BS), :], zeros)
+        return jnp.where(block < HALF, source[0][pl.ds(first, BS), :], late)
+
     def one(reader, carry):
         column = (reader // C) * (Z * C) + mine * C + lax.rem(reader, C)
         for s, source in enumerate(sources):
+            found = [block_of(source, asked[s, slot, column]) for slot in range(CAP)]
             for slot in range(CAP):
-                block = asked[s, slot, column]
-                entry = (reader * count + s) * CAP + slot
-                if len(source) == 1:
-                    start = pl.multiple_of(HEAD + jnp.minimum(block, HB - 1) * BS, HEAD)
-                    out_ref[entry] = jnp.where(block < HB, source[0][pl.ds(start, BS), :], zeros)
-                else:
-                    first = pl.multiple_of(HEAD + jnp.minimum(block, HALF - 1) * BS, HEAD)
-                    second = pl.multiple_of(jnp.clip(block - HALF, 0, HALF - 1) * BS, BS)
-                    late = jnp.where(block < HB, source[1][pl.ds(second, BS), :], zeros)
-                    out_ref[entry] = jnp.where(block < HALF, source[0][pl.ds(first, BS), :], late)
+                out_ref[(reader * count + s) * CAP + slot] = found[slot]
         return carry
 
     lax.fori_loop(0, G, one, 0)
@@ -124,43 +138,36 @@
     )(my_z, *[part for source in sources for part in source], *after)
 
 
-def aggregate_kernel(sides, count, skip, code_ref, other_ref, blocks_ref, table_ref, *refs):
-    halos, refs = refs[:count], refs[count:]
-    tiles_ref, out_ref, table, halo, tiles, table_sem, halo_sem, tiles_sem = refs
+def aggregate_kernel(sides, count, skip, code_ref, other_ref, blocks_ref, table, tiles, *refs):
+    halos, (out_ref, halo, sem) = refs[:count], refs[count:]
 
     def local(row):
         pair = (row, other_ref[row])
         return [blocks_ref[block] for block in pair] if skip else pair
 
-    copy = pltpu.make_async_copy(table_ref.at[pl.ds(skip, table.shape[0])], table, table_sem)
-    copy.start()
-
     def start(row, carry):
-        pltpu.make_async_copy(tiles_ref.at[row], tiles.at[row], tiles_sem.at[row // STEP]).start()
         for slot in range(TPR - 2):
             code = code_ref[row * (TPR - 2) + slot]
-            distance, group, number = code // 256, lax.rem(code // 8, 32), lax.rem(code, 8)
+            distance, group, number = code >> 8, (code >> 3) & 31, code & 7
             for side, (piece, source, sources) in enumerate(sides):
 
                 @pl.when(distance == side)
                 def _(piece=piece, source=source, sources=sources, group=group, number=number, slot=slot):
                     place = (group * sources + source) * CAP + number
-                    pltpu.make_async_copy(halos[piece].at[place], halo.at[row, slot], halo_sem.at[row // STEP]).start()
+                    pltpu.make_async_copy(halos[piece].at[place], halo.at[row, slot], sem.at[row >> 2]).start()
 
         return carry
 
     lax.fori_loop(0, NB, start, 0)
-    copy.wait()
 
     def compute(group, carry):
         rows = pl.ds(group * STEP, STEP)
-        pltpu.make_async_copy(tiles_ref.at[rows], tiles.at[rows], tiles_sem.at[group]).wait()
-        pltpu.make_async_copy(halo.at[rows], halo.at[rows], halo_sem.at[group]).wait()
+        pltpu.make_async_copy(halo.at[rows], halo.at[rows], sem.at[group]).wait()
         for k in range(STEP):
             row = group * STEP + k
             left = jnp.concatenate([tiles[row, t] for t in range(TPR)], axis=1)
             right = jnp.concatenate(
-                [table[pl.ds(pl.multiple_of(block * BS, BS), BS), :] for block in local(row)]
+                [table[pl.ds(pl.multiple_of(skip + block * BS, HEAD), BS), :] for block in local(row)]
                 + [halo[row, t] for t in range(TPR - 2)],
                 axis=0,
             )
@@ -175,19 +182,12 @@
     return call(
         functools.partial(aggregate_kernel, sides, len(halos), skip),
         jax.ShapeDtypeStruct((ROWS, BS), BF16),
-        [SMEM] * 3 + [ANY] * (len(halos) + 2),
+        [SMEM] * 3 + [VMEM] * 2 + [ANY] * len(halos),
         VMEM,
-        [
-            pltpu.VMEM((table.shape[0] - skip, BS), BF16),
-            pltpu.VMEM((NB, TPR - 2, BS, BS), BF16),
-            pltpu.VMEM((NB, TPR, BS, BS), BF16),
-            pltpu.SemaphoreType.DMA,
-            pltpu.SemaphoreType.DMA((NB // STEP,)),
-            pltpu.SemaphoreType.DMA((NB // STEP,)),
-        ],
+        [pltpu.VMEM((NB, TPR - 2, BS, BS), BF16), pltpu.SemaphoreType.DMA((NB // STEP,))],
         (2 * NB * TPR * BS**3, 2 * NB * TPR * BS * BS * 2, 0),
         "aggregate",
-    )(code, other, blocks, table, *halos, tiles)
+    )(code, other, blocks, table, tiles, *halos)
 
 
 def sigmoid(value):
@@ -225,7 +225,8 @@
     )(*summed, weight)
 
 
-def second_kernel(x_ref, summed_ref, weight_ref, cot_ref, out_ref, delta_ref, back_ref):
+def second_kernel(x_ref, summed_ref, weight_ref, cot_ref, after_ref, out_ref, grad_ref, back_ref, delta_ref):
+    del after_ref
     step = 128
 
     def one(row, carry):
@@ -246,46 +247,56 @@
         return carry
 
     lax.fori_loop(0, QUARTER // step, one, 0)
-
-
-def second_layer(my_x, summed, weight, cot):
-    piece = jax.ShapeDtypeStruct((X, QUARTER, BS), BF16)
-    return call(
-        second_kernel,
-        (piece, jax.ShapeDtypeStruct((QUARTER, X * BS), BF16), piece),
-        [SMEM] + [VMEM] * 3,
-        (VMEM,) * 3,
-        [],
-        (4 * QUARTER * 512 * 512, 5 * 1024 * 1024, QUARTER * 512),
-        "second_layer",
-    )(my_x, summed, weight, cot)
-
-
-def grad_second_kernel(summed_ref, delta_ref, out_ref):
     for k in range(X):
-        out_ref[k * BS : (k + 1) * BS, :] = lax.dot_general(
+        grad_ref[k * BS : (k + 1) * BS, :] = lax.dot_general(
             summed_ref[k], delta_ref[...], (((0,), (0,)), ((), ())), preferred_element_type=F32
         ).astype(BF16)
 
 
-def grad_second_part(summed, delta):
-    return call(
-        grad_second_kernel,
-        jax.ShapeDtypeStruct((X * BS, X * BS), BF16),
-        [VMEM] * 2,
-        VMEM,
-        [],
-        (2 * QUARTER * 512 * 512, 3 * 1024 * 1024, 0),
-        "grad_second",
-    )(summed, delta)
-
-
-def prepare_kernel(x_ref, tiles_ref, s0, s1, s2, far0, far1, turned_ref, summed_ref, tiles, sem):
+def second_layer(my_x, summed, weight, cot, after):
+    piece = jax.ShapeDtypeStruct((X, QUARTER, BS), BF16)
+    return call(
+        second_kernel,
+        (piece, jax.ShapeDtypeStruct((X * BS, X * BS), BF16), piece),
+        [SMEM] + [VMEM] * 3 + [ANY],
+        (VMEM,) * 3,
+        [pltpu.VMEM((QUARTER, X * BS), BF16)],
+        (6 * QUARTER * 512 * 512, 5 * 1024 * 1024, QUARTER * 512),
+        "second_layer",
+    )(my_x, summed, weight, cot, after)
+
+
+def turn_kernel(tiles_ref, after_ref, turned_ref, tiles, sem):
+    del after_ref
+
     def start(row, carry):
         pltpu.make_async_copy(tiles_ref.at[row, pl.ds(0, 2)], tiles.at[row], sem).start()
         return carry
 
     lax.fori_loop(0, NB, start, 0)
+    pltpu.make_async_copy(tiles, tiles, sem).wait()
+
+    def turn_tiles(row, carry):
+        for t in range(2):
+            turned_ref[row, pl.ds(t * BS, BS), :] = tiles[row, t].T
+        return carry
+
+    lax.fori_loop(0, NB, turn_tiles, 0, unroll=2)
+
+
+def turn_local(tiles, after):
+    return call(
+        turn_kernel,
+        jax.ShapeDtypeStruct((NB, 2 * BS, BS), BF16),
+        [ANY, ANY],
+        VMEM,
+        [pltpu.VMEM((NB, 2, BS, BS), BF16), pltpu.SemaphoreType.DMA],
+        (0, 4 * 1024 * 1024, 0),
+        "turn_local",
+    )(tiles, after)
+
+
+def prepare_kernel(x_ref, s0, s1, s2, far0, far1, summed_ref):
     x = x_ref[0]
     half = ROWS // 2
     for source, step, begin in ((s0, 0, 0), (s1, X - 1, 0), (s2, 1, 0), (far0, 2, 0), (far1, 2, half)):
@@ -298,26 +309,18 @@
             return carry
 
         lax.fori_loop(0, source.shape[0] // BS, one, 0, unroll=4)
-    pltpu.make_async_copy(tiles, tiles, sem).wait()
-
-    def turn_tiles(row, carry):
-        for t in range(2):
-            turned_ref[row, pl.ds(t * BS, BS), :] = tiles[row, t].T
-        return carry
-
-    lax.fori_loop(0, NB, turn_tiles, 0, unroll=2)
-
-
-def prepare(my_x, tiles, summed):
+
+
+def prepare(my_x, summed):
     return call(
         prepare_kernel,
-        (jax.ShapeDtypeStruct((NB, 2 * BS, BS), BF16), jax.ShapeDtypeStruct((X * BS, ROWS), BF16)),
-        [SMEM, ANY] + [VMEM] * 5,
-        (VMEM, VMEM),
-        [pltpu.VMEM((NB, 2, BS, BS), BF16), pltpu.SemaphoreType.DMA],
-        (0, 10 * 1024 * 1024, 0),
+        jax.ShapeDtypeStruct((X * BS, ROWS), BF16),
+        [SMEM] + [VMEM] * 5,
+        VMEM,
+        [],
+        (0, 7 * 1024 * 1024, 0),
         "prepare",
-    )(my_x, tiles, *summed)
+    )(my_x, *summed)
 
 
 def last_kernel(other_ref, back_ref, turned_ref, slope_ref, summed_ref, second_ref, out_ref, total, delta):
@@ -460,7 +463,7 @@
     my_x = lax.axis_index("mp").astype(jnp.int32)
     blocks = send_blocks[0].T
     other = tile_columns[:, 1]
-    table_input = pack(blocks, send_counts, input_history, tile_columns)
+    table_input = pack(blocks, send_counts, input_history)
 
     def hop(pair):
         return shift(pair[0], 1), shift(pair[1], -1)
@@ -474,14 +477,15 @@
     def beside(*sources, after=()):
         return apart(lambda sources, after: send(*sources, after=after), my_z, sources, after)
 
-    def step_zero(table, blocks, counts, history):
-        return hop((table, table)), beside(table), pack(blocks, counts, history, table)
+    def step_zero(table, blocks, counts, history, first, second):
+        weight = jnp.concatenate([first, second])
+        return hop((table, table)), beside(table), pack(blocks, counts, history), weight
 
     def step_one(pair, other):
         return hop(pair), hop((other, other)), beside(*pair, other)
 
     def step_two(pair, other):
-        return hop(pair), hop(other), beside(*pair, *other)
+        return hop(pair), hop(other), beside(*pair, other[0])
 
     def step_three(pair, other):
         return far_hop(pair), hop(other), beside(*pair, other[0])
@@ -489,22 +493,23 @@
     def step_four(far, other, after):
         return far_hop(other), beside(far, after=after)
 
-    weights = lax.all_gather(jnp.concatenate([weight_first, weight_second]), "mp", axis=0, tiled=False)
+    one, piece0, table_hidden, weight = apart(
+        step_zero, my_z, table_input, blocks, send_counts, hidden_history, weight_first, weight_second
+    )
+    weights = lax.all_gather(weight, "mp", axis=0, tiled=False)
     cot = lax.all_gather(cotangent, "mp", axis=0, tiled=False)
     cot_rows = lax.dynamic_slice(cot, (0, my_x * QUARTER, 0), (X, QUARTER, BS))
     order = jnp.stack([my_x, (my_x - 1) % X, (my_x + 1) % X, (my_x + 2) % X])
     columns = lax.dynamic_slice(weights, (0, 0, my_x * BS), (X, BS, BS))[order].reshape(X * BS, BS)
     weight_all = weights[:, BS:].reshape(X * BS, X * BS)
 
-    one, piece0, table_hidden = apart(step_zero, my_z, table_input, blocks, send_counts, hidden_history)
     two, one_hidden, piece1 = apart(step_one, my_z, one, table_hidden)
     three, two_hidden, piece2 = apart(step_two, my_z, two, one_hidden)
     far, three_hidden, piece3 = apart(step_three, my_z, three, two_hidden)
-    far_hidden, piece4 = apart(step_four, my_z, far, three_hidden, (columns, weight_all, cot_rows))
-    piece5 = send(far_hidden, *three_hidden, two_hidden[1])
-
-    sides_input = ((0, 0, 1), (1, 1, 3), (2, 1, 4), (3, 1, 3), (4, 0, 1), (3, 0, 3), (2, 0, 4), (1, 0, 3))
-    sides_hidden = ((0, 2, 3), (1, 3, 4), (3, 3, 4), (3, 2, 4), (3, 0, 4), (3, 1, 4), (2, 2, 3), (1, 2, 4))
+    far_hidden, piece4 = apart(step_four, my_z, far, three_hidden, (weights, cot))
+
+    sides_input = ((0, 0, 1), (1, 1, 3), (2, 1, 3), (3, 1, 3), (4, 0, 1), (3, 0, 3), (2, 0, 3), (1, 0, 3))
+    sides_hidden = ((0, 2, 3), (3, 4, 5), (3, 3, 5), (3, 2, 5), (3, 0, 5), (3, 1, 5), (2, 2, 3), (1, 2, 3))
     use = tile_columns[:, 2:] - NB
     owner, slot = use // CAP, use % CAP
     group = (owner // (Z * C)) * C + owner % C
@@ -512,18 +517,19 @@
 
     batch = batch_blocks.reshape(-1)
     halo_input = (piece0, piece1, piece2, piece3, piece4)
+    summed_first = aggregate(sides_input, HEAD, table_input, halo_input, tile_values, code, other, batch)
+    piece5 = send(far_hidden, *three_hidden, two_hidden[1], one_hidden[1], after=(summed_first,))
     halo_hidden = (piece1, piece2, piece3, piece5)
-    summed_first = aggregate(sides_input, HEAD, table_input, halo_input, tile_values, code, other, batch)
     all_first = gather_features(summed_first)
     hidden_first, slope_first = first_layer(all_first, columns)
-    turned_tiles, turned_first = prepare(my_x.reshape(1), tile_values, all_first)
+    turned_tiles = turn_local(tile_values, summed_first)
+    turned_first = prepare(my_x.reshape(1), all_first)
     summed_second = aggregate(sides_hidden, 0, hidden_first, halo_hidden, tile_values, code, other, batch)
     rows_second = exchange(summed_second.reshape(X, QUARTER, BS), "mp")
-    out_rows, delta_rows, back_rows = second_layer(
-        my_x.reshape(1), rows_second, weight_all, cot_rows
+    out_rows, part_second, back_rows = second_layer(
+        my_x.reshape(1), rows_second, weight_all, cot_rows, turned_first
     )
     back_second = exchange(back_rows, "mp").reshape(ROWS, BS)
-    part_second = grad_second_part(rows_second, delta_rows)
     got = last_part(other, back_second, turned_tiles, slope_first, turned_first, part_second)
 
     dealt = X * G

time: 397 us -> 389 us (0.980)
  blocking collectives: 205 us -> 182 us
  waiting for transfers between devices: 42 us -> 59.2 us
  Pallas kernels: 55.6 us -> 48.6 us
  starting transfers between devices: 46.6 us -> 51.4 us
    all_to_all x8 -> x7, blocking collectives: 205 us -> 182 us  [exchange(): return lax.all_to_all(value, axes, split_axis=0, concat_axis=0, tiled=True)]
    all_to_all x3 -> x4, waiting for transfers between devices: 0.76 us -> 19.6 us  [exchange(): return lax.all_to_all(value, axes, split_axis=0, concat_axis=0, tiled=True)]
    pallas_call x2, Pallas kernels: 16.5 us -> 8.18 us  [aggregate(): call(functools.partial(aggregate_kernel, sides, len(halos), skip), jax.Sh...]
    all_to_all x3 -> x4, starting transfers between devices: 12.1 us -> 16.8 us  [exchange(): return lax.all_to_all(value, axes, split_axis=0, concat_axis=0, tiled=True)]
    unnamed x70 -> x47, local copies, waits for them, and re-layouts: 19.1 us -> 18.6 us
  transfers between devices with their start and end apart: 28 -> 29, of which waited for: 7 -> 10; matrix products, arithmetic and copies ran while one was open for 2% -> 3% of each run, Pallas kernels for 9% -> 7%
where the time goes in v3:
time: 389 us; the launch traced here: 387 us
  blocking collectives  182 us (47%)
  waiting for transfers between devices  59.2 us (15%)
  starting transfers between devices  51.4 us (13%)
  Pallas kernels  48.6 us (12%)
  local copies, waits for them, and re-layouts  31.9 us (8%)
  between operations  14.3 us (4%)
    all_to_all x7, blocking collectives, exchange(): return lax.all_to_all(value, axes, split_axis=0, concat_axis=0, tiled=True)  182 us
    ppermute x7, waiting for transfers between devices, turn(): return lax.ppermute(value, 'mp', [(i, (i + step) % X) for i in range(X)])  32.7 us
    ppermute x16, starting transfers between devices, shift(): return lax.ppermute(value, 'z', [(i, (i + step) % Z) for i in range(Z)])  25.8 us
    all_to_all x4, waiting for transfers between devices, exchange(): return lax.all_to_all(value, axes, split_axis=0, concat_axis=0, tiled=True)  19.6 us
    pallas_call x6, Pallas kernels, stage(): call(functools.partial(stage_kernel, sizes), jax.ShapeDtypeStruct((entrie...  19.1 us
    unnamed x47, local copies, waits for them, and re-layouts  18.6 us
    all_to_all x4, starting transfers between devices, exchange(): return lax.all_to_all(value, axes, split_axis=0, concat_axis=0, tiled=True)  16.8 us
    ppermute x7, starting transfers between devices, turn(): return lax.ppermute(value, 'mp', [(i, (i + step) % X) for i in range(X)])  8.66 us
  transfers between devices with their start and end apart: 29, of which 10 were waited for; matrix products, arithmetic and copies ran while one was open for 3% of the time, Pallas kernels for 7%

profile of v3, /device:TPU:1, one launch (start us, length us, event | category | flops | bytes accessed | tf_op | source)
XLA Modules:
  0.0 387.2 jit_solution(9536188341548396081)
XLA Ops:
  10.6 29.6 %conditional.10 = (bf16[4112,128]{1,0:T(8,128)(2,1)}, bf16[4112,128]{1,0:T(8,128)(2,1)}, bf16[24,128,128]{2,1,0:T(8,128)(2,1)}, bf16[4112,128]{1,0:T(8,128)(2,1)S(1)}, bf16[256,512]{1,0:T(8,128)(2,1)S(1)}) conditional(s32[]{:T(128)} %convert_element_type.30, () %tuple.78, (bf16[4112,128]{1,0:T(8,128)(2,1)S(1)}, s32[]{:T(128)}, s32[3,64]{1,0:T(4,128)S(1)}, ...), branch_computations={%region_0.0_spmd, %region_1.0_spmd} | conditional | flops 524290 | bytes 15237278 | solution.py:447
  17.2 18.6 %conditional = (bf16[24,128,128]{2,1,0:T(8,128)(2,1)}) conditional(s32[]{:T(128)} %convert_element_type.9, () %tuple.47, (s32[]{:T(128)}, bf16[4112,128]{1,0:T(8,128)(2,1)S(1)}) %tuple.48), branch_computations={%region_2.0_spmd, %region_3.0_spmd} | conditional | bytes 3145736 | solution.py:447
  18.2 17.5 %all_to_all.50 = bf16[8,384,128]{2,1,0:T(8,128)(2,1)} all-to-all(bf16[8,384,128]{2,1,0:T(8,128)(2,1)S(1)} %bitcast.57), channel_id=1, replica_groups=mesh['y'=4,'z'=8,'core'=2,'mp'=4] {'y','core'}, dimensions={0} | all-to-all | bytes 1572864 | tf_op jit(solution)/shard_map/cond/branch_1_fun/cond/branch_1_fun/all_to_all | solution.py:433
  41.9 47.7 %conditional.11 = (bf16[4112,128]{1,0:T(8,128)(2,1)}, bf16[4112,128]{1,0:T(8,128)(2,1)}, bf16[4112,128]{1,0:T(8,128)(2,1)}, bf16[4112,128]{1,0:T(8,128)(2,1)}, bf16[72,128,128]{2,1,0:T(8,128)(2,1)}) conditional(s32[]{:T(128)} %convert_element_type.30, () %tuple.80, (bf16[4112,128]{1,0:T(8,128)(2,1)}, bf16[4112,128]{1,0:T(8,128)(2,1)}, ...), branch_computations={%region_4.5_spmd, %region_5.8_spmd} | conditional | flops 2 | bytes 26280188 | solution.py:447
  47.3 39.6 %conditional.1 = (bf16[72,128,128]{2,1,0:T(8,128)(2,1)}) conditional(s32[]{:T(128)} %convert_element_type.12, () %tuple.51, (s32[]{:T(128)}, bf16[4112,128]{1,0:T(8,128)(2,1)}, bf16[4112,128]{1,0:T(8,128)(2,1)}, bf16[4112,128]{1,0:T(8,128)(2,1)}) %tuple.52), branch_computations={%region_6.6_spmd, %region_7.7_spmd} | conditional | bytes 9437192 | solution.py:447
  50.9 36.0 %all_to_all.51 = bf16[8,1152,128]{2,1,0:T(8,128)(2,1)} all-to-all(bf16[8,1152,128]{2,1,0:T(8,128)(2,1)S(1)} %bitcast.53), channel_id=1, replica_groups=mesh['y'=4,'z'=8,'core'=2,'mp'=4] {'y','core'}, dimensions={0} | all-to-all | bytes 4718592 | tf_op jit(solution)/shard_map/cond/branch_1_fun/cond/branch_1_fun/all_to_all | solution.py:433
  89.6 46.7 %conditional.12 = (bf16[4112,128]{1,0:T(8,128)(2,1)}, bf16[4112,128]{1,0:T(8,128)(2,1)}, bf16[4112,128]{1,0:T(8,128)(2,1)}, bf16[4112,128]{1,0:T(8,128)(2,1)}, bf16[72,128,128]{2,1,0:T(8,128)(2,1)}) conditional(s32[]{:T(128)} %convert_element_type.30, () %tuple.82, (bf16[4112,128]{1,0:T(8,128)(2,1)}, bf16[4112,128]{1,0:T(8,128)(2,1)}, ...), branch_computations={%region_8.9_spmd, %region_9.12_spmd} | conditional | flops 2 | bytes 26280188 | solution.py:447
  94.9 40.6 %conditional.2 = (bf16[72,128,128]{2,1,0:T(8,128)(2,1)}) conditional(s32[]{:T(128)} %convert_element_type.16, () %tuple.55, (s32[]{:T(128)}, bf16[4112,128]{1,0:T(8,128)(2,1)}, bf16[4112,128]{1,0:T(8,128)(2,1)}, bf16[4112,128]{1,0:T(8,128)(2,1)}) %tuple.56), branch_computations={%region_10.10_spmd, %region_11.11_spmd} | conditional | bytes 9437192 | solution.py:447
  98.5 37.0 %all_to_all.52 = bf16[8,1152,128]{2,1,0:T(8,128)(2,1)} all-to-all(bf16[8,1152,128]{2,1,0:T(8,128)(2,1)S(1)} %bitcast.54), channel_id=1, replica_groups=mesh['y'=4,'z'=8,'core'=2,'mp'=4] {'y','core'}, dimensions={0} | all-to-all | bytes 4718592 | tf_op jit(solution)/shard_map/cond/branch_1_fun/cond/branch_1_fun/all_to_all | solution.py:433
  136.3 49.4 %conditional.13 = (bf16[2064,128]{1,0:T(8,128)(2,1)}, bf16[2048,128]{1,0:T(8,128)(2,1)}, bf16[4112,128]{1,0:T(8,128)(2,1)}, bf16[4112,128]{1,0:T(8,128)(2,1)}, bf16[72,128,128]{2,1,0:T(8,128)(2,1)}) conditional(s32[]{:T(128)} %convert_element_type.30, () %tuple.84, (bf16[4112,128]{1,0:T(8,128)(2,1)}, bf16[4112,128]{1,0:T(8,128)(2,1)}, ...), branch_computations={%region_12.13_spmd, %region_13.16_spmd} | conditional | flops 2 | bytes 24174846 | solution.py:447
  144.1 41.5 %conditional.3 = (bf16[72,128,128]{2,1,0:T(8,128)(2,1)}) conditional(s32[]{:T(128)} %convert_element_type.17, () %tuple.59, (s32[]{:T(128)}, bf16[4112,128]{1,0:T(8,128)(2,1)}, bf16[4112,128]{1,0:T(8,128)(2,1)}, bf16[4112,128]{1,0:T(8,128)(2,1)}) %tuple.60), branch_computations={%region_14.14_spmd, %region_15.15_spmd} | conditional | bytes 9437192 | solution.py:447
  147.7 37.9 %all_to_all.53 = bf16[8,1152,128]{2,1,0:T(8,128)(2,1)} all-to-all(bf16[8,1152,128]{2,1,0:T(8,128)(2,1)S(1)} %bitcast.55), channel_id=1, replica_groups=mesh['y'=4,'z'=8,'core'=2,'mp'=4] {'y','core'}, dimensions={0} | all-to-all | bytes 4718592 | tf_op jit(solution)/shard_map/cond/branch_1_fun/cond/branch_1_fun/all_to_all | solution.py:433
  185.7 24.3 %conditional.14 = (bf16[2064,128]{1,0:T(8,128)(2,1)}, bf16[2048,128]{1,0:T(8,128)(2,1)}, bf16[24,128,128]{2,1,0:T(8,128)(2,1)}) conditional(s32[]{:T(128)} %convert_element_type.30, () %tuple.86, (bf16[4112,128]{1,0:T(8,128)(2,1)}, bf16[4112,128]{1,0:T(8,128)(2,1)}, s32[]{:T(128)}, bf16[2064,128]{1,0:T(8,128)(2,1)}, bf16[2048,128]{1,0:T(8,128)(2,1)}, ...), branch_computations={%region_16.17_spmd, %region_17.20_spmd} | conditional | flops 2 | bytes 9461926 | solution.py:447
  190.7 19.2 %conditional.4 = (bf16[24,128,128]{2,1,0:T(8,128)(2,1)}) conditional(s32[]{:T(128)} %convert_element_type.26, () %tuple.63, (s32[]{:T(128)}, bf16[2064,128]{1,0:T(8,128)(2,1)}, bf16[2048,128]{1,0:T(8,128)(2,1)}, bf16[4,256,512]{2,1,0:T(8,128)(2,1)}, bf16[4,3072,128]{2,1,0:T(8,128)(2,1)}) %tuple.64), branch_computations={%region_18.18_spmd, %region_19.19_spmd} | conditional | bytes 3145736 | solution.py:447
  193.0 16.9 %all_to_all.54 = bf16[8,384,128]{2,1,0:T(8,128)(2,1)} all-to-all(bf16[8,384,128]{2,1,0:T(8,128)(2,1)S(1)} %bitcast.58), channel_id=1, replica_groups=mesh['y'=4,'z'=8,'core'=2,'mp'=4] {'y','core'}, dimensions={0} | all-to-all | bytes 1572864 | tf_op jit(solution)/shard_map/cond/branch_1_fun/cond/branch_1_fun/all_to_all | solution.py:433
  215.7 5.0 %stage.11 = bf16[120,128,128]{2,1,0:T(8,128)(2,1)S(1)} custom-call(s32[1]{0:T(128)} %bitcast.27.z_ref, bf16[2064,128]{1,0:T(8,128)(2,1)} %get-tuple-element.211.refs_0_, bf16[2048,128]{1,0:T(8,128)(2,1)} %get-tuple-element.212.refs_1_, bf16[4112,128]{1,0:T(8,128)(2,1)} %get-tuple-element.204.refs_2_, bf16[4112,128]{1,0:T(8,128)(2,1)} %get-tuple-element.205.refs_3_, ...), custom_call_target="tpu_custom_call" | custom-call | bytes 7864320 | tf_op jit(solution)/shard_map/stage/pallas_call | solution.py:126
  222.7 5.5 %all-to-all-start.5 = ((bf16[8,1920,128]{2,1,0:T(8,128)(2,1)}), bf16[8,1920,128]{2,1,0:T(8,128)(2,1)}, u32[]{:S(2)}, u32[]{:S(2)}) async-start(bf16[8,1920,128]{2,1,0:T(8,128)(2,1)} %bitcast.52), calls=%async_computation.5 | async-start | bytes 7864320 | tf_op jit(solution)/shard_map/all_to_all | solution.py:433
  230.9 17.6 %collective-permute-done.16.s1 = bf16[3072,128]{1,0:T(8,128)(2,1)S(1)} collective-permute-done((bf16[3072,128]{1,0:T(8,128)(2,1)S(1)}, bf16[3072,128]{1,0:T(8,128)(2,1)S(1)}, u32[]{:S(2)}, u32[]{:S(2)}) %collective-permute-start.16) | collective-permute-done | bytes 786464 | tf_op jit(solution)/shard_map/ppermute | solution.py:422
  254.3 6.2 %collective-permute-done.18.far0 = bf16[1536,128]{1,0:T(8,128)(2,1)S(1)} collective-permute-done((bf16[1536,128]{1,0:T(8,128)(2,1)}, bf16[1536,128]{1,0:T(8,128)(2,1)S(1)}, u32[]{:S(2)}, u32[]{:S(2)}) %collective-permute-start.18) | collective-permute-done | bytes 393248 | tf_op jit(solution)/shard_map/ppermute | solution.py:422
  265.4 9.0 %all-to-all-done.5 = bf16[8,1920,128]{2,1,0:T(8,128)(2,1)} async-done(((bf16[8,1920,128]{2,1,0:T(8,128)(2,1)}), bf16[8,1920,128]{2,1,0:T(8,128)(2,1)}, u32[]{:S(2)}, u32[]{:S(2)}) %all-to-all-start.5) | async-done | bytes 3932192 | tf_op jit(solution)/shard_map/all_to_all | solution.py:433
  311.1 7.4 %all-to-all-done.7 = bf16[4,768,128]{2,1,0:T(8,128)(2,1)S(1)} async-done(((bf16[4,768,128]{2,1,0:T(8,128)(2,1)}), bf16[4,768,128]{2,1,0:T(8,128)(2,1)S(1)}, u32[]{:S(2)}, u32[]{:S(2)}) %all-to-all-start.7) | async-done | bytes 786464 | tf_op jit(solution)/shard_map/all_to_all | solution.py:433
  325.5 19.3 %all_to_all.55.got_ref = bf16[32,16,640]{2,1,0:T(8,128)(2,1)S(1)} all-to-all(bf16[32,16,640]{2,1,0:T(8,128)(2,1)S(1)} %bitcast.59), channel_id=1, replica_groups=mesh['y'=4,'z'=8,'core'=2,'mp'=4] {'mp','y','core'}, dimensions={0} | all-to-all | bytes 1310720 | tf_op jit(solution)/shard_map/all_to_all | solution.py:433
  345.0 16.8 %all_to_all.56 = bf16[8,32,512]{2,1,0:T(8,128)(2,1)S(1)} all-to-all(bf16[8,32,512]{2,1,0:T(8,128)(2,1)S(1)} %get-tuple-element.218), channel_id=1, replica_groups=mesh['y'=4,'z'=8,'core'=2,'mp'=4] {'z'}, dimensions={0} | all-to-all | bytes 524288 | tf_op jit(solution)/shard_map/all_to_all | solution.py:433
  369.7 8.7 %collective-permute-done.20.refs_1_ = bf16[768,128]{1,0:T(8,128)(2,1)S(1)} collective-permute-done((bf16[768,128]{1,0:T(8,128)(2,1)S(1)}, bf16[768,128]{1,0:T(8,128)(2,1)S(1)}, u32[]{:S(2)}, u32[]{:S(2)}) %collective-permute-start.20) | collective-permute-done | bytes 196640 | tf_op jit(solution)/shard_map/ppermute | solution.py:422
  (138 shorter events, 131.9 us)
Async XLA Ops:
  7.2 178.5 %all-gather.5.cloned.1.call-start = ((), (), s32[]{:S(2)}) async-start(), calls=%async_computation.11 | async-start | bytes 1310720 | tf_op jit(solution)/shard_map/all_gather | solution.py:499
  10.6 29.6 %collective-permute-start.14 = (bf16[4112,128]{1,0:T(8,128)(2,1)S(1)}, bf16[4112,128]{1,0:T(8,128)(2,1)}, u32[]{:S(2)}, u32[]{:S(2)}) collective-permute-start(bf16[4112,128]{1,0:T(8,128)(2,1)S(1)} %get-tuple-element.98), channel_id=1, source_target_pairs={{0,8},{8,16},{16,24},{24,32},{32,40},{40,48},{48,56},{56,0},{1,9},... | collective-permute-start | bytes 3158024 | tf_op jit(solution)/shard_map/cond/branch_1_fun/ppermute | solution.py:418
  13.1 27.0 %collective-permute-start.15 = (bf16[4112,128]{1,0:T(8,128)(2,1)S(1)}, bf16[4112,128]{1,0:T(8,128)(2,1)}, u32[]{:S(2)}, u32[]{:S(2)}) collective-permute-start(bf16[4112,128]{1,0:T(8,128)(2,1)S(1)} %get-tuple-element.98), channel_id=1, source_target_pairs={{0,56},{8,0},{16,8},{24,16},{32,24},{40,32},{48,40},{56,48},{1,57}... | collective-permute-start | bytes 3158024 | tf_op jit(solution)/shard_map/cond/branch_1_fun/ppermute | solution.py:418
  40.9 144.8 %all-gather.7.cloned.1.call-start = ((), (), s32[]{:S(2)}) async-start(), calls=%async_computation.12 | async-start | bytes 3932160 | tf_op jit(solution)/shard_map/all_gather | solution.py:500
  41.9 45.1 %collective-permute-start = (bf16[4112,128]{1,0:T(8,128)(2,1)}, bf16[4112,128]{1,0:T(8,128)(2,1)}, u32[]{:S(2)}, u32[]{:S(2)}) collective-permute-start(bf16[4112,128]{1,0:T(8,128)(2,1)} %get-tuple-element.122), channel_id=1, source_target_pairs={{0,8},{8,16},{16,24},{24,32},{32,40},{40,48},{48,56},{56,0},{1,9},... | collective-permute-start | bytes 3158024 | tf_op jit(solution)/shard_map/cond/branch_1_fun/ppermute | solution.py:418
  42.0 45.0 %collective-permute-start.1 = (bf16[4112,128]{1,0:T(8,128)(2,1)}, bf16[4112,128]{1,0:T(8,128)(2,1)}, u32[]{:S(2)}, u32[]{:S(2)}) collective-permute-start(bf16[4112,128]{1,0:T(8,128)(2,1)} %get-tuple-element.123), channel_id=1, source_target_pairs={{0,56},{8,0},{16,8},{24,16},{32,24},{40,32},{48,40},{56,48},{1,57}... | collective-permute-start | bytes 3158024 | tf_op jit(solution)/shard_map/cond/branch_1_fun/ppermute | solution.py:418
  44.7 44.9 %collective-permute-start.2 = (bf16[4112,128]{1,0:T(8,128)(2,1)}, bf16[4112,128]{1,0:T(8,128)(2,1)}, u32[]{:S(2)}, u32[]{:S(2)}) collective-permute-start(bf16[4112,128]{1,0:T(8,128)(2,1)} %get-tuple-element.124), channel_id=1, source_target_pairs={{0,8},{8,16},{16,24},{24,32},{32,40},{40,48},{48,56},{56,0},{1,9},... | collective-permute-start | bytes 3158024 | tf_op jit(solution)/shard_map/cond/branch_1_fun/ppermute | solution.py:418
  44.7 44.9 %collective-permute-start.3 = (bf16[4112,128]{1,0:T(8,128)(2,1)}, bf16[4112,128]{1,0:T(8,128)(2,1)}, u32[]{:S(2)}, u32[]{:S(2)}) collective-permute-start(bf16[4112,128]{1,0:T(8,128)(2,1)} %get-tuple-element.124), channel_id=1, source_target_pairs={{0,56},{8,0},{16,8},{24,16},{32,24},{40,32},{48,40},{56,48},{1,57}... | collective-permute-start | bytes 3158024 | tf_op jit(solution)/shard_map/cond/branch_1_fun/ppermute | solution.py:418
  89.6 46.0 %collective-permute-start.4 = (bf16[4112,128]{1,0:T(8,128)(2,1)}, bf16[4112,128]{1,0:T(8,128)(2,1)}, u32[]{:S(2)}, u32[]{:S(2)}) collective-permute-start(bf16[4112,128]{1,0:T(8,128)(2,1)} %get-tuple-element.130), channel_id=1, source_target_pairs={{0,8},{8,16},{16,24},{24,32},{32,40},{40,48},{48,56},{56,0},{1,9},... | collective-permute-start | bytes 3158024 | tf_op jit(solution)/shard_map/cond/branch_1_fun/ppermute | solution.py:418
  90.5 45.1 %collective-permute-start.5 = (bf16[4112,128]{1,0:T(8,128)(2,1)}, bf16[4112,128]{1,0:T(8,128)(2,1)}, u32[]{:S(2)}, u32[]{:S(2)}) collective-permute-start(bf16[4112,128]{1,0:T(8,128)(2,1)} %get-tuple-element.131), channel_id=1, source_target_pairs={{0,56},{8,0},{16,8},{24,16},{32,24},{40,32},{48,40},{56,48},{1,57}... | collective-permute-start | bytes 3158024 | tf_op jit(solution)/shard_map/cond/branch_1_fun/ppermute | solution.py:418
  92.3 44.0 %collective-permute-start.6 = (bf16[4112,128]{1,0:T(8,128)(2,1)}, bf16[4112,128]{1,0:T(8,128)(2,1)}, u32[]{:S(2)}, u32[]{:S(2)}) collective-permute-start(bf16[4112,128]{1,0:T(8,128)(2,1)} %get-tuple-element.132), channel_id=1, source_target_pairs={{0,8},{8,16},{16,24},{24,32},{32,40},{40,48},{48,56},{56,0},{1,9},... | collective-permute-start | bytes 3158024 | tf_op jit(solution)/shard_map/cond/branch_1_fun/ppermute | solution.py:418
  92.3 44.0 %collective-permute-start.7 = (bf16[4112,128]{1,0:T(8,128)(2,1)}, bf16[4112,128]{1,0:T(8,128)(2,1)}, u32[]{:S(2)}, u32[]{:S(2)}) collective-permute-start(bf16[4112,128]{1,0:T(8,128)(2,1)} %get-tuple-element.133), channel_id=1, source_target_pairs={{0,56},{8,0},{16,8},{24,16},{32,24},{40,32},{48,40},{56,48},{1,57}... | collective-permute-start | bytes 3158024 | tf_op jit(solution)/shard_map/cond/branch_1_fun/ppermute | solution.py:418
  136.3 49.3 %collective-permute-start.10 = (bf16[4112,128]{1,0:T(8,128)(2,1)}, bf16[4112,128]{1,0:T(8,128)(2,1)}, u32[]{:S(2)}, u32[]{:S(2)}) collective-permute-start(bf16[4112,128]{1,0:T(8,128)(2,1)} %get-tuple-element.141), channel_id=1, source_target_pairs={{0,8},{8,16},{16,24},{24,32},{32,40},{40,48},{48,56},{56,0},{1,9},... | collective-permute-start | bytes 3158024 | tf_op jit(solution)/shard_map/cond/branch_1_fun/ppermute | solution.py:418
  136.7 48.9 %collective-permute-start.11 = (bf16[4112,128]{1,0:T(8,128)(2,1)}, bf16[4112,128]{1,0:T(8,128)(2,1)}, u32[]{:S(2)}, u32[]{:S(2)}) collective-permute-start(bf16[4112,128]{1,0:T(8,128)(2,1)} %get-tuple-element.142), channel_id=1, source_target_pairs={{0,56},{8,0},{16,8},{24,16},{32,24},{40,32},{48,40},{56,48},{1,57}... | collective-permute-start | bytes 3158024 | tf_op jit(solution)/shard_map/cond/branch_1_fun/ppermute | solution.py:418
  140.0 45.6 %collective-permute-start.8 = (bf16[2064,128]{1,0:T(8,128)(2,1)S(1)}, bf16[2064,128]{1,0:T(8,128)(2,1)}, u32[]{:S(2)}, u32[]{:S(2)}) collective-permute-start(bf16[2064,128]{1,0:T(8,128)(2,1)S(1)} %slice.30), channel_id=1, source_target_pairs={{0,8},{8,16},{16,24},{24,32},{32,40},{40,48},{48,56},{56,0},{1,9},... | collective-permute-start | bytes 1585160 | tf_op jit(solution)/shard_map/cond/branch_1_fun/ppermute | solution.py:418
  141.2 44.4 %collective-permute-start.9 = (bf16[2048,128]{1,0:T(8,128)(2,1)S(1)}, bf16[2048,128]{1,0:T(8,128)(2,1)}, u32[]{:S(2)}, u32[]{:S(2)}) collective-permute-start(bf16[2048,128]{1,0:T(8,128)(2,1)S(1)} %slice.31), channel_id=1, source_target_pairs={{0,56},{8,0},{16,8},{24,16},{32,24},{40,32},{48,40},{56,48},{1,57}... | collective-permute-start | bytes 1572872 | tf_op jit(solution)/shard_map/cond/branch_1_fun/ppermute | solution.py:418
  186.8 23.2 %collective-permute-start.12 = (bf16[2064,128]{1,0:T(8,128)(2,1)S(1)}, bf16[2064,128]{1,0:T(8,128)(2,1)}, u32[]{:S(2)}, u32[]{:S(2)}) collective-permute-start(bf16[2064,128]{1,0:T(8,128)(2,1)S(1)} %slice.32), channel_id=1, source_target_pairs={{0,8},{8,16},{16,24},{24,32},{32,40},{40,48},{48,56},{56,0},{1,9},... | collective-permute-start | bytes 1585160 | tf_op jit(solution)/shard_map/cond/branch_1_fun/ppermute | solution.py:418
  188.0 22.0 %collective-permute-start.13 = (bf16[2048,128]{1,0:T(8,128)(2,1)S(1)}, bf16[2048,128]{1,0:T(8,128)(2,1)}, u32[]{:S(2)}, u32[]{:S(2)}) collective-permute-start(bf16[2048,128]{1,0:T(8,128)(2,1)S(1)} %slice.33), channel_id=1, source_target_pairs={{0,56},{8,0},{16,8},{24,16},{32,24},{40,32},{48,40},{56,48},{1,57}... | collective-permute-start | bytes 1572872 | tf_op jit(solution)/shard_map/cond/branch_1_fun/ppermute | solution.py:418
  222.7 51.7 %all-to-all-start.5 = ((bf16[8,1920,128]{2,1,0:T(8,128)(2,1)}), bf16[8,1920,128]{2,1,0:T(8,128)(2,1)}, u32[]{:S(2)}, u32[]{:S(2)}) async-start(bf16[8,1920,128]{2,1,0:T(8,128)(2,1)} %bitcast.52), calls=%async_computation.5 | async-start | bytes 7864320 | tf_op jit(solution)/shard_map/all_to_all | solution.py:433
  228.2 20.3 %collective-permute-start.16 = (bf16[3072,128]{1,0:T(8,128)(2,1)S(1)}, bf16[3072,128]{1,0:T(8,128)(2,1)S(1)}, u32[]{:S(2)}, u32[]{:S(2)}) collective-permute-start(bf16[3072,128]{1,0:T(8,128)(2,1)S(1)} %aggregate.2.s0.refs_6_.after_ref), channel_id=1, source_target_pairs={{0,1},{1,2},{2,3},{3,0},{4,5},{5,6},{6,7},{7,4},{8,9},{9,10},{10,1... | collective-permute-start | bytes 2359304 | tf_op jit(solution)/shard_map/ppermute | solution.py:422
  229.5 19.8 %collective-permute-start.17 = (bf16[3072,128]{1,0:T(8,128)(2,1)S(1)}, bf16[3072,128]{1,0:T(8,128)(2,1)S(1)}, u32[]{:S(2)}, u32[]{:S(2)}) collective-permute-start(bf16[3072,128]{1,0:T(8,128)(2,1)S(1)} %aggregate.2.s0.refs_6_.after_ref), channel_id=1, source_target_pairs={{0,3},{1,0},{2,1},{3,2},{4,7},{5,4},{6,5},{7,6},{8,11},{9,8},{10,9... | collective-permute-start | bytes 2359304 | tf_op jit(solution)/shard_map/ppermute | solution.py:422
  282.2 15.2 %all-to-all-start.6 = ((bf16[4,768,128]{2,1,0:T(8,128)(2,1)}), bf16[4,768,128]{2,1,0:T(8,128)(2,1)S(1)}, u32[]{:S(2)}, u32[]{:S(2)}) async-start(bf16[4,768,128]{2,1,0:T(8,128)(2,1)} %bitcast.30), calls=%async_computation.6 | async-start | bytes 1572864 | tf_op jit(solution)/shard_map/all_to_all | solution.py:433
  305.1 13.4 %all-to-all-start.7 = ((bf16[4,768,128]{2,1,0:T(8,128)(2,1)}), bf16[4,768,128]{2,1,0:T(8,128)(2,1)S(1)}, u32[]{:S(2)}, u32[]{:S(2)}) async-start(bf16[4,768,128]{2,1,0:T(8,128)(2,1)} %get-tuple-element.213), calls=%async_computation.7 | async-start | bytes 1572864 | tf_op jit(solution)/shard_map/all_to_all | solution.py:433
  362.5 17.0 %all-to-all-start.10 = ((bf16[8,32,512]{2,1,0:T(8,128)(2,1)}), bf16[8,32,512]{2,1,0:T(8,128)(2,1)S(1)}, u32[]{:S(2)}, u32[]{:S(2)}) async-start(bf16[8,32,512]{2,1,0:T(8,128)(2,1)} %broadcast_in_dim.2), calls=%async_computation.10 | async-start | bytes 524288 | tf_op jit(solution)/shard_map/all_to_all | solution.py:433
  (28 other events, 130.8 us)
Sparse Core Ops, SparseCore 0:
  41.0 26.5 all-gather.4
  69.4 43.3 all-gather.6

commit v4 on v3

--- a/solution.py
+++ b/solution.py
@@ -392,6 +392,27 @@
         cost_estimate=pl.CostEstimate(flops=0, bytes_accessed=1024 * 1024, transcendentals=0),
         name="sum_parts",
     )(got, held)
+
+
+def planes_kernel(parts_ref, after_ref, out_ref):
+    del after_ref
+    total = parts_ref[0].astype(F32)
+    for z in range(1, Z):
+        total += parts_ref[z].astype(F32)
+    for reader in range(G):
+        out_ref[reader] = total.astype(BF16)
+
+
+def sum_planes(parts, after):
+    return call(
+        planes_kernel,
+        jax.ShapeDtypeStruct((G,) + parts.shape[1:], BF16),
+        [VMEM, ANY],
+        VMEM,
+        [],
+        (0, 1024 * 1024, 0),
+        "sum_planes",
+    )(parts, after)
 
 
 def assemble_kernel(x_ref, *refs):
@@ -537,8 +558,7 @@
     parts, out_rows = sum_parts(got, out_rows)
     quarters = [out_rows[0]] + [turn(out_rows[k], k) for k in range(1, X)]
     layer_out = assemble(my_x.reshape(1), quarters)
-    both = exchange(parts, "z").astype(F32).sum(0).astype(BF16)
-    both = exchange(jnp.broadcast_to(both[None], (G,) + both.shape), ("y", "core"))
+    both = exchange(sum_planes(exchange(parts, "z"), layer_out), ("y", "core"))
     both = both.reshape(G, 2, -1, X * BS).astype(F32)
     grad_first = both[:, 0].reshape(BS, X * BS)
     grad_second = both[:, 1].reshape(BS, X * BS)

time: 389 us -> 384 us (0.987)
  blocking collectives: 182 us -> 175 us
    all_to_all x7, blocking collectives: 182 us -> 175 us  [exchange(): return lax.all_to_all(value, axes, split_axis=0, concat_axis=0, tiled=True)]
    unnamed x47 -> x49, local copies, waits for them, and re-layouts: 18.6 us -> 19.7 us
where the time goes in v4:
time: 384 us; the launch traced here: 382 us
  blocking collectives  175 us (46%)
  waiting for transfers between devices  59.3 us (15%)
  starting transfers between devices  52.2 us (14%)
  Pallas kernels  49.3 us (13%)
  local copies, waits for them, and re-layouts  32.2 us (8%)
  between operations  14.3 us (4%)
    all_to_all x7, blocking collectives, exchange(): return lax.all_to_all(value, axes, split_axis=0, concat_axis=0, tiled=True)  175 us
    ppermute x7, waiting for transfers between devices, turn(): return lax.ppermute(value, 'mp', [(i, (i + step) % X) for i in range(X)])  32.7 us
    ppermute x16, starting transfers between devices, shift(): return lax.ppermute(value, 'z', [(i, (i + step) % Z) for i in range(Z)])  25.8 us
    unnamed x49, local copies, waits for them, and re-layouts  19.7 us
    all_to_all x4, waiting for transfers between devices, exchange(): return lax.all_to_all(value, axes, split_axis=0, concat_axis=0, tiled=True)  19.7 us
    pallas_call x6, Pallas kernels, stage(): call(functools.partial(stage_kernel, sizes), jax.ShapeDtypeStruct((entrie...  19.1 us
    all_to_all x4, starting transfers between devices, exchange(): return lax.all_to_all(value, axes, split_axis=0, concat_axis=0, tiled=True)  17.6 us
    ppermute x7, starting transfers between devices, turn(): return lax.ppermute(value, 'mp', [(i, (i + step) % X) for i in range(X)])  8.66 us
  transfers between devices with their start and end apart: 29, of which 10 were waited for; matrix products, arithmetic and copies ran while one was open for 3% of the time, Pallas kernels for 7%

profile of v4, /device:TPU:1, one launch (start us, length us, event | category | flops | bytes accessed | tf_op | source)
XLA Modules:
  0.0 382.4 jit_solution(9013469200280390828)
XLA Ops:
  10.6 29.6 %conditional.10 = (bf16[4112,128]{1,0:T(8,128)(2,1)}, bf16[4112,128]{1,0:T(8,128)(2,1)}, bf16[24,128,128]{2,1,0:T(8,128)(2,1)}, bf16[4112,128]{1,0:T(8,128)(2,1)S(1)}, bf16[256,512]{1,0:T(8,128)(2,1)S(1)}) conditional(s32[]{:T(128)} %convert_element_type.28, () %tuple.78, (bf16[4112,128]{1,0:T(8,128)(2,1)S(1)}, s32[]{:T(128)}, s32[3,64]{1,0:T(4,128)S(1)}, ...), branch_computations={%region_0.0_spmd, %region_1.0_spmd} | conditional | flops 524290 | bytes 15237278 | solution.py:468
  17.2 18.6 %conditional = (bf16[24,128,128]{2,1,0:T(8,128)(2,1)}) conditional(s32[]{:T(128)} %convert_element_type.9, () %tuple.47, (s32[]{:T(128)}, bf16[4112,128]{1,0:T(8,128)(2,1)S(1)}) %tuple.48), branch_computations={%region_2.0_spmd, %region_3.0_spmd} | conditional | bytes 3145736 | solution.py:468
  18.2 17.5 %all_to_all.50 = bf16[8,384,128]{2,1,0:T(8,128)(2,1)} all-to-all(bf16[8,384,128]{2,1,0:T(8,128)(2,1)S(1)} %bitcast.57), channel_id=1, replica_groups=mesh['y'=4,'z'=8,'core'=2,'mp'=4] {'y','core'}, dimensions={0} | all-to-all | bytes 1572864 | tf_op jit(solution)/shard_map/cond/branch_1_fun/cond/branch_1_fun/all_to_all | solution.py:454
  41.9 47.7 %conditional.11 = (bf16[4112,128]{1,0:T(8,128)(2,1)}, bf16[4112,128]{1,0:T(8,128)(2,1)}, bf16[4112,128]{1,0:T(8,128)(2,1)}, bf16[4112,128]{1,0:T(8,128)(2,1)}, bf16[72,128,128]{2,1,0:T(8,128)(2,1)}) conditional(s32[]{:T(128)} %convert_element_type.28, () %tuple.80, (bf16[4112,128]{1,0:T(8,128)(2,1)}, bf16[4112,128]{1,0:T(8,128)(2,1)}, ...), branch_computations={%region_4.5_spmd, %region_5.8_spmd} | conditional | flops 2 | bytes 26280188 | solution.py:468
  47.3 39.6 %conditional.1 = (bf16[72,128,128]{2,1,0:T(8,128)(2,1)}) conditional(s32[]{:T(128)} %convert_element_type.12, () %tuple.51, (s32[]{:T(128)}, bf16[4112,128]{1,0:T(8,128)(2,1)}, bf16[4112,128]{1,0:T(8,128)(2,1)}, bf16[4112,128]{1,0:T(8,128)(2,1)}) %tuple.52), branch_computations={%region_6.6_spmd, %region_7.7_spmd} | conditional | bytes 9437192 | solution.py:468
  50.9 36.0 %all_to_all.51 = bf16[8,1152,128]{2,1,0:T(8,128)(2,1)} all-to-all(bf16[8,1152,128]{2,1,0:T(8,128)(2,1)S(1)} %bitcast.53), channel_id=1, replica_groups=mesh['y'=4,'z'=8,'core'=2,'mp'=4] {'y','core'}, dimensions={0} | all-to-all | bytes 4718592 | tf_op jit(solution)/shard_map/cond/branch_1_fun/cond/branch_1_fun/all_to_all | solution.py:454
  89.6 46.7 %conditional.12 = (bf16[4112,128]{1,0:T(8,128)(2,1)}, bf16[4112,128]{1,0:T(8,128)(2,1)}, bf16[4112,128]{1,0:T(8,128)(2,1)}, bf16[4112,128]{1,0:T(8,128)(2,1)}, bf16[72,128,128]{2,1,0:T(8,128)(2,1)}) conditional(s32[]{:T(128)} %convert_element_type.28, () %tuple.82, (bf16[4112,128]{1,0:T(8,128)(2,1)}, bf16[4112,128]{1,0:T(8,128)(2,1)}, ...), branch_computations={%region_8.9_spmd, %region_9.12_spmd} | conditional | flops 2 | bytes 26280188 | solution.py:468
  94.9 40.6 %conditional.2 = (bf16[72,128,128]{2,1,0:T(8,128)(2,1)}) conditional(s32[]{:T(128)} %convert_element_type.22, () %tuple.55, (s32[]{:T(128)}, bf16[4112,128]{1,0:T(8,128)(2,1)}, bf16[4112,128]{1,0:T(8,128)(2,1)}, bf16[4112,128]{1,0:T(8,128)(2,1)}) %tuple.56), branch_computations={%region_10.10_spmd, %region_11.11_spmd} | conditional | bytes 9437192 | solution.py:468
  98.5 37.0 %all_to_all.52 = bf16[8,1152,128]{2,1,0:T(8,128)(2,1)} all-to-all(bf16[8,1152,128]{2,1,0:T(8,128)(2,1)S(1)} %bitcast.54), channel_id=1, replica_groups=mesh['y'=4,'z'=8,'core'=2,'mp'=4] {'y','core'}, dimensions={0} | all-to-all | bytes 4718592 | tf_op jit(solution)/shard_map/cond/branch_1_fun/cond/branch_1_fun/all_to_all | solution.py:454
  136.3 49.4 %conditional.13 = (bf16[2064,128]{1,0:T(8,128)(2,1)}, bf16[2048,128]{1,0:T(8,128)(2,1)}, bf16[4112,128]{1,0:T(8,128)(2,1)}, bf16[4112,128]{1,0:T(8,128)(2,1)}, bf16[72,128,128]{2,1,0:T(8,128)(2,1)}) conditional(s32[]{:T(128)} %convert_element_type.28, () %tuple.84, (bf16[4112,128]{1,0:T(8,128)(2,1)}, bf16[4112,128]{1,0:T(8,128)(2,1)}, ...), branch_computations={%region_12.13_spmd, %region_13.16_spmd} | conditional | flops 2 | bytes 24174846 | solution.py:468
  144.1 41.5 %conditional.3 = (bf16[72,128,128]{2,1,0:T(8,128)(2,1)}) conditional(s32[]{:T(128)} %convert_element_type.23, () %tuple.59, (s32[]{:T(128)}, bf16[4112,128]{1,0:T(8,128)(2,1)}, bf16[4112,128]{1,0:T(8,128)(2,1)}, bf16[4112,128]{1,0:T(8,128)(2,1)}) %tuple.60), branch_computations={%region_14.14_spmd, %region_15.15_spmd} | conditional | bytes 9437192 | solution.py:468
  147.7 37.9 %all_to_all.53 = bf16[8,1152,128]{2,1,0:T(8,128)(2,1)} all-to-all(bf16[8,1152,128]{2,1,0:T(8,128)(2,1)S(1)} %bitcast.55), channel_id=1, replica_groups=mesh['y'=4,'z'=8,'core'=2,'mp'=4] {'y','core'}, dimensions={0} | all-to-all | bytes 4718592 | tf_op jit(solution)/shard_map/cond/branch_1_fun/cond/branch_1_fun/all_to_all | solution.py:454
  185.7 24.2 %conditional.14 = (bf16[2064,128]{1,0:T(8,128)(2,1)}, bf16[2048,128]{1,0:T(8,128)(2,1)}, bf16[24,128,128]{2,1,0:T(8,128)(2,1)}) conditional(s32[]{:T(128)} %convert_element_type.28, () %tuple.86, (bf16[4112,128]{1,0:T(8,128)(2,1)}, bf16[4112,128]{1,0:T(8,128)(2,1)}, s32[]{:T(128)}, bf16[2064,128]{1,0:T(8,128)(2,1)}, bf16[2048,128]{1,0:T(8,128)(2,1)}, ...), branch_computations={%region_16.17_spmd, %region_17.20_spmd} | conditional | flops 2 | bytes 9461926 | solution.py:468
  190.7 19.2 %conditional.4 = (bf16[24,128,128]{2,1,0:T(8,128)(2,1)}) conditional(s32[]{:T(128)} %convert_element_type.24, () %tuple.63, (s32[]{:T(128)}, bf16[2064,128]{1,0:T(8,128)(2,1)}, bf16[2048,128]{1,0:T(8,128)(2,1)}, bf16[4,256,512]{2,1,0:T(8,128)(2,1)}, bf16[4,3072,128]{2,1,0:T(8,128)(2,1)}) %tuple.64), branch_computations={%region_18.18_spmd, %region_19.19_spmd} | conditional | bytes 3145736 | solution.py:468
  193.0 16.9 %all_to_all.54 = bf16[8,384,128]{2,1,0:T(8,128)(2,1)} all-to-all(bf16[8,384,128]{2,1,0:T(8,128)(2,1)S(1)} %bitcast.58), channel_id=1, replica_groups=mesh['y'=4,'z'=8,'core'=2,'mp'=4] {'y','core'}, dimensions={0} | all-to-all | bytes 1572864 | tf_op jit(solution)/shard_map/cond/branch_1_fun/cond/branch_1_fun/all_to_all | solution.py:454
  215.7 5.0 %stage.11 = bf16[120,128,128]{2,1,0:T(8,128)(2,1)S(1)} custom-call(s32[1]{0:T(128)} %bitcast.27.z_ref, bf16[2064,128]{1,0:T(8,128)(2,1)} %get-tuple-element.211.refs_0_, bf16[2048,128]{1,0:T(8,128)(2,1)} %get-tuple-element.212.refs_1_, bf16[4112,128]{1,0:T(8,128)(2,1)} %get-tuple-element.204.refs_2_, bf16[4112,128]{1,0:T(8,128)(2,1)} %get-tuple-element.205.refs_3_, ...), custom_call_target="tpu_custom_call" | custom-call | bytes 7864320 | tf_op jit(solution)/shard_map/stage/pallas_call | solution.py:126
  222.7 5.4 %all-to-all-start.5 = ((bf16[8,1920,128]{2,1,0:T(8,128)(2,1)}), bf16[8,1920,128]{2,1,0:T(8,128)(2,1)}, u32[]{:S(2)}, u32[]{:S(2)}) async-start(bf16[8,1920,128]{2,1,0:T(8,128)(2,1)} %bitcast.52), calls=%async_computation.5 | async-start | bytes 7864320 | tf_op jit(solution)/shard_map/all_to_all | solution.py:454
  230.8 17.6 %collective-permute-done.16.s1 = bf16[3072,128]{1,0:T(8,128)(2,1)S(1)} collective-permute-done((bf16[3072,128]{1,0:T(8,128)(2,1)S(1)}, bf16[3072,128]{1,0:T(8,128)(2,1)S(1)}, u32[]{:S(2)}, u32[]{:S(2)}) %collective-permute-start.16) | collective-permute-done | bytes 786464 | tf_op jit(solution)/shard_map/ppermute | solution.py:443
  254.3 6.2 %collective-permute-done.18.far0 = bf16[1536,128]{1,0:T(8,128)(2,1)S(1)} collective-permute-done((bf16[1536,128]{1,0:T(8,128)(2,1)}, bf16[1536,128]{1,0:T(8,128)(2,1)S(1)}, u32[]{:S(2)}, u32[]{:S(2)}) %collective-permute-start.18) | collective-permute-done | bytes 393248 | tf_op jit(solution)/shard_map/ppermute | solution.py:443
  265.3 9.0 %all-to-all-done.5 = bf16[8,1920,128]{2,1,0:T(8,128)(2,1)} async-done(((bf16[8,1920,128]{2,1,0:T(8,128)(2,1)}), bf16[8,1920,128]{2,1,0:T(8,128)(2,1)}, u32[]{:S(2)}, u32[]{:S(2)}) %all-to-all-start.5) | async-done | bytes 3932192 | tf_op jit(solution)/shard_map/all_to_all | solution.py:454
  311.0 7.4 %all-to-all-done.7 = bf16[4,768,128]{2,1,0:T(8,128)(2,1)S(1)} async-done(((bf16[4,768,128]{2,1,0:T(8,128)(2,1)}), bf16[4,768,128]{2,1,0:T(8,128)(2,1)S(1)}, u32[]{:S(2)}, u32[]{:S(2)}) %all-to-all-start.7) | async-done | bytes 786464 | tf_op jit(solution)/shard_map/all_to_all | solution.py:454
  325.4 19.3 %all_to_all.55.got_ref = bf16[32,16,640]{2,1,0:T(8,128)(2,1)S(1)} all-to-all(bf16[32,16,640]{2,1,0:T(8,128)(2,1)S(1)} %bitcast.59), channel_id=1, replica_groups=mesh['y'=4,'z'=8,'core'=2,'mp'=4] {'mp','y','core'}, dimensions={0} | all-to-all | bytes 1310720 | tf_op jit(solution)/shard_map/all_to_all | solution.py:454
  353.6 8.7 %collective-permute-done.20.refs_1_ = bf16[768,128]{1,0:T(8,128)(2,1)S(1)} collective-permute-done((bf16[768,128]{1,0:T(8,128)(2,1)S(1)}, bf16[768,128]{1,0:T(8,128)(2,1)S(1)}, u32[]{:S(2)}, u32[]{:S(2)}) %collective-permute-start.20) | collective-permute-done | bytes 196640 | tf_op jit(solution)/shard_map/ppermute | solution.py:443
  364.6 10.1 %all_to_all.56 = bf16[8,32,512]{2,1,0:T(8,128)(2,1)S(1)} all-to-all(bf16[8,32,512]{2,1,0:T(8,128)(2,1)S(1)} %sum_planes.1), channel_id=1, replica_groups=mesh['y'=4,'z'=8,'core'=2,'mp'=4] {'y','core'}, dimensions={0} | all-to-all | bytes 524288 | tf_op jit(solution)/shard_map/all_to_all | solution.py:454
  (139 shorter events, 133.8 us)
Async XLA Ops:
  7.2 178.5 %all-gather.5.cloned.1.call-start = ((), (), s32[]{:S(2)}) async-start(), calls=%async_computation.11 | async-start | bytes 1310720 | tf_op jit(solution)/shard_map/all_gather | solution.py:520
  10.6 29.6 %collective-permute-start.14 = (bf16[4112,128]{1,0:T(8,128)(2,1)S(1)}, bf16[4112,128]{1,0:T(8,128)(2,1)}, u32[]{:S(2)}, u32[]{:S(2)}) collective-permute-start(bf16[4112,128]{1,0:T(8,128)(2,1)S(1)} %get-tuple-element.98), channel_id=1, source_target_pairs={{0,8},{8,16},{16,24},{24,32},{32,40},{40,48},{48,56},{56,0},{1,9},... | collective-permute-start | bytes 3158024 | tf_op jit(solution)/shard_map/cond/branch_1_fun/ppermute | solution.py:439
  13.1 27.0 %collective-permute-start.15 = (bf16[4112,128]{1,0:T(8,128)(2,1)S(1)}, bf16[4112,128]{1,0:T(8,128)(2,1)}, u32[]{:S(2)}, u32[]{:S(2)}) collective-permute-start(bf16[4112,128]{1,0:T(8,128)(2,1)S(1)} %get-tuple-element.98), channel_id=1, source_target_pairs={{0,56},{8,0},{16,8},{24,16},{32,24},{40,32},{48,40},{56,48},{1,57}... | collective-permute-start | bytes 3158024 | tf_op jit(solution)/shard_map/cond/branch_1_fun/ppermute | solution.py:439
  40.9 144.8 %all-gather.7.cloned.1.call-start = ((), (), s32[]{:S(2)}) async-start(), calls=%async_computation.12 | async-start | bytes 3932160 | tf_op jit(solution)/shard_map/all_gather | solution.py:521
  41.9 45.1 %collective-permute-start = (bf16[4112,128]{1,0:T(8,128)(2,1)}, bf16[4112,128]{1,0:T(8,128)(2,1)}, u32[]{:S(2)}, u32[]{:S(2)}) collective-permute-start(bf16[4112,128]{1,0:T(8,128)(2,1)} %get-tuple-element.122), channel_id=1, source_target_pairs={{0,8},{8,16},{16,24},{24,32},{32,40},{40,48},{48,56},{56,0},{1,9},... | collective-permute-start | bytes 3158024 | tf_op jit(solution)/shard_map/cond/branch_1_fun/ppermute | solution.py:439
  42.0 45.0 %collective-permute-start.1 = (bf16[4112,128]{1,0:T(8,128)(2,1)}, bf16[4112,128]{1,0:T(8,128)(2,1)}, u32[]{:S(2)}, u32[]{:S(2)}) collective-permute-start(bf16[4112,128]{1,0:T(8,128)(2,1)} %get-tuple-element.123), channel_id=1, source_target_pairs={{0,56},{8,0},{16,8},{24,16},{32,24},{40,32},{48,40},{56,48},{1,57}... | collective-permute-start | bytes 3158024 | tf_op jit(solution)/shard_map/cond/branch_1_fun/ppermute | solution.py:439
  44.7 44.9 %collective-permute-start.2 = (bf16[4112,128]{1,0:T(8,128)(2,1)}, bf16[4112,128]{1,0:T(8,128)(2,1)}, u32[]{:S(2)}, u32[]{:S(2)}) collective-permute-start(bf16[4112,128]{1,0:T(8,128)(2,1)} %get-tuple-element.124), channel_id=1, source_target_pairs={{0,8},{8,16},{16,24},{24,32},{32,40},{40,48},{48,56},{56,0},{1,9},... | collective-permute-start | bytes 3158024 | tf_op jit(solution)/shard_map/cond/branch_1_fun/ppermute | solution.py:439
  44.7 44.9 %collective-permute-start.3 = (bf16[4112,128]{1,0:T(8,128)(2,1)}, bf16[4112,128]{1,0:T(8,128)(2,1)}, u32[]{:S(2)}, u32[]{:S(2)}) collective-permute-start(bf16[4112,128]{1,0:T(8,128)(2,1)} %get-tuple-element.124), channel_id=1, source_target_pairs={{0,56},{8,0},{16,8},{24,16},{32,24},{40,32},{48,40},{56,48},{1,57}... | collective-permute-start | bytes 3158024 | tf_op jit(solution)/shard_map/cond/branch_1_fun/ppermute | solution.py:439
  89.6 46.0 %collective-permute-start.4 = (bf16[4112,128]{1,0:T(8,128)(2,1)}, bf16[4112,128]{1,0:T(8,128)(2,1)}, u32[]{:S(2)}, u32[]{:S(2)}) collective-permute-start(bf16[4112,128]{1,0:T(8,128)(2,1)} %get-tuple-element.130), channel_id=1, source_target_pairs={{0,8},{8,16},{16,24},{24,32},{32,40},{40,48},{48,56},{56,0},{1,9},... | collective-permute-start | bytes 3158024 | tf_op jit(solution)/shard_map/cond/branch_1_fun/ppermute | solution.py:439
  90.5 45.1 %collective-permute-start.5 = (bf16[4112,128]{1,0:T(8,128)(2,1)}, bf16[4112,128]{1,0:T(8,128)(2,1)}, u32[]{:S(2)}, u32[]{:S(2)}) collective-permute-start(bf16[4112,128]{1,0:T(8,128)(2,1)} %get-tuple-element.131), channel_id=1, source_target_pairs={{0,56},{8,0},{16,8},{24,16},{32,24},{40,32},{48,40},{56,48},{1,57}... | collective-permute-start | bytes 3158024 | tf_op jit(solution)/shard_map/cond/branch_1_fun/ppermute | solution.py:439
  92.3 44.0 %collective-permute-start.6 = (bf16[4112,128]{1,0:T(8,128)(2,1)}, bf16[4112,128]{1,0:T(8,128)(2,1)}, u32[]{:S(2)}, u32[]{:S(2)}) collective-permute-start(bf16[4112,128]{1,0:T(8,128)(2,1)} %get-tuple-element.132), channel_id=1, source_target_pairs={{0,8},{8,16},{16,24},{24,32},{32,40},{40,48},{48,56},{56,0},{1,9},... | collective-permute-start | bytes 3158024 | tf_op jit(solution)/shard_map/cond/branch_1_fun/ppermute | solution.py:439
  92.3 44.0 %collective-permute-start.7 = (bf16[4112,128]{1,0:T(8,128)(2,1)}, bf16[4112,128]{1,0:T(8,128)(2,1)}, u32[]{:S(2)}, u32[]{:S(2)}) collective-permute-start(bf16[4112,128]{1,0:T(8,128)(2,1)} %get-tuple-element.133), channel_id=1, source_target_pairs={{0,56},{8,0},{16,8},{24,16},{32,24},{40,32},{48,40},{56,48},{1,57}... | collective-permute-start | bytes 3158024 | tf_op jit(solution)/shard_map/cond/branch_1_fun/ppermute | solution.py:439
  136.3 49.3 %collective-permute-start.10 = (bf16[4112,128]{1,0:T(8,128)(2,1)}, bf16[4112,128]{1,0:T(8,128)(2,1)}, u32[]{:S(2)}, u32[]{:S(2)}) collective-permute-start(bf16[4112,128]{1,0:T(8,128)(2,1)} %get-tuple-element.141), channel_id=1, source_target_pairs={{0,8},{8,16},{16,24},{24,32},{32,40},{40,48},{48,56},{56,0},{1,9},... | collective-permute-start | bytes 3158024 | tf_op jit(solution)/shard_map/cond/branch_1_fun/ppermute | solution.py:439
  136.7 48.9 %collective-permute-start.11 = (bf16[4112,128]{1,0:T(8,128)(2,1)}, bf16[4112,128]{1,0:T(8,128)(2,1)}, u32[]{:S(2)}, u32[]{:S(2)}) collective-permute-start(bf16[4112,128]{1,0:T(8,128)(2,1)} %get-tuple-element.142), channel_id=1, source_target_pairs={{0,56},{8,0},{16,8},{24,16},{32,24},{40,32},{48,40},{56,48},{1,57}... | collective-permute-start | bytes 3158024 | tf_op jit(solution)/shard_map/cond/branch_1_fun/ppermute | solution.py:439
  140.0 45.6 %collective-permute-start.8 = (bf16[2064,128]{1,0:T(8,128)(2,1)S(1)}, bf16[2064,128]{1,0:T(8,128)(2,1)}, u32[]{:S(2)}, u32[]{:S(2)}) collective-permute-start(bf16[2064,128]{1,0:T(8,128)(2,1)S(1)} %slice.30), channel_id=1, source_target_pairs={{0,8},{8,16},{16,24},{24,32},{32,40},{40,48},{48,56},{56,0},{1,9},... | collective-permute-start | bytes 1585160 | tf_op jit(solution)/shard_map/cond/branch_1_fun/ppermute | solution.py:439
  141.2 44.4 %collective-permute-start.9 = (bf16[2048,128]{1,0:T(8,128)(2,1)S(1)}, bf16[2048,128]{1,0:T(8,128)(2,1)}, u32[]{:S(2)}, u32[]{:S(2)}) collective-permute-start(bf16[2048,128]{1,0:T(8,128)(2,1)S(1)} %slice.31), channel_id=1, source_target_pairs={{0,56},{8,0},{16,8},{24,16},{32,24},{40,32},{48,40},{56,48},{1,57}... | collective-permute-start | bytes 1572872 | tf_op jit(solution)/shard_map/cond/branch_1_fun/ppermute | solution.py:439
  186.8 23.1 %collective-permute-start.12 = (bf16[2064,128]{1,0:T(8,128)(2,1)S(1)}, bf16[2064,128]{1,0:T(8,128)(2,1)}, u32[]{:S(2)}, u32[]{:S(2)}) collective-permute-start(bf16[2064,128]{1,0:T(8,128)(2,1)S(1)} %slice.32), channel_id=1, source_target_pairs={{0,8},{8,16},{16,24},{24,32},{32,40},{40,48},{48,56},{56,0},{1,9},... | collective-permute-start | bytes 1585160 | tf_op jit(solution)/shard_map/cond/branch_1_fun/ppermute | solution.py:439
  188.0 22.0 %collective-permute-start.13 = (bf16[2048,128]{1,0:T(8,128)(2,1)S(1)}, bf16[2048,128]{1,0:T(8,128)(2,1)}, u32[]{:S(2)}, u32[]{:S(2)}) collective-permute-start(bf16[2048,128]{1,0:T(8,128)(2,1)S(1)} %slice.33), channel_id=1, source_target_pairs={{0,56},{8,0},{16,8},{24,16},{32,24},{40,32},{48,40},{56,48},{1,57}... | collective-permute-start | bytes 1572872 | tf_op jit(solution)/shard_map/cond/branch_1_fun/ppermute | solution.py:439
  222.7 51.6 %all-to-all-start.5 = ((bf16[8,1920,128]{2,1,0:T(8,128)(2,1)}), bf16[8,1920,128]{2,1,0:T(8,128)(2,1)}, u32[]{:S(2)}, u32[]{:S(2)}) async-start(bf16[8,1920,128]{2,1,0:T(8,128)(2,1)} %bitcast.52), calls=%async_computation.5 | async-start | bytes 7864320 | tf_op jit(solution)/shard_map/all_to_all | solution.py:454
  228.1 20.3 %collective-permute-start.16 = (bf16[3072,128]{1,0:T(8,128)(2,1)S(1)}, bf16[3072,128]{1,0:T(8,128)(2,1)S(1)}, u32[]{:S(2)}, u32[]{:S(2)}) collective-permute-start(bf16[3072,128]{1,0:T(8,128)(2,1)S(1)} %aggregate.2.s0.refs_6_.after_ref), channel_id=1, source_target_pairs={{0,1},{1,2},{2,3},{3,0},{4,5},{5,6},{6,7},{7,4},{8,9},{9,10},{10,1... | collective-permute-start | bytes 2359304 | tf_op jit(solution)/shard_map/ppermute | solution.py:443
  229.4 19.8 %collective-permute-start.17 = (bf16[3072,128]{1,0:T(8,128)(2,1)S(1)}, bf16[3072,128]{1,0:T(8,128)(2,1)S(1)}, u32[]{:S(2)}, u32[]{:S(2)}) collective-permute-start(bf16[3072,128]{1,0:T(8,128)(2,1)S(1)} %aggregate.2.s0.refs_6_.after_ref), channel_id=1, source_target_pairs={{0,3},{1,0},{2,1},{3,2},{4,7},{5,4},{6,5},{7,6},{8,11},{9,8},{10,9... | collective-permute-start | bytes 2359304 | tf_op jit(solution)/shard_map/ppermute | solution.py:443
  282.1 15.2 %all-to-all-start.6 = ((bf16[4,768,128]{2,1,0:T(8,128)(2,1)}), bf16[4,768,128]{2,1,0:T(8,128)(2,1)S(1)}, u32[]{:S(2)}, u32[]{:S(2)}) async-start(bf16[4,768,128]{2,1,0:T(8,128)(2,1)} %bitcast.30), calls=%async_computation.6 | async-start | bytes 1572864 | tf_op jit(solution)/shard_map/all_to_all | solution.py:454
  305.0 13.4 %all-to-all-start.7 = ((bf16[4,768,128]{2,1,0:T(8,128)(2,1)}), bf16[4,768,128]{2,1,0:T(8,128)(2,1)S(1)}, u32[]{:S(2)}, u32[]{:S(2)}) async-start(bf16[4,768,128]{2,1,0:T(8,128)(2,1)} %get-tuple-element.213), calls=%async_computation.7 | async-start | bytes 1572864 | tf_op jit(solution)/shard_map/all_to_all | solution.py:454
  345.5 17.9 %all-to-all-start.9 = ((bf16[8,32,512]{2,1,0:T(8,128)(2,1)}), bf16[8,32,512]{2,1,0:T(8,128)(2,1)S(1)}, u32[]{:S(2)}, u32[]{:S(2)}) async-start(bf16[8,32,512]{2,1,0:T(8,128)(2,1)} %get-tuple-element.218), calls=%async_computation.9 | async-start | bytes 524288 | tf_op jit(solution)/shard_map/all_to_all | solution.py:454
  (29 other events, 131.8 us)
Sparse Core Ops, SparseCore 0:
  41.0 26.5 all-gather.4
  69.4 43.3 all-gather.6

commit v5 on v4

--- a/solution.py
+++ b/solution.py
@@ -506,7 +506,7 @@
         return hop(pair), hop((other, other)), beside(*pair, other)
 
     def step_two(pair, other):
-        return hop(pair), hop(other), beside(*pair, other[0])
+        return hop(pair), hop(other), beside(*pair, *other)
 
     def step_three(pair, other):
         return far_hop(pair), hop(other), beside(*pair, other[0])
@@ -529,8 +529,8 @@
     far, three_hidden, piece3 = apart(step_three, my_z, three, two_hidden)
     far_hidden, piece4 = apart(step_four, my_z, far, three_hidden, (weights, cot))
 
-    sides_input = ((0, 0, 1), (1, 1, 3), (2, 1, 3), (3, 1, 3), (4, 0, 1), (3, 0, 3), (2, 0, 3), (1, 0, 3))
-    sides_hidden = ((0, 2, 3), (3, 4, 5), (3, 3, 5), (3, 2, 5), (3, 0, 5), (3, 1, 5), (2, 2, 3), (1, 2, 3))
+    sides_input = ((0, 0, 1), (1, 1, 3), (2, 1, 4), (3, 1, 3), (4, 0, 1), (3, 0, 3), (2, 0, 4), (1, 0, 3))
+    sides_hidden = ((0, 2, 3), (1, 3, 4), (3, 3, 4), (3, 2, 4), (3, 0, 4), (3, 1, 4), (2, 2, 3), (1, 2, 4))
     use = tile_columns[:, 2:] - NB
     owner, slot = use // CAP, use % CAP
     group = (owner // (Z * C)) * C + owner % C
@@ -539,7 +539,7 @@
     batch = batch_blocks.reshape(-1)
     halo_input = (piece0, piece1, piece2, piece3, piece4)
     summed_first = aggregate(sides_input, HEAD, table_input, halo_input, tile_values, code, other, batch)
-    piece5 = send(far_hidden, *three_hidden, two_hidden[1], one_hidden[1], after=(summed_first,))
+    piece5 = send(far_hidden, *three_hidden, two_hidden[1], after=(summed_first,))
     halo_hidden = (piece1, piece2, piece3, piece5)
     all_first = gather_features(summed_first)
     hidden_first, slope_first = first_layer(all_first, columns)

time: 384 us -> 380 us (0.990)
  waiting for transfers between devices: 59.3 us -> 47.4 us
  blocking collectives: 175 us -> 183 us
    all_to_all x4, waiting for transfers between devices: 19.7 us -> 8.54 us  [exchange(): return lax.all_to_all(value, axes, split_axis=0, concat_axis=0, tiled=True)]
    all_to_all x7, blocking collectives: 175 us -> 183 us  [exchange(): return lax.all_to_all(value, axes, split_axis=0, concat_axis=0, tiled=True)]
    unnamed x49 -> x47, local copies, waits for them, and re-layouts: 19.7 us -> 17.4 us
  transfers between devices with their start and end apart: 29 -> 29, of which waited for: 10 -> 9; matrix products, arithmetic and copies ran while one was open for 3% -> 3% of each run, Pallas kernels for 7% -> 7%
where the time goes in v5:
time: 380 us; the launch traced here: 378 us
  blocking collectives  183 us (48%)
  starting transfers between devices  52.5 us (14%)
  Pallas kernels  51 us (13%)
  waiting for transfers between devices  47.4 us (12%)
  local copies, waits for them, and re-layouts  29.9 us (8%)
  between operations  14.3 us (4%)
    all_to_all x7, blocking collectives, exchange(): return lax.all_to_all(value, axes, split_axis=0, concat_axis=0, tiled=True)  183 us
    ppermute x7, waiting for transfers between devices, turn(): return lax.ppermute(value, 'mp', [(i, (i + step) % X) for i in range(X)])  32.7 us
    ppermute x16, starting transfers between devices, shift(): return lax.ppermute(value, 'z', [(i, (i + step) % Z) for i in range(Z)])  25.9 us
    pallas_call x6, Pallas kernels, stage(): call(functools.partial(stage_kernel, sizes), jax.ShapeDtypeStruct((entrie...  19.2 us
    all_to_all x4, starting transfers between devices, exchange(): return lax.all_to_all(value, axes, split_axis=0, concat_axis=0, tiled=True)  17.8 us
    unnamed x47, local copies, waits for them, and re-layouts  17.4 us
    pallas_call x2, Pallas kernels, aggregate(): call(functools.partial(aggregate_kernel, sides, len(halos), skip), jax.Sh...  9.86 us
    ppermute x7, starting transfers between devices, turn(): return lax.ppermute(value, 'mp', [(i, (i + step) % X) for i in range(X)])  8.66 us
  transfers between devices with their start and end apart: 29, of which 9 were waited for; matrix products, arithmetic and copies ran while one was open for 3% of the time, Pallas kernels for 7%

profile of v5, /device:TPU:1, one launch (start us, length us, event | category | flops | bytes accessed | tf_op | source)
XLA Modules:
  0.0 378.0 jit_solution(7555035101057896026)
XLA Ops:
  10.6 29.6 %conditional.10 = (bf16[4112,128]{1,0:T(8,128)(2,1)}, bf16[4112,128]{1,0:T(8,128)(2,1)}, bf16[24,128,128]{2,1,0:T(8,128)(2,1)}, bf16[4112,128]{1,0:T(8,128)(2,1)S(1)}, bf16[256,512]{1,0:T(8,128)(2,1)S(1)}) conditional(s32[]{:T(128)} %convert_element_type.28, () %tuple.78, (bf16[4112,128]{1,0:T(8,128)(2,1)S(1)}, s32[]{:T(128)}, s32[3,64]{1,0:T(4,128)S(1)}, ...), branch_computations={%region_0.0_spmd, %region_1.0_spmd} | conditional | flops 524290 | bytes 15237278 | solution.py:468
  17.2 18.6 %conditional = (bf16[24,128,128]{2,1,0:T(8,128)(2,1)}) conditional(s32[]{:T(128)} %convert_element_type.9, () %tuple.47, (s32[]{:T(128)}, bf16[4112,128]{1,0:T(8,128)(2,1)S(1)}) %tuple.48), branch_computations={%region_2.0_spmd, %region_3.0_spmd} | conditional | bytes 3145736 | solution.py:468
  18.2 17.5 %all_to_all.50 = bf16[8,384,128]{2,1,0:T(8,128)(2,1)} all-to-all(bf16[8,384,128]{2,1,0:T(8,128)(2,1)S(1)} %bitcast.57), channel_id=1, replica_groups=mesh['y'=4,'z'=8,'core'=2,'mp'=4] {'y','core'}, dimensions={0} | all-to-all | bytes 1572864 | tf_op jit(solution)/shard_map/cond/branch_1_fun/cond/branch_1_fun/all_to_all | solution.py:454
  41.9 47.7 %conditional.11 = (bf16[4112,128]{1,0:T(8,128)(2,1)}, bf16[4112,128]{1,0:T(8,128)(2,1)}, bf16[4112,128]{1,0:T(8,128)(2,1)}, bf16[4112,128]{1,0:T(8,128)(2,1)}, bf16[72,128,128]{2,1,0:T(8,128)(2,1)}) conditional(s32[]{:T(128)} %convert_element_type.28, () %tuple.80, (bf16[4112,128]{1,0:T(8,128)(2,1)}, bf16[4112,128]{1,0:T(8,128)(2,1)}, ...), branch_computations={%region_4.5_spmd, %region_5.8_spmd} | conditional | flops 2 | bytes 26280188 | solution.py:468
  47.3 39.6 %conditional.1 = (bf16[72,128,128]{2,1,0:T(8,128)(2,1)}) conditional(s32[]{:T(128)} %convert_element_type.12, () %tuple.51, (s32[]{:T(128)}, bf16[4112,128]{1,0:T(8,128)(2,1)}, bf16[4112,128]{1,0:T(8,128)(2,1)}, bf16[4112,128]{1,0:T(8,128)(2,1)}) %tuple.52), branch_computations={%region_6.6_spmd, %region_7.7_spmd} | conditional | bytes 9437192 | solution.py:468
  50.9 36.0 %all_to_all.51 = bf16[8,1152,128]{2,1,0:T(8,128)(2,1)} all-to-all(bf16[8,1152,128]{2,1,0:T(8,128)(2,1)S(1)} %bitcast.54), channel_id=1, replica_groups=mesh['y'=4,'z'=8,'core'=2,'mp'=4] {'y','core'}, dimensions={0} | all-to-all | bytes 4718592 | tf_op jit(solution)/shard_map/cond/branch_1_fun/cond/branch_1_fun/all_to_all | solution.py:454
  89.6 55.2 %conditional.12 = (bf16[4112,128]{1,0:T(8,128)(2,1)}, bf16[4112,128]{1,0:T(8,128)(2,1)}, bf16[4112,128]{1,0:T(8,128)(2,1)}, bf16[4112,128]{1,0:T(8,128)(2,1)}, bf16[96,128,128]{2,1,0:T(8,128)(2,1)}) conditional(s32[]{:T(128)} %convert_element_type.28, () %tuple.82, (bf16[4112,128]{1,0:T(8,128)(2,1)}, bf16[4112,128]{1,0:T(8,128)(2,1)}, ...), branch_computations={%region_8.9_spmd, %region_9.12_spmd} | conditional | flops 2 | bytes 29425924 | solution.py:468
  94.9 49.9 %conditional.2 = (bf16[96,128,128]{2,1,0:T(8,128)(2,1)}) conditional(s32[]{:T(128)} %convert_element_type.22, () %tuple.55, (s32[]{:T(128)}, bf16[4112,128]{1,0:T(8,128)(2,1)}, bf16[4112,128]{1,0:T(8,128)(2,1)}, bf16[4112,128]{1,0:T(8,128)(2,1)}, bf16[4112,128]{1,0:T(8,128)(2,1)}) %tuple.56), branch_computations={%region_10.10_spmd, %region_11.11_spmd} | conditional | bytes 12582920 | solution.py:468
  99.2 45.6 %all_to_all.52 = bf16[8,1536,128]{2,1,0:T(8,128)(2,1)} all-to-all(bf16[8,1536,128]{2,1,0:T(8,128)(2,1)S(1)} %bitcast.53), channel_id=1, replica_groups=mesh['y'=4,'z'=8,'core'=2,'mp'=4] {'y','core'}, dimensions={0} | all-to-all | bytes 6291456 | tf_op jit(solution)/shard_map/cond/branch_1_fun/cond/branch_1_fun/all_to_all | solution.py:454
  144.8 46.2 %conditional.13 = (bf16[2064,128]{1,0:T(8,128)(2,1)}, bf16[2048,128]{1,0:T(8,128)(2,1)}, bf16[4112,128]{1,0:T(8,128)(2,1)}, bf16[4112,128]{1,0:T(8,128)(2,1)}, bf16[72,128,128]{2,1,0:T(8,128)(2,1)}) conditional(s32[]{:T(128)} %convert_element_type.28, () %tuple.84, (bf16[4112,128]{1,0:T(8,128)(2,1)}, bf16[4112,128]{1,0:T(8,128)(2,1)}, ...), branch_computations={%region_12.13_spmd, %region_13.16_spmd} | conditional | flops 2 | bytes 24174846 | solution.py:468
  152.7 38.3 %conditional.3 = (bf16[72,128,128]{2,1,0:T(8,128)(2,1)}) conditional(s32[]{:T(128)} %convert_element_type.23, () %tuple.59, (s32[]{:T(128)}, bf16[4112,128]{1,0:T(8,128)(2,1)}, bf16[4112,128]{1,0:T(8,128)(2,1)}, bf16[4112,128]{1,0:T(8,128)(2,1)}) %tuple.60), branch_computations={%region_14.14_spmd, %region_15.15_spmd} | conditional | bytes 9437192 | solution.py:468
  156.3 34.7 %all_to_all.53 = bf16[8,1152,128]{2,1,0:T(8,128)(2,1)} all-to-all(bf16[8,1152,128]{2,1,0:T(8,128)(2,1)S(1)} %bitcast.55), channel_id=1, replica_groups=mesh['y'=4,'z'=8,'core'=2,'mp'=4] {'y','core'}, dimensions={0} | all-to-all | bytes 4718592 | tf_op jit(solution)/shard_map/cond/branch_1_fun/cond/branch_1_fun/all_to_all | solution.py:454
  191.1 24.3 %conditional.14 = (bf16[2064,128]{1,0:T(8,128)(2,1)}, bf16[2048,128]{1,0:T(8,128)(2,1)}, bf16[24,128,128]{2,1,0:T(8,128)(2,1)}) conditional(s32[]{:T(128)} %convert_element_type.28, () %tuple.86, (bf16[4112,128]{1,0:T(8,128)(2,1)}, bf16[4112,128]{1,0:T(8,128)(2,1)}, s32[]{:T(128)}, bf16[2064,128]{1,0:T(8,128)(2,1)}, bf16[2048,128]{1,0:T(8,128)(2,1)}, ...), branch_computations={%region_16.17_spmd, %region_17.20_spmd} | conditional | flops 2 | bytes 9461926 | solution.py:468
  196.1 19.3 %conditional.4 = (bf16[24,128,128]{2,1,0:T(8,128)(2,1)}) conditional(s32[]{:T(128)} %convert_element_type.24, () %tuple.63, (s32[]{:T(128)}, bf16[2064,128]{1,0:T(8,128)(2,1)}, bf16[2048,128]{1,0:T(8,128)(2,1)}, bf16[4,256,512]{2,1,0:T(8,128)(2,1)}, bf16[4,3072,128]{2,1,0:T(8,128)(2,1)}) %tuple.64), branch_computations={%region_18.18_spmd, %region_19.19_spmd} | conditional | bytes 3145736 | solution.py:468
  198.5 16.9 %all_to_all.54 = bf16[8,384,128]{2,1,0:T(8,128)(2,1)} all-to-all(bf16[8,384,128]{2,1,0:T(8,128)(2,1)S(1)} %bitcast.58), channel_id=1, replica_groups=mesh['y'=4,'z'=8,'core'=2,'mp'=4] {'y','core'}, dimensions={0} | all-to-all | bytes 1572864 | tf_op jit(solution)/shard_map/cond/branch_1_fun/cond/branch_1_fun/all_to_all | solution.py:454
  227.3 5.4 %all-to-all-start.5 = ((bf16[8,1536,128]{2,1,0:T(8,128)(2,1)}), bf16[8,1536,128]{2,1,0:T(8,128)(2,1)}, u32[]{:S(2)}, u32[]{:S(2)}) async-start(bf16[8,1536,128]{2,1,0:T(8,128)(2,1)} %bitcast.52), calls=%async_computation.5 | async-start | bytes 6291456 | tf_op jit(solution)/shard_map/all_to_all | solution.py:454
  235.4 17.6 %collective-permute-done.16.s1 = bf16[3072,128]{1,0:T(8,128)(2,1)S(1)} collective-permute-done((bf16[3072,128]{1,0:T(8,128)(2,1)S(1)}, bf16[3072,128]{1,0:T(8,128)(2,1)S(1)}, u32[]{:S(2)}, u32[]{:S(2)}) %collective-permute-start.16) | collective-permute-done | bytes 786464 | tf_op jit(solution)/shard_map/ppermute | solution.py:443
  258.8 6.2 %collective-permute-done.18.far0 = bf16[1536,128]{1,0:T(8,128)(2,1)S(1)} collective-permute-done((bf16[1536,128]{1,0:T(8,128)(2,1)}, bf16[1536,128]{1,0:T(8,128)(2,1)S(1)}, u32[]{:S(2)}, u32[]{:S(2)}) %collective-permute-start.18) | collective-permute-done | bytes 393248 | tf_op jit(solution)/shard_map/ppermute | solution.py:443
  271.5 6.1 %aggregate.3 = bf16[3072,128]{1,0:T(8,128)(2,1)} custom-call(s32[72]{0:T(128)S(1)} %reshape.251.code_ref, s32[24]{0:T(128)S(1)} %slice_bitcast_fusion.4.other_ref, s32[24]{0:T(128)S(1)} %bitcast.63, bf16[3072,128]{1,0:T(8,128)(2,1)S(1)} %copy-done.13, bf16[24,5,128,128]{3,2,1,0:T(8,128)(2,1)} %tiles_ref.1, ...), custom_call_target="tpu_custom_call" | custom-call | flops 503316480 | bytes 7864320 | tf_op jit(solution)/shard_map/aggregate/pallas_call | solution.py:182
  305.2 6.1 %all-to-all-done.7 = bf16[4,768,128]{2,1,0:T(8,128)(2,1)S(1)} async-done(((bf16[4,768,128]{2,1,0:T(8,128)(2,1)}), bf16[4,768,128]{2,1,0:T(8,128)(2,1)S(1)}, u32[]{:S(2)}, u32[]{:S(2)}) %all-to-all-start.7) | async-done | bytes 786464 | tf_op jit(solution)/shard_map/all_to_all | solution.py:454
  318.3 21.7 %all_to_all.55.got_ref = bf16[32,16,640]{2,1,0:T(8,128)(2,1)S(1)} all-to-all(bf16[32,16,640]{2,1,0:T(8,128)(2,1)S(1)} %bitcast.59), channel_id=1, replica_groups=mesh['y'=4,'z'=8,'core'=2,'mp'=4] {'mp','y','core'}, dimensions={0} | all-to-all | bytes 1310720 | tf_op jit(solution)/shard_map/all_to_all | solution.py:454
  340.9 5.0 %all-to-all-start.9 = ((bf16[8,32,512]{2,1,0:T(8,128)(2,1)}), bf16[8,32,512]{2,1,0:T(8,128)(2,1)S(1)}, u32[]{:S(2)}, u32[]{:S(2)}) async-start(bf16[8,32,512]{2,1,0:T(8,128)(2,1)} %get-tuple-element.221), calls=%async_computation.9 | async-start | bytes 524288 | tf_op jit(solution)/shard_map/all_to_all | solution.py:454
  349.2 8.7 %collective-permute-done.20.refs_1_ = bf16[768,128]{1,0:T(8,128)(2,1)S(1)} collective-permute-done((bf16[768,128]{1,0:T(8,128)(2,1)S(1)}, bf16[768,128]{1,0:T(8,128)(2,1)S(1)}, u32[]{:S(2)}, u32[]{:S(2)}) %collective-permute-start.20) | collective-permute-done | bytes 196640 | tf_op jit(solution)/shard_map/ppermute | solution.py:443
  360.2 10.1 %all_to_all.56 = bf16[8,32,512]{2,1,0:T(8,128)(2,1)S(1)} all-to-all(bf16[8,32,512]{2,1,0:T(8,128)(2,1)S(1)} %sum_planes.1), channel_id=1, replica_groups=mesh['y'=4,'z'=8,'core'=2,'mp'=4] {'y','core'}, dimensions={0} | all-to-all | bytes 524288 | tf_op jit(solution)/shard_map/all_to_all | solution.py:454
  (137 shorter events, 126.0 us)
Async XLA Ops:
  7.2 183.9 %all-gather.5.cloned.1.call-start = ((), (), s32[]{:S(2)}) async-start(), calls=%async_computation.11 | async-start | bytes 1310720 | tf_op jit(solution)/shard_map/all_gather | solution.py:520
  10.6 29.6 %collective-permute-start.14 = (bf16[4112,128]{1,0:T(8,128)(2,1)S(1)}, bf16[4112,128]{1,0:T(8,128)(2,1)}, u32[]{:S(2)}, u32[]{:S(2)}) collective-permute-start(bf16[4112,128]{1,0:T(8,128)(2,1)S(1)} %get-tuple-element.100), channel_id=1, source_target_pairs={{0,8},{8,16},{16,24},{24,32},{32,40},{40,48},{48,56},{56,0},{1,9},... | collective-permute-start | bytes 3158024 | tf_op jit(solution)/shard_map/cond/branch_1_fun/ppermute | solution.py:439
  13.1 27.0 %collective-permute-start.15 = (bf16[4112,128]{1,0:T(8,128)(2,1)S(1)}, bf16[4112,128]{1,0:T(8,128)(2,1)}, u32[]{:S(2)}, u32[]{:S(2)}) collective-permute-start(bf16[4112,128]{1,0:T(8,128)(2,1)S(1)} %get-tuple-element.100), channel_id=1, source_target_pairs={{0,56},{8,0},{16,8},{24,16},{32,24},{40,32},{48,40},{56,48},{1,57}... | collective-permute-start | bytes 3158024 | tf_op jit(solution)/shard_map/cond/branch_1_fun/ppermute | solution.py:439
  40.9 150.2 %all-gather.7.cloned.1.call-start = ((), (), s32[]{:S(2)}) async-start(), calls=%async_computation.12 | async-start | bytes 3932160 | tf_op jit(solution)/shard_map/all_gather | solution.py:521
  41.9 45.1 %collective-permute-start = (bf16[4112,128]{1,0:T(8,128)(2,1)}, bf16[4112,128]{1,0:T(8,128)(2,1)}, u32[]{:S(2)}, u32[]{:S(2)}) collective-permute-start(bf16[4112,128]{1,0:T(8,128)(2,1)} %get-tuple-element.124), channel_id=1, source_target_pairs={{0,8},{8,16},{16,24},{24,32},{32,40},{40,48},{48,56},{56,0},{1,9},... | collective-permute-start | bytes 3158024 | tf_op jit(solution)/shard_map/cond/branch_1_fun/ppermute | solution.py:439
  42.0 45.0 %collective-permute-start.1 = (bf16[4112,128]{1,0:T(8,128)(2,1)}, bf16[4112,128]{1,0:T(8,128)(2,1)}, u32[]{:S(2)}, u32[]{:S(2)}) collective-permute-start(bf16[4112,128]{1,0:T(8,128)(2,1)} %get-tuple-element.125), channel_id=1, source_target_pairs={{0,56},{8,0},{16,8},{24,16},{32,24},{40,32},{48,40},{56,48},{1,57}... | collective-permute-start | bytes 3158024 | tf_op jit(solution)/shard_map/cond/branch_1_fun/ppermute | solution.py:439
  44.7 44.9 %collective-permute-start.2 = (bf16[4112,128]{1,0:T(8,128)(2,1)}, bf16[4112,128]{1,0:T(8,128)(2,1)}, u32[]{:S(2)}, u32[]{:S(2)}) collective-permute-start(bf16[4112,128]{1,0:T(8,128)(2,1)} %get-tuple-element.126), channel_id=1, source_target_pairs={{0,8},{8,16},{16,24},{24,32},{32,40},{40,48},{48,56},{56,0},{1,9},... | collective-permute-start | bytes 3158024 | tf_op jit(solution)/shard_map/cond/branch_1_fun/ppermute | solution.py:439
  44.7 44.9 %collective-permute-start.3 = (bf16[4112,128]{1,0:T(8,128)(2,1)}, bf16[4112,128]{1,0:T(8,128)(2,1)}, u32[]{:S(2)}, u32[]{:S(2)}) collective-permute-start(bf16[4112,128]{1,0:T(8,128)(2,1)} %get-tuple-element.126), channel_id=1, source_target_pairs={{0,56},{8,0},{16,8},{24,16},{32,24},{40,32},{48,40},{56,48},{1,57}... | collective-permute-start | bytes 3158024 | tf_op jit(solution)/shard_map/cond/branch_1_fun/ppermute | solution.py:439
  89.6 55.2 %collective-permute-start.4 = (bf16[4112,128]{1,0:T(8,128)(2,1)}, bf16[4112,128]{1,0:T(8,128)(2,1)}, u32[]{:S(2)}, u32[]{:S(2)}) collective-permute-start(bf16[4112,128]{1,0:T(8,128)(2,1)} %get-tuple-element.133), channel_id=1, source_target_pairs={{0,8},{8,16},{16,24},{24,32},{32,40},{40,48},{48,56},{56,0},{1,9},... | collective-permute-start | bytes 3158024 | tf_op jit(solution)/shard_map/cond/branch_1_fun/ppermute | solution.py:439
  90.5 54.3 %collective-permute-start.5 = (bf16[4112,128]{1,0:T(8,128)(2,1)}, bf16[4112,128]{1,0:T(8,128)(2,1)}, u32[]{:S(2)}, u32[]{:S(2)}) collective-permute-start(bf16[4112,128]{1,0:T(8,128)(2,1)} %get-tuple-element.134), channel_id=1, source_target_pairs={{0,56},{8,0},{16,8},{24,16},{32,24},{40,32},{48,40},{56,48},{1,57}... | collective-permute-start | bytes 3158024 | tf_op jit(solution)/shard_map/cond/branch_1_fun/ppermute | solution.py:439
  92.3 52.5 %collective-permute-start.6 = (bf16[4112,128]{1,0:T(8,128)(2,1)}, bf16[4112,128]{1,0:T(8,128)(2,1)}, u32[]{:S(2)}, u32[]{:S(2)}) collective-permute-start(bf16[4112,128]{1,0:T(8,128)(2,1)} %get-tuple-element.135), channel_id=1, source_target_pairs={{0,8},{8,16},{16,24},{24,32},{32,40},{40,48},{48,56},{56,0},{1,9},... | collective-permute-start | bytes 3158024 | tf_op jit(solution)/shard_map/cond/branch_1_fun/ppermute | solution.py:439
  92.3 52.5 %collective-permute-start.7 = (bf16[4112,128]{1,0:T(8,128)(2,1)}, bf16[4112,128]{1,0:T(8,128)(2,1)}, u32[]{:S(2)}, u32[]{:S(2)}) collective-permute-start(bf16[4112,128]{1,0:T(8,128)(2,1)} %get-tuple-element.136), channel_id=1, source_target_pairs={{0,56},{8,0},{16,8},{24,16},{32,24},{40,32},{48,40},{56,48},{1,57}... | collective-permute-start | bytes 3158024 | tf_op jit(solution)/shard_map/cond/branch_1_fun/ppermute | solution.py:439
  144.8 46.2 %collective-permute-start.10 = (bf16[4112,128]{1,0:T(8,128)(2,1)}, bf16[4112,128]{1,0:T(8,128)(2,1)}, u32[]{:S(2)}, u32[]{:S(2)}) collective-permute-start(bf16[4112,128]{1,0:T(8,128)(2,1)} %get-tuple-element.144), channel_id=1, source_target_pairs={{0,8},{8,16},{16,24},{24,32},{32,40},{40,48},{48,56},{56,0},{1,9},... | collective-permute-start | bytes 3158024 | tf_op jit(solution)/shard_map/cond/branch_1_fun/ppermute | solution.py:439
  144.9 46.1 %collective-permute-start.11 = (bf16[4112,128]{1,0:T(8,128)(2,1)}, bf16[4112,128]{1,0:T(8,128)(2,1)}, u32[]{:S(2)}, u32[]{:S(2)}) collective-permute-start(bf16[4112,128]{1,0:T(8,128)(2,1)} %get-tuple-element.145), channel_id=1, source_target_pairs={{0,56},{8,0},{16,8},{24,16},{32,24},{40,32},{48,40},{56,48},{1,57}... | collective-permute-start | bytes 3158024 | tf_op jit(solution)/shard_map/cond/branch_1_fun/ppermute | solution.py:439
  148.7 42.4 %collective-permute-start.8 = (bf16[2064,128]{1,0:T(8,128)(2,1)S(1)}, bf16[2064,128]{1,0:T(8,128)(2,1)}, u32[]{:S(2)}, u32[]{:S(2)}) collective-permute-start(bf16[2064,128]{1,0:T(8,128)(2,1)S(1)} %slice.30), channel_id=1, source_target_pairs={{0,8},{8,16},{16,24},{24,32},{32,40},{40,48},{48,56},{56,0},{1,9},... | collective-permute-start | bytes 1585160 | tf_op jit(solution)/shard_map/cond/branch_1_fun/ppermute | solution.py:439
  149.8 41.2 %collective-permute-start.9 = (bf16[2048,128]{1,0:T(8,128)(2,1)S(1)}, bf16[2048,128]{1,0:T(8,128)(2,1)}, u32[]{:S(2)}, u32[]{:S(2)}) collective-permute-start(bf16[2048,128]{1,0:T(8,128)(2,1)S(1)} %slice.31), channel_id=1, source_target_pairs={{0,56},{8,0},{16,8},{24,16},{32,24},{40,32},{48,40},{56,48},{1,57}... | collective-permute-start | bytes 1572872 | tf_op jit(solution)/shard_map/cond/branch_1_fun/ppermute | solution.py:439
  192.2 23.2 %collective-permute-start.12 = (bf16[2064,128]{1,0:T(8,128)(2,1)S(1)}, bf16[2064,128]{1,0:T(8,128)(2,1)}, u32[]{:S(2)}, u32[]{:S(2)}) collective-permute-start(bf16[2064,128]{1,0:T(8,128)(2,1)S(1)} %slice.32), channel_id=1, source_target_pairs={{0,8},{8,16},{16,24},{24,32},{32,40},{40,48},{48,56},{56,0},{1,9},... | collective-permute-start | bytes 1585160 | tf_op jit(solution)/shard_map/cond/branch_1_fun/ppermute | solution.py:439
  193.4 22.0 %collective-permute-start.13 = (bf16[2048,128]{1,0:T(8,128)(2,1)S(1)}, bf16[2048,128]{1,0:T(8,128)(2,1)}, u32[]{:S(2)}, u32[]{:S(2)}) collective-permute-start(bf16[2048,128]{1,0:T(8,128)(2,1)S(1)} %slice.33), channel_id=1, source_target_pairs={{0,56},{8,0},{16,8},{24,16},{32,24},{40,32},{48,40},{56,48},{1,57}... | collective-permute-start | bytes 1572872 | tf_op jit(solution)/shard_map/cond/branch_1_fun/ppermute | solution.py:439
  227.3 43.0 %all-to-all-start.5 = ((bf16[8,1536,128]{2,1,0:T(8,128)(2,1)}), bf16[8,1536,128]{2,1,0:T(8,128)(2,1)}, u32[]{:S(2)}, u32[]{:S(2)}) async-start(bf16[8,1536,128]{2,1,0:T(8,128)(2,1)} %bitcast.52), calls=%async_computation.5 | async-start | bytes 6291456 | tf_op jit(solution)/shard_map/all_to_all | solution.py:454
  232.7 20.3 %collective-permute-start.16 = (bf16[3072,128]{1,0:T(8,128)(2,1)S(1)}, bf16[3072,128]{1,0:T(8,128)(2,1)S(1)}, u32[]{:S(2)}, u32[]{:S(2)}) collective-permute-start(bf16[3072,128]{1,0:T(8,128)(2,1)S(1)} %aggregate.2.s0.refs_5_.after_ref), channel_id=1, source_target_pairs={{0,1},{1,2},{2,3},{3,0},{4,5},{5,6},{6,7},{7,4},{8,9},{9,10},{10,1... | collective-permute-start | bytes 2359304 | tf_op jit(solution)/shard_map/ppermute | solution.py:443
  233.9 19.8 %collective-permute-start.17 = (bf16[3072,128]{1,0:T(8,128)(2,1)S(1)}, bf16[3072,128]{1,0:T(8,128)(2,1)S(1)}, u32[]{:S(2)}, u32[]{:S(2)}) collective-permute-start(bf16[3072,128]{1,0:T(8,128)(2,1)S(1)} %aggregate.2.s0.refs_5_.after_ref), channel_id=1, source_target_pairs={{0,3},{1,0},{2,1},{3,2},{4,7},{5,4},{6,5},{7,6},{8,11},{9,8},{10,9... | collective-permute-start | bytes 2359304 | tf_op jit(solution)/shard_map/ppermute | solution.py:443
  277.6 13.9 %all-to-all-start.6 = ((bf16[4,768,128]{2,1,0:T(8,128)(2,1)}), bf16[4,768,128]{2,1,0:T(8,128)(2,1)S(1)}, u32[]{:S(2)}, u32[]{:S(2)}) async-start(bf16[4,768,128]{2,1,0:T(8,128)(2,1)} %bitcast.30), calls=%async_computation.6 | async-start | bytes 1572864 | tf_op jit(solution)/shard_map/all_to_all | solution.py:454
  299.2 12.1 %all-to-all-start.7 = ((bf16[4,768,128]{2,1,0:T(8,128)(2,1)}), bf16[4,768,128]{2,1,0:T(8,128)(2,1)S(1)}, u32[]{:S(2)}, u32[]{:S(2)}) async-start(bf16[4,768,128]{2,1,0:T(8,128)(2,1)} %get-tuple-element.216), calls=%async_computation.7 | async-start | bytes 1572864 | tf_op jit(solution)/shard_map/all_to_all | solution.py:454
  340.9 18.2 %all-to-all-start.9 = ((bf16[8,32,512]{2,1,0:T(8,128)(2,1)}), bf16[8,32,512]{2,1,0:T(8,128)(2,1)S(1)}, u32[]{:S(2)}, u32[]{:S(2)}) async-start(bf16[8,32,512]{2,1,0:T(8,128)(2,1)} %get-tuple-element.221), calls=%async_computation.9 | async-start | bytes 524288 | tf_op jit(solution)/shard_map/all_to_all | solution.py:454
  (28 other events, 131.9 us)
Sparse Core Ops, SparseCore 0:
  41.0 26.5 all-gather.4
  69.4 43.3 all-gather.6
